TPU v7x, 256 devices: a whole 4x4x8 slice. The times are simulated.
256 devices in a mesh: ctx: 128 (over z, x_hi, y, core), tp: 2 (over x_lo).
Axes of the slice: x: 4 (x_hi: 2, x_lo: 2; x = x_hi * 2 + x_lo), y: 4, z: 8, core: 2. Of those that a mesh axis runs over, the one named last changes fastest.
Arguments:
- queries: bfloat16 [8192, 1536], P('ctx', 'tp'), may hold values from -512 to 512
- keys: bfloat16 [8192, 1536], P('ctx', 'tp'), may hold values from -8 to 8
- values: bfloat16 [8192, 1536], P('ctx', 'tp'), may hold values from -6 to 6
- wo: bfloat16 [1536, 3072], P('tp'), may hold values from -0.15625 to 0.15625
- frame_tokens: int32 [128], replicated, may hold values from 32 to 64, as said below
Outputs:
- projected: bfloat16 [8192, 3072], P(('ctx', 'tp'))
Inputs may be any that keep to these rules, and one draw needn't show every extreme that they name: `frame_tokens`: at least 32 tokens of every frame are live.
All inputs are finite; a program needn't handle non-finite values.
Results may differ from a plain program's by a relative error of at most 0.014.
Values may be sent and summed in bfloat16 or wider, within the bound.
No kernel may reach another device: no remote copies, remote signals or barrier semaphores. Data moves between devices by JAX's collectives and lax.ppermute only.
A program may use at most 128 MiB of HBM per device.

v0:
```python
import math

import jax
import jax.numpy as jnp
from jax import lax
from jax.sharding import PartitionSpec as P

HEAD_DIM = 128
FRAME = 64


def lookup_counts(frame_index, frame_tokens):
    frame_ids = jnp.arange(frame_tokens.shape[0], dtype=jnp.int32)
    picked = jnp.where(frame_index[:, None] == frame_ids[None, :], frame_tokens[None, :], 0)
    return jnp.sum(picked, axis=1)


def piece_update(
    state, query_rows, query_frames, key_piece, value_piece, frame_tokens, lower, upper
):
    run_max, run_total, run_acc = state
    count = key_piece.shape[0]
    head_count = query_rows.shape[1]
    key_pos = jnp.arange(count, dtype=jnp.int32)
    key_frame = key_pos // FRAME
    key_live = (
        (key_pos % FRAME < lookup_counts(key_frame, frame_tokens))
        & (key_pos >= lower)
        & (key_pos < upper)
    )
    key_heads = key_piece.reshape(count, head_count, HEAD_DIM)
    value_heads = value_piece.reshape(count, head_count, HEAD_DIM)
    scores = jnp.einsum("qhd,khd->hqk", query_rows, key_heads, preferred_element_type=jnp.float32)
    scores = scores * (1.0 / math.sqrt(HEAD_DIM))
    allowed = (key_frame[None, :] <= query_frames[:, None]) & key_live[None, :]
    scores = jnp.where(allowed[None], scores, -jnp.inf)
    new_max = jnp.maximum(run_max, jnp.max(scores, axis=-1))
    weights = jnp.exp(scores - new_max[:, :, None])
    new_total = jnp.sum(weights, axis=-1)
    added = jnp.einsum(
        "hqk,khd->qhd",
        weights.astype(jnp.bfloat16),
        value_heads,
        preferred_element_type=jnp.float32,
    )
    return (new_max, new_total, added)


def on_device(queries, keys, values, wo, frame_tokens):
    tok_rows = queries.shape[0]
    head_count = queries.shape[1] // HEAD_DIM
    ctx_size = lax.axis_size("ctx")
    ctx_index = lax.axis_index("ctx")
    all_rows = ctx_size * tok_rows
    row_offsets = jnp.arange(tok_rows, dtype=jnp.int32)
    query_pos = ctx_index * tok_rows + row_offsets
    query_frames = query_pos // FRAME
    query_rows = queries.reshape(tok_rows, head_count, HEAD_DIM)

    def empty_state():
        return (
            jnp.full((head_count, tok_rows), -1e30, jnp.float32),
            jnp.zeros((head_count, tok_rows), jnp.float32),
            jnp.zeros((tok_rows, head_count, HEAD_DIM), jnp.float32),
        )

    own_lower = jnp.int32(0)
    own_upper = jnp.int32(all_rows)
    own_state = empty_state()
    guest_state = empty_state()
    key_piece = lax.all_gather(keys, "ctx", axis=0, tiled=True)
    value_piece = lax.all_gather(values, "ctx", axis=0, tiled=True)
    own_state = piece_update(
        own_state,
        query_rows,
        query_frames,
        key_piece,
        value_piece,
        frame_tokens,
        own_lower,
        own_upper,
    )
    own_state, guest_state = (own_state, guest_state)
    run_max, run_total, run_acc = own_state
    heads_out = run_acc / jnp.transpose(run_total)[:, :, None]
    query_live = query_pos % FRAME < lookup_counts(query_frames, frame_tokens)
    heads_out = jnp.where(query_live[:, None, None], heads_out, 0.0)
    attended = heads_out.astype(jnp.bfloat16).reshape(tok_rows, head_count * HEAD_DIM)
    return lax.psum_scatter(
        jnp.dot(attended, wo, preferred_element_type=jnp.float32).astype(jnp.bfloat16),
        "tp",
        scatter_dimension=0,
        tiled=True,
    )


def solution(mesh):
    in_specs = (P("ctx", "tp"), P("ctx", "tp"), P("ctx", "tp"), P("tp", None), P())
    out_specs = P(("ctx", "tp"), None)
    return jax.shard_map(
        on_device, mesh=mesh, in_specs=in_specs, out_specs=out_specs, check_vma=False
    )
```

profile of v0, /device:TPU:32, one launch (start us, length us, event | category | flops | bytes accessed | tf_op | source)
XLA Modules:
  0.0 344.5 jit_solution(5539024813720861966)
XLA Ops:
  6.5 0.0 copy-start
  6.5 0.0 all-gather.3.cloned.1.call-start
  6.5 0.7 all-gather.3.cloned.1.call-update
  7.3 0.0 all-gather.5.cloned.1.call-start
  7.3 0.7 all-gather.5.cloned.1.call-update
  8.0 0.0 reduce-scatter.2.cloned.1.call-start
  8.1 0.8 select_reduce_fusion.1
  8.9 3.2 select_reduce_fusion
  12.2 0.4 compare_and_fusion
  12.6 140.9 %all-gather.3.cloned.1.call-done = bf16[8192,768]{1,0:T(8,128)(2,1)} async-done(((bf16[64,768]{1,0:T(8,128)(2,1)}), bf16[8192,768]{1,0:T(8,128)(2,1)}) %all-gather.3.cloned.1.call-update) | async-done | bytes 12582928 | tf_op jit(solution)/shard_map/all_gather | solution.py:71
  153.5 16.6 %copy.19 = bf16[8192,768]{0,1:T(8,128)(2,1)} copy(bf16[8192,768]{1,0:T(8,128)(2,1)} %all-gather.3.cloned.1.call-done) | data formatting | bytes 25165824 | tf_op jit(solution)/shard_map/all_gather | solution.py:71
  170.2 0.0 copy-done
  170.2 6.8 %fusion.34 = (f32[6,64]{1,0:T(8,128)S(1)}, f32[6,64,8192]{2,1,0:T(8,128)S(1)}) fusion(bf16[8192,6,128]{0,2,1:T(8,128)(2,1)} %bitcast.31, pred[64,8192]{1,0:T(8,128)(4,1)S(1)} %compare_and_fusion, bf16[64,768]{1,0:T(8,128)(2,1)S(1)} %copy-done), kind=kOutput, calls=%fused_computation.43 | convolution fusion | flops 814743168 | bytes 25789952 | tf_op jit(solution)/shard_map/qhd,khd->hqk/dot_general | solution.py:33
  177.0 0.0 copy-start.2
  177.0 4.6 %copy-done.2 = f32[6,64,8192]{2,1,0:T(8,128)} copy-done((f32[6,64,8192]{2,1,0:T(8,128)}, f32[6,64,8192]{2,1,0:T(8,128)S(1)}, u32[]{:S(2)}) %copy-start.2) | copy-done | bytes 12582936
  181.6 2.0 fusion
  183.5 110.6 %all-gather.5.cloned.1.call-done = bf16[8192,768]{1,0:T(8,128)(2,1)} async-done(((bf16[64,768]{1,0:T(8,128)(2,1)}), bf16[8192,768]{1,0:T(8,128)(2,1)}) %all-gather.5.cloned.1.call-update) | async-done | bytes 12582928 | tf_op jit(solution)/shard_map/all_gather | solution.py:72
  294.1 0.0 slice-start
  294.1 15.9 %copy.22 = bf16[8192,768]{0,1:T(8,128)(2,1)} copy(bf16[8192,768]{1,0:T(8,128)(2,1)} %all-gather.5.cloned.1.call-done) | data formatting | bytes 25165824 | tf_op jit(solution)/shard_map/all_gather | solution.py:72
  310.0 0.0 copy-start.1
  310.0 0.0 slice-start.1
  310.0 10.8 %fusion.17 = bf16[6,8,8,128]{3,2,1,0:T(8,128)(2,1)S(1)} fusion(bf16[8192,6,128]{0,2,1:T(8,128)(2,1)} %bitcast.30, f32[6,64,8192]{2,1,0:T(8,128)} %copy-done.2, f32[6,64]{1,0:T(8,128)S(1)} %broadcast_maximum_fusion, f32[64,6]{0,1:T(8,128)S(1)} %bitcast.34, pred[64]{0:T(512)(128)(4,1)S(1)} %fusion.33), kind=kOutput, calls=%fused_computation.14 | convolution fusion | flops 811745280 | bytes 25267264 | tf_op jit(solution)/shard_map/hqk,khd->qhd/dot_general | solution.py:40
  320.9 0.0 slice-done
  320.9 0.0 slice-done.1
  320.9 1.7 convolution_convert_fusion
  322.6 0.0 reduce-scatter.2.cloned.1.call-update
  322.6 15.4 %reduce-scatter.2.cloned.1.call-done = bf16[32,3072]{1,0:T(8,128)(2,1)} async-done(((bf16[64,3072]{1,0:T(8,128)(2,1)}), bf16[32,3072]{1,0:T(8,128)(2,1)}) %reduce-scatter.2.cloned.1.call-update) | async-done | bytes 196624 | tf_op jit(solution)/shard_map/reduce_scatter | solution.py:89
  338.0 0.0 copy-done.1
  (6 shorter events, 0.0 us)
Async XLA Ops:
  6.5 163.6 %copy-start = (bf16[64,768]{1,0:T(8,128)(2,1)S(1)}, bf16[64,768]{1,0:T(8,128)(2,1)}, u32[]{:S(2)}) copy-start(bf16[64,768]{1,0:T(8,128)(2,1)} %param.5) | copy-start | bytes 294916
  6.5 147.0 %all-gather.3.cloned.1.call-start = ((), (), s32[]{:S(2)}) async-start(), calls=%async_computation.1 | async-start | bytes 12681216 | tf_op jit(solution)/shard_map/all_gather | solution.py:71
  7.3 286.9 %all-gather.5.cloned.1.call-start = ((), (), s32[]{:S(2)}) async-start(), calls=%async_computation.2 | async-start | bytes 12681216 | tf_op jit(solution)/shard_map/all_gather | solution.py:72
  8.0 330.0 %reduce-scatter.2.cloned.1.call-start = ((), (), s32[]{:S(2)}) async-start(), calls=%async_computation.3 | async-start | bytes 589824 | tf_op jit(solution)/shard_map/reduce_scatter | solution.py:89
  177.0 4.6 %copy-start.2 = (f32[6,64,8192]{2,1,0:T(8,128)}, f32[6,64,8192]{2,1,0:T(8,128)S(1)}, u32[]{:S(2)}) copy-start(f32[6,64,8192]{2,1,0:T(8,128)S(1)} %get-tuple-element.6) | copy-start | bytes 37748740
  294.1 26.7 %slice-start = ((s8[4718592]{0:T(1024)(128)(4,1)}), s8[524288]{0:T(1024)(128)(4,1)S(1)}, s32[]{:S(2)}) async-start(s8[4718592]{0:T(1024)(128)(4,1)} %bitcast.32), calls=%async_computation.4 | async-start | bytes 1048576
  310.0 28.0 %copy-start.1 = (bf16[64,768]{1,0:T(8,128)(2,1)S(1)}, bf16[64,768]{1,0:T(8,128)(2,1)}, u32[]{:S(2)}) copy-start(bf16[64,768]{1,0:T(8,128)(2,1)} %param.5) | copy-start | bytes 294916
  310.0 10.8 %slice-start.1 = ((s8[4718592]{0:T(1024)(128)(4,1)}), s8[4194304]{0:T(1024)(128)(4,1)S(1)}, s32[]{:S(2)}) async-start(s8[4718592]{0:T(1024)(128)(4,1)} %bitcast.32), calls=%async_computation.5 | async-start | bytes 8388608
Sparse Core Ops, SparseCore 0:
  11.2 142.2 all-gather.2
  157.4 136.7 all-gather.4
  322.7 15.2 reduce-scatter.1
where the time goes:
time: 347 us; the launch traced here: 345 us
  waiting for transfers between devices  268 us (77%)
  local copies, waits for them, and re-layouts  37.1 us (11%)
  matrix products  19.3 us (6%)
  between operations  13.2 us (4%)
  other arithmetic  6.48 us (2%)
    all_gather x1, waiting for transfers between devices, on_device(): key_piece = lax.all_gather(keys, 'ctx', axis=0, tiled=True)  141 us
    all_gather x1, waiting for transfers between devices, on_device(): value_piece = lax.all_gather(values, 'ctx', axis=0, tiled=True)  111 us
    all_gather x1, local copies, waits for them, and re-layouts, on_device(): key_piece = lax.all_gather(keys, 'ctx', axis=0, tiled=True)  16.6 us
    all_gather x1, local copies, waits for them, and re-layouts, on_device(): value_piece = lax.all_gather(values, 'ctx', axis=0, tiled=True)  15.9 us
    reduce_scatter x1, waiting for transfers between devices, on_device(): lax.psum_scatter(jnp.dot(attended, wo, preferred_element_type=jnp.float32...  15.4 us
    dot_general x1, matrix products, piece_update(): jnp.einsum('hqk,khd->qhd', weights.astype(jnp.bfloat16), value_heads, pre...  10.8 us
  transfers between devices with their start and end apart: 3, of which 3 were waited for; matrix products, arithmetic and copies ran while one was open for 9% of the time, Pallas kernels for 0%

commit v1 on v0

v1 whole, which is shorter than its diff:
```python
import functools
import math

import jax
import jax.numpy as jnp
from jax import lax
from jax.experimental import pallas as pl
from jax.experimental.pallas import tpu as pltpu
from jax.sharding import Mesh, PartitionSpec as P

HEAD_DIM = 128
FRAME = 64
PLANES = 8
COLUMNS = 8
HEADS = 6
WIDE = HEADS * HEAD_DIM
STATS = 128
CTX = ("z", "xh", "y", "core")
MASKED = -(2.0**24)
FLOOR = -(2.0**22)
EXP2_SCALE = math.log2(math.e) / math.sqrt(HEAD_DIM)


def fill_bias(bias_ref, frames, counts_ref, my_plane, my_core):
    rows = lax.broadcasted_iota(jnp.int32, (FRAME, 128), 0)
    lanes = lax.broadcasted_iota(jnp.int32, (FRAME, 128), 1)
    query_frames = (my_plane * COLUMNS + lanes) * 2 + my_core
    for i, frame in enumerate(frames):
        allowed = (rows < counts_ref[frame]) & (frame <= query_frames)
        bias_ref[i * FRAME : (i + 1) * FRAME, :] = jnp.where(allowed, 0.0, MASKED).astype(
            jnp.bfloat16
        )


def block_frame(place, offset, other):
    plane, column, core = place
    block_plane = lax.rem(plane + offset + PLANES, PLANES)
    return (block_plane * COLUMNS + column) * 2 + (1 - core if other else core)


def attend(offsets, has_state, last, *refs):
    place_ref, counts_ref, q_ref, *refs = refs
    kv_refs, refs = refs[: len(offsets)], refs[len(offsets) :]
    if has_state:
        acc_in, max_in, sum_in, *refs = refs
    outs, (bias_ref, hot_ref) = refs[:-2], refs[-2:]
    place = plane, column, core = place_ref[0], place_ref[1], place_ref[2]
    sign = 2 * core - 1
    blocks, frames = [], []
    for ref, (kind, distance, other_sender) in zip(kv_refs, offsets):
        direction = -sign if other_sender else sign
        for slot in range(2):
            if kind == "half":
                break
            blocks.append((ref, slot))
            frames.append(block_frame(place, direction * distance, (slot == 1) != other_sender))
        if kind == "half":
            blocks.append((ref, 0))
            frames.append(block_frame(place, distance, other_sender))
    fill_bias(bias_ref, frames, counts_ref, plane, core)
    rows = lax.broadcasted_iota(jnp.int32, (FRAME, 128), 1)
    for j in range(COLUMNS):
        hot_ref[j * FRAME : (j + 1) * FRAME, :] = jnp.where(rows == j, 1.0, 0.0).astype(jnp.bfloat16)
    keys_n = len(blocks) * FRAME
    ones = jnp.ones((keys_n, 128), jnp.bfloat16)
    q_tile = 256
    for h in range(HEADS):
        cols = slice(h * HEAD_DIM, (h + 1) * HEAD_DIM)
        k_head = jnp.concatenate([ref[slot, 0, :, cols] for ref, slot in blocks], axis=0)
        v_head = jnp.concatenate([ref[slot, 1, :, cols] for ref, slot in blocks], axis=0)
        k_wide = jnp.concatenate([k_head, bias_ref[...]], axis=1)
        v_wide = jnp.concatenate([v_head, ones], axis=1)
        for t in range(COLUMNS * FRAME // q_tile):
            at = slice(t * q_tile, (t + 1) * q_tile)
            frames_at = slice(t * q_tile // FRAME, (t + 1) * q_tile // FRAME)
            q_head = q_ref[frames_at, :, cols].reshape(q_tile, HEAD_DIM)
            q_wide = jnp.concatenate([q_head, hot_ref[at, :]], axis=1)
            scores = lax.dot_general(
                q_wide, k_wide, (((1,), (1,)), ((), ())), preferred_element_type=jnp.float32
            )
            top = jnp.maximum(jnp.max(scores, axis=1, keepdims=True), FLOOR)
            if has_state:
                before = max_in[at, h : h + 1]
                top = jnp.maximum(top, before)
            weights = jnp.exp2((scores - top) * EXP2_SCALE).astype(jnp.bfloat16)
            both = jnp.dot(weights, v_wide, preferred_element_type=jnp.float32)
            acc, total = both[:, :HEAD_DIM], both[:, HEAD_DIM : HEAD_DIM + 1]
            if has_state:
                fade = jnp.exp2((before - top) * EXP2_SCALE)
                acc = acc + acc_in[at, cols] * fade
                total = total + sum_in[at, h : h + 1] * fade
            if not last:
                acc_out, max_out, sum_out = outs
                acc_out[at, cols] = acc
                max_out[at, h : h + 1] = top
                sum_out[at, h : h + 1] = total
            else:
                (out,) = outs
                mean = (acc * (1.0 / jnp.maximum(total, 1e-30))).astype(jnp.bfloat16)
                out[frames_at, :, cols] = mean.reshape(q_tile // FRAME, FRAME, HEAD_DIM)
                parts = []
                for value, count in ((top, 3), (total, 2)):
                    for _ in range(count):
                        part = value.astype(jnp.bfloat16)
                        parts.append(part)
                        value = value - part.astype(jnp.float32)
                for i, part in enumerate(parts):
                    lane = WIDE + h * 8 + i
                    out[frames_at, :, lane : lane + 1] = part.reshape(q_tile // FRAME, FRAME, 1)


def attend_call(place, counts, q_all, kv, offsets, state, last):
    rows = COLUMNS * FRAME
    keys_n = sum(1 if kind == "half" else 2 for kind, _, _ in offsets) * FRAME
    if last:
        out_shape = jax.ShapeDtypeStruct((COLUMNS, FRAME, WIDE + STATS), jnp.bfloat16)
        out_specs = pl.BlockSpec(memory_space=pltpu.VMEM)
    else:
        out_shape = [
            jax.ShapeDtypeStruct((rows, WIDE), jnp.float32),
            jax.ShapeDtypeStruct((rows, 128), jnp.float32),
            jax.ShapeDtypeStruct((rows, 128), jnp.float32),
        ]
        out_specs = [pl.BlockSpec(memory_space=pltpu.VMEM)] * 3
    vmem = pl.BlockSpec(memory_space=pltpu.VMEM)
    smem = pl.BlockSpec(memory_space=pltpu.SMEM)
    flops = 2 * 2 * rows * keys_n * WIDE
    return pl.pallas_call(
        functools.partial(attend, offsets, state is not None, last),
        out_shape=out_shape,
        in_specs=[smem, smem] + [vmem] * (1 + len(kv) + (3 if state is not None else 0)),
        out_specs=out_specs,
        scratch_shapes=[
            pltpu.VMEM((keys_n, 128), jnp.bfloat16),
            pltpu.VMEM((rows, 128), jnp.bfloat16),
        ],
        compiler_params=pltpu.CompilerParams(vmem_limit_bytes=40 * 2**20),
        cost_estimate=pl.CostEstimate(
            flops=flops, bytes_accessed=4 * 2**20, transcendentals=rows * keys_n * HEADS
        ),
        name="attend_last" if last else "attend_first",
    )(place, counts, q_all, *kv, *(state if state is not None else ()))


def project(tp_count, place_ref, counts_ref, parts_ref, wo_ref, send_ref, keep_ref, att_ref):
    plane, column, core, tp = place_ref[0], place_ref[1], place_ref[2], place_ref[3]
    frame = (plane * COLUMNS + column) * 2 + core
    rows = lax.broadcasted_iota(jnp.int32, (FRAME, 1), 0)
    live = rows < counts_ref[frame]
    for h in range(HEADS):
        cols = slice(h * HEAD_DIM, (h + 1) * HEAD_DIM)
        tops, totals = [], []
        for j in range(COLUMNS):
            lane = WIDE + h * 8
            st = parts_ref[j, :, WIDE : WIDE + STATS].astype(jnp.float32)
            st = st[:, h * 8 : h * 8 + 5]
            tops.append(st[:, 0:1] + st[:, 1:2] + st[:, 2:3])
            totals.append(st[:, 3:4] + st[:, 4:5])
        top = functools.reduce(jnp.maximum, tops)
        shares = [n * jnp.exp2((m - top) * EXP2_SCALE) for m, n in zip(tops, totals)]
        total = functools.reduce(jnp.add, shares)
        acc = functools.reduce(
            jnp.add,
            [parts_ref[j, :, cols].astype(jnp.float32) * shares[j] for j in range(COLUMNS)],
        )
        out = jnp.where(live, acc / total, 0.0)
        att_ref[:, cols] = out.astype(jnp.bfloat16)
    half = FRAME // tp_count
    mine = pl.ds(pl.multiple_of(tp * half, half), half)
    theirs = pl.ds(pl.multiple_of((1 - tp) * half, half), half)
    att = jnp.concatenate([att_ref[theirs, :], att_ref[mine, :]], axis=0)
    step = 512
    for n in range(0, wo_ref.shape[1], step):
        out = jnp.dot(att, wo_ref[:, n : n + step], preferred_element_type=jnp.float32)
        send_ref[:, n : n + step] = out[:half].astype(jnp.bfloat16)
        keep_ref[:, n : n + step] = out[half:]


def project_call(place, counts, parts, wo):
    vmem = pl.BlockSpec(memory_space=pltpu.VMEM)
    smem = pl.BlockSpec(memory_space=pltpu.SMEM)
    width = wo.shape[1]
    return pl.pallas_call(
        functools.partial(project, 2),
        out_shape=[
            jax.ShapeDtypeStruct((FRAME // 2, width), jnp.bfloat16),
            jax.ShapeDtypeStruct((FRAME // 2, width), jnp.float32),
        ],
        in_specs=[smem, smem, vmem, vmem],
        out_specs=[vmem, vmem],
        scratch_shapes=[pltpu.VMEM((FRAME, WIDE), jnp.bfloat16)],
        compiler_params=pltpu.CompilerParams(vmem_limit_bytes=40 * 2**20),
        name="project",
    )(place, counts, parts, wo)


SWAP = [(0, 1), (1, 0)]


def split_ring(distance):
    return [
        (z * 2 + c, (z + (distance if c == 0 else -distance)) % PLANES * 2 + c)
        for z in range(PLANES)
        for c in range(2)
    ]


def on_device(queries, keys, values, wo, frame_tokens):
    place = jnp.stack(
        [
            lax.axis_index("z"),
            lax.axis_index("xh") * 4 + lax.axis_index("y"),
            lax.axis_index("core"),
            lax.axis_index("tp"),
        ]
    ).astype(jnp.int32)
    own = jnp.stack([keys, values])
    own2 = jnp.stack([own, lax.ppermute(own, "core", SWAP)])
    zc = ("z", "core")
    near = lax.ppermute(own2, zc, split_ring(1))
    second = lax.ppermute(own2, zc, split_ring(2))
    q_all = lax.all_to_all(
        jnp.broadcast_to(queries[None], (COLUMNS, FRAME, WIDE)), ("xh", "y"), 0, 0, tiled=True
    )
    third = lax.ppermute(second, zc, split_ring(1))
    fourth = lax.ppermute(second[:1], zc, split_ring(2))
    near_o = lax.ppermute(near, "core", SWAP)
    second_o = lax.ppermute(second, "core", SWAP)
    third_o = lax.ppermute(third, "core", SWAP)
    fourth_o = lax.ppermute(fourth, "core", SWAP)
    first = [own2, near, near_o, second, second_o]
    first_off = [
        ("both", 0, False),
        ("both", 1, False),
        ("both", 1, True),
        ("both", 2, False),
        ("both", 2, True),
    ]
    rest = [third, third_o, fourth, fourth_o]
    rest_off = [("both", 3, False), ("both", 3, True), ("half", 4, False), ("half", 4, True)]
    state = attend_call(place, frame_tokens, q_all, first, first_off, None, False)
    partial = attend_call(place, frame_tokens, q_all, rest, rest_off, state, True)
    parts = lax.all_to_all(partial, ("xh", "y"), 0, 0, tiled=True)
    send, keep = project_call(place, frame_tokens, parts, wo)
    got = lax.ppermute(send, "tp", SWAP)
    return (keep + got.astype(jnp.float32)).astype(jnp.bfloat16)


def solution(mesh):
    fine = Mesh(mesh.devices.reshape(PLANES, 2, 4, 2, 2), CTX + ("tp",))
    in_specs = (P(CTX, "tp"), P(CTX, "tp"), P(CTX, "tp"), P("tp", None), P())
    out_specs = P(CTX + ("tp",), None)
    return jax.shard_map(
        on_device, mesh=fine, in_specs=in_specs, out_specs=out_specs, check_vma=False
    )
```

time: 347 us -> 86.5 us (0.25)
  waiting for transfers between devices: 268 us -> 23 us
  local copies, waits for them, and re-layouts: 37.1 us -> 4.85 us
  blocking collectives: 0 us -> 21.3 us
  starting transfers between devices: 0.08 us -> 19.8 us
  matrix products: 19.3 us -> 0 us
  Pallas kernels: 0 us -> 15.4 us
  between operations: 13.2 us -> 0.07 us
  other arithmetic: 6.48 us -> 1.81 us
    all_gather x2 -> x0, waiting for transfers between devices: 252 us -> none  [the longest x1 141 us: on_device(): key_piece = lax.all_gather(keys, 'ctx', axis=0, tiled=True)]
    all_gather x2 -> x0, local copies, waits for them, and re-layouts: 32.5 us -> none  [the longest x1 16.6 us: on_device(): key_piece = lax.all_gather(keys, 'ctx', axis=0, tiled=True)]
    all_to_all x0 -> x1, blocking collectives: none -> 21.3 us  [on_device(): parts = lax.all_to_all(partial, ('xh', 'y'), 0, 0, tiled=True)]
    ppermute x0 -> x10, waiting for transfers between devices: none -> 20.8 us  [the longest x1 9.08 us: on_device(): second = lax.ppermute(own2, zc, split_ring(2))]
    dot_general x3 -> x0, matrix products: 19.3 us -> none  [the longest x1 10.8 us: piece_update(): jnp.einsum('hqk,khd->qhd', weights.astype(jnp.bfloat16), value_heads, pre...]
    reduce_scatter x1 -> x0, waiting for transfers between devices: 15.4 us -> none  [on_device(): lax.psum_scatter(jnp.dot(attended, wo, preferred_element_type=jnp.float32...]
    pallas_call x0 -> x3, Pallas kernels: none -> 15.4 us  [the longest x2 12.1 us: attend_call(): pl.pallas_call(functools.partial(attend, offsets, state is not None, last...]
    ppermute x0 -> x10, starting transfers between devices: none -> 12.9 us  [the longest x1 4.73 us: on_device(): fourth = lax.ppermute(second[:1], zc, split_ring(2))]
  transfers between devices with their start and end apart: 3 -> 11, of which waited for: 3 -> 5; matrix products, arithmetic and copies ran while one was open for 9% -> 2% of each run, Pallas kernels for 0% -> 5%
where the time goes in v1:
time: 86.5 us; the launch traced here: 86.2 us
  waiting for transfers between devices  23 us (27%)
  blocking collectives  21.3 us (25%)
  starting transfers between devices  19.8 us (23%)
  Pallas kernels  15.4 us (18%)
  local copies, waits for them, and re-layouts  4.85 us (6%)
  other arithmetic  1.81 us (2%)
    all_to_all x1, blocking collectives, on_device(): parts = lax.all_to_all(partial, ('xh', 'y'), 0, 0, tiled=True)  21.3 us
    pallas_call x2, Pallas kernels, attend_call(): pl.pallas_call(functools.partial(attend, offsets, state is not None, last...  12.1 us
    ppermute x1, waiting for transfers between devices, on_device(): second = lax.ppermute(own2, zc, split_ring(2))  9.08 us
    all_to_all x1, starting transfers between devices, on_device(): lax.all_to_all(jnp.broadcast_to(queries[None], (COLUMNS, FRAME, WIDE)), (...  6.93 us
    ppermute x1, waiting for transfers between devices, on_device(): fourth = lax.ppermute(second[:1], zc, split_ring(2))  5.23 us
    ppermute x1, waiting for transfers between devices, on_device(): got = lax.ppermute(send, 'tp', SWAP)  5.06 us
    ppermute x1, starting transfers between devices, on_device(): fourth = lax.ppermute(second[:1], zc, split_ring(2))  4.73 us
    ppermute x1, starting transfers between devices, on_device(): second = lax.ppermute(own2, zc, split_ring(2))  3.35 us
  transfers between devices with their start and end apart: 11, of which 5 were waited for; matrix products, arithmetic and copies ran while one was open for 2% of the time, Pallas kernels for 5%

profile of v1, /device:TPU:32, one launch (start us, length us, event | category | flops | bytes accessed | tf_op | source)
XLA Modules:
  0.0 86.2 jit_solution(9121048132877325087)
XLA Ops:
  0.0 1.0 %fusion = (bf16[1,2,64,768]{3,2,1,0:T(8,128)(2,1)S(1)}, bf16[2,64,768]{2,1,0:T(8,128)(2,1)S(1)}) fusion(bf16[1,64,768]{2,1,0:T(8,128)(2,1)} %bitcast.10, bf16[1,64,768]{2,1,0:T(8,128)(2,1)} %bitcast.11), kind=kLoop, calls=%fused_computation.4 | loop fusion | flops 98304 | bytes 589824 | tf_op jit(solution)/shard_map/stack | solution.py:218
  1.0 0.1 collective-permute-start
  1.1 1.4 %collective-permute-done = bf16[2,64,768]{2,1,0:T(8,128)(2,1)S(1)} collective-permute-done((bf16[2,64,768]{2,1,0:T(8,128)(2,1)S(1)}, bf16[2,64,768]{2,1,0:T(8,128)(2,1)S(1)}, u32[]{:S(2)}, u32[]{:S(2)}) %collective-permute-start) | collective-permute-done | bytes 196640 | tf_op jit(solution)/shard_map/ppermute | solution.py:218
  2.5 3.3 %collective-permute-start.1 = (bf16[2,2,64,768]{3,2,1,0:T(8,128)(2,1)S(1)}, bf16[2,2,64,768]{3,2,1,0:T(8,128)(2,1)S(1)}, u32[]{:S(2)}, u32[]{:S(2)}) collective-permute-start(bf16[2,2,64,768]{3,2,1,0:T(8,128)(2,1)S(1)} %pad_maximum_fusion.refs_3_), channel_id=1, source_target_pairs={{0,64},{2,194},{32,96},{34,226},{64,128},{66,2},{96,160},{98,34},{... | collective-permute-start | bytes 1179656 | tf_op jit(solution)/shard_map/ppermute | solution.py:221
  5.9 3.1 %collective-permute-start.6 = (bf16[2,2,64,768]{3,2,1,0:T(8,128)(2,1)S(1)}, bf16[2,2,64,768]{3,2,1,0:T(8,128)(2,1)S(1)}, u32[]{:S(2)}, u32[]{:S(2)}) collective-permute-start(bf16[2,2,64,768]{3,2,1,0:T(8,128)(2,1)S(1)} %pad_maximum_fusion.refs_3_), channel_id=1, source_target_pairs={{0,32},{2,226},{32,64},{34,2},{64,96},{66,34},{96,128},{98,66},{12... | collective-permute-start | bytes 1179656 | tf_op jit(solution)/shard_map/ppermute | solution.py:220
  9.0 9.1 %collective-permute-done.1.refs_6_ = bf16[2,2,64,768]{3,2,1,0:T(8,128)(2,1)S(1)} collective-permute-done((bf16[2,2,64,768]{3,2,1,0:T(8,128)(2,1)S(1)}, bf16[2,2,64,768]{3,2,1,0:T(8,128)(2,1)S(1)}, u32[]{:S(2)}, u32[]{:S(2)}) %collective-permute-start.1) | collective-permute-done | bytes 393248 | tf_op jit(solution)/shard_map/ppermute | solution.py:221
  18.1 0.4 collective-permute-start.2
  18.5 1.8 %broadcast_in_dim.2 = bf16[8,64,768]{2,1,0:T(8,128)(2,1)} broadcast(bf16[64,768]{1,0:T(8,128)(2,1)} %param.5), dimensions={1,2} | broadcast | bytes 884736 | tf_op jit(solution)/shard_map/broadcast_in_dim | solution.py:223
  20.3 6.9 %all-to-all-start = ((bf16[8,64,768]{2,1,0:T(8,128)(2,1)}), bf16[8,64,768]{2,1,0:T(8,128)(2,1)S(1)}, u32[]{:S(2)}, u32[]{:S(2)}) async-start(bf16[8,64,768]{2,1,0:T(8,128)(2,1)} %broadcast_in_dim.2), calls=%async_computation | async-start | bytes 1572864 | tf_op jit(solution)/shard_map/all_to_all | solution.py:222
  27.3 0.0 collective-permute-start.8
  27.3 0.0 collective-permute-done.6.refs_4_
  27.3 0.5 collective-permute-start.7
  27.8 4.7 %collective-permute-start.4 = (bf16[1,2,64,768]{3,2,1,0:T(8,128)(2,1)S(1)}, bf16[1,2,64,768]{3,2,1,0:T(8,128)(2,1)S(1)}, u32[]{:S(2)}, u32[]{:S(2)}) collective-permute-start(bf16[1,2,64,768]{3,2,1,0:T(8,128)(2,1)S(1)} %slice.4), channel_id=1, source_target_pairs={{0,64},{2,194},{32,96},{34,226},{64,128},{66,2},{96,160},{98,34},{... | collective-permute-start | bytes 589832 | tf_op jit(solution)/shard_map/ppermute | solution.py:226
  32.5 0.0 collective-permute-done.2.refs_3_
  32.5 0.0 collective-permute-start.3
  32.5 5.2 %collective-permute-done.4.refs_5_ = bf16[1,2,64,768]{3,2,1,0:T(8,128)(2,1)S(1)} collective-permute-done((bf16[1,2,64,768]{3,2,1,0:T(8,128)(2,1)S(1)}, bf16[1,2,64,768]{3,2,1,0:T(8,128)(2,1)S(1)}, u32[]{:S(2)}, u32[]{:S(2)}) %collective-permute-start.4) | collective-permute-done | bytes 196640 | tf_op jit(solution)/shard_map/ppermute | solution.py:226
  37.7 0.0 collective-permute-start.5
  37.8 0.0 copy-start.2
  37.8 0.1 pad_add_fusion.refs_0_.place_ref
  37.8 2.2 %all-to-all-done.refs_2_ = bf16[8,64,768]{2,1,0:T(8,128)(2,1)S(1)} async-done(((bf16[8,64,768]{2,1,0:T(8,128)(2,1)}), bf16[8,64,768]{2,1,0:T(8,128)(2,1)S(1)}, u32[]{:S(2)}, u32[]{:S(2)}) %all-to-all-start) | async-done | bytes 786464 | tf_op jit(solution)/shard_map/all_to_all | solution.py:222
  40.0 0.0 collective-permute-done.8.refs_7_
  40.0 0.0 collective-permute-done.7.refs_5_
  40.0 0.0 copy-start.1
  40.1 0.7 copy-done.1
  40.7 4.2 %attend_first.1 = (f32[512,768]{1,0:T(8,128)S(1)}, f32[512,128]{1,0:T(8,128)S(1)}, f32[512,128]{1,0:T(8,128)S(1)}) custom-call(s32[4]{0:T(128)S(1)} %pad_add_fusion.refs_0_.place_ref, s32[128]{0:T(128)S(1)} %copy-done.1, bf16[8,64,768]{2,1,0:T(8,128)(2,1)S(1)} %all-to-all-done.refs_2_, bf16[2,2,64,768]{3,2,1,0:T(8,128)(2,1)S(1)} %pad_maximum_fusion.refs_3_, ...), custom_call_target="tpu_custom_call" | custom-call | flops 1006632960 | bytes 4194304 | tf_op jit(solution)/shard_map/attend_first/pallas_call | solution.py:128
  45.0 0.0 collective-permute-done.5.refs_6_
  45.0 0.0 collective-permute-done.3.refs_4_
  45.0 7.8 %attend_last.1 = bf16[8,64,896]{2,1,0:T(8,128)(2,1)S(1)} custom-call(s32[4]{0:T(128)S(1)} %pad_add_fusion.refs_0_.place_ref, s32[128]{0:T(128)S(1)} %copy-done.1, bf16[8,64,768]{2,1,0:T(8,128)(2,1)S(1)} %all-to-all-done.refs_2_, bf16[2,2,64,768]{3,2,1,0:T(8,128)(2,1)S(1)} %collective-permute-done.2.refs_3_, ...), custom_call_target="tpu_custom_call" | custom-call | flops 603979776 | bytes 4194304 | tf_op jit(solution)/shard_map/attend_last/pallas_call | solution.py:128
  52.8 21.3 %all_to_all.10.parts_ref = bf16[8,64,896]{2,1,0:T(8,128)(2,1)S(1)} all-to-all(bf16[8,64,896]{2,1,0:T(8,128)(2,1)S(1)} %attend_last.1), channel_id=1, replica_groups=mesh['z'=8,'xh'=2,'y'=4,'core'=2,'tp'=2] {'xh','y'}, dimensions={0} | all-to-all | bytes 1835008 | tf_op jit(solution)/shard_map/all_to_all | solution.py:243
  74.1 0.0 copy-done.2
  74.1 0.0 copy-start
  74.1 2.3 %copy-done = bf16[768,3072]{1,0:T(8,128)(2,1)S(1)} copy-done((bf16[768,3072]{1,0:T(8,128)(2,1)S(1)}, bf16[768,3072]{1,0:T(8,128)(2,1)}, u32[]{:S(2)}) %copy-start) | copy-done | bytes 4718616
  76.4 3.3 %project.1 = (bf16[32,3072]{1,0:T(8,128)(2,1)S(1)}, f32[32,3072]{1,0:T(8,128)S(1)}) custom-call(s32[4]{0:T(128)S(1)} %pad_add_fusion.refs_0_.place_ref, s32[128]{0:T(128)S(1)} %copy-done.2, bf16[8,64,896]{2,1,0:T(8,128)(2,1)S(1)} %all_to_all.10.parts_ref, bf16[768,3072]{1,0:T(8,128)(2,1)S(1)} %copy-done), custom_call_target="tpu_custom_call" | custom-call | tf_op jit(solution)/shard_map/project/pallas_call | solution.py:183
  79.7 0.7 collective-permute-start.9
  80.4 5.1 %collective-permute-done.9 = bf16[32,3072]{1,0:T(8,128)(2,1)S(1)} collective-permute-done((bf16[32,3072]{1,0:T(8,128)(2,1)S(1)}, bf16[32,3072]{1,0:T(8,128)(2,1)S(1)}, u32[]{:S(2)}, u32[]{:S(2)}) %collective-permute-start.9) | collective-permute-done | bytes 196640 | tf_op jit(solution)/shard_map/ppermute | solution.py:245
  85.5 0.7 add_convert_fusion
  (2 shorter events, 0.1 us)
Async XLA Ops:
  1.0 1.5 %collective-permute-start = (bf16[2,64,768]{2,1,0:T(8,128)(2,1)S(1)}, bf16[2,64,768]{2,1,0:T(8,128)(2,1)S(1)}, u32[]{:S(2)}, u32[]{:S(2)}) collective-permute-start(bf16[2,64,768]{2,1,0:T(8,128)(2,1)S(1)} %get-tuple-element.16), channel_id=1, source_target_pairs={{0,2},{2,0},{1,3},{3,1},{4,6},{6,4},{5,7},{7,5},{8,10},{10,8},{9,1... | collective-permute-start | bytes 589832 | tf_op jit(solution)/shard_map/ppermute | solution.py:218
  2.5 15.6 %collective-permute-start.1 = (bf16[2,2,64,768]{3,2,1,0:T(8,128)(2,1)S(1)}, bf16[2,2,64,768]{3,2,1,0:T(8,128)(2,1)S(1)}, u32[]{:S(2)}, u32[]{:S(2)}) collective-permute-start(bf16[2,2,64,768]{3,2,1,0:T(8,128)(2,1)S(1)} %pad_maximum_fusion.refs_3_), channel_id=1, source_target_pairs={{0,64},{2,194},{32,96},{34,226},{64,128},{66,2},{96,160},{98,34},{... | collective-permute-start | bytes 1179656 | tf_op jit(solution)/shard_map/ppermute | solution.py:221
  5.9 21.4 %collective-permute-start.6 = (bf16[2,2,64,768]{3,2,1,0:T(8,128)(2,1)S(1)}, bf16[2,2,64,768]{3,2,1,0:T(8,128)(2,1)S(1)}, u32[]{:S(2)}, u32[]{:S(2)}) collective-permute-start(bf16[2,2,64,768]{3,2,1,0:T(8,128)(2,1)S(1)} %pad_maximum_fusion.refs_3_), channel_id=1, source_target_pairs={{0,32},{2,226},{32,64},{34,2},{64,96},{66,34},{96,128},{98,66},{12... | collective-permute-start | bytes 1179656 | tf_op jit(solution)/shard_map/ppermute | solution.py:220
  18.1 14.4 %collective-permute-start.2 = (bf16[2,2,64,768]{3,2,1,0:T(8,128)(2,1)S(1)}, bf16[2,2,64,768]{3,2,1,0:T(8,128)(2,1)S(1)}, u32[]{:S(2)}, u32[]{:S(2)}) collective-permute-start(bf16[2,2,64,768]{3,2,1,0:T(8,128)(2,1)S(1)} %collective-permute-done.1.refs_6_), channel_id=1, source_target_pairs={{0,32},{2,226},{32,64},{34,2},{64,96},{66,34},{96,128},{98,66},{12... | collective-permute-start | bytes 1179656 | tf_op jit(solution)/shard_map/ppermute | solution.py:225
  20.3 19.7 %all-to-all-start = ((bf16[8,64,768]{2,1,0:T(8,128)(2,1)}), bf16[8,64,768]{2,1,0:T(8,128)(2,1)S(1)}, u32[]{:S(2)}, u32[]{:S(2)}) async-start(bf16[8,64,768]{2,1,0:T(8,128)(2,1)} %broadcast_in_dim.2), calls=%async_computation | async-start | bytes 1572864 | tf_op jit(solution)/shard_map/all_to_all | solution.py:222
  27.3 12.8 %collective-permute-start.8 = (bf16[2,2,64,768]{3,2,1,0:T(8,128)(2,1)S(1)}, bf16[2,2,64,768]{3,2,1,0:T(8,128)(2,1)S(1)}, u32[]{:S(2)}, u32[]{:S(2)}) collective-permute-start(bf16[2,2,64,768]{3,2,1,0:T(8,128)(2,1)S(1)} %collective-permute-done.1.refs_6_), channel_id=1, source_target_pairs={{0,2},{2,0},{1,3},{3,1},{4,6},{6,4},{5,7},{7,5},{8,10},{10,8},{9,1... | collective-permute-start | bytes 1179656 | tf_op jit(solution)/shard_map/ppermute | solution.py:228
  27.3 12.8 %collective-permute-start.7 = (bf16[2,2,64,768]{3,2,1,0:T(8,128)(2,1)S(1)}, bf16[2,2,64,768]{3,2,1,0:T(8,128)(2,1)}, u32[]{:S(2)}, u32[]{:S(2)}) collective-permute-start(bf16[2,2,64,768]{3,2,1,0:T(8,128)(2,1)S(1)} %collective-permute-done.6.refs_4_), channel_id=1, source_target_pairs={{0,2},{2,0},{1,3},{3,1},{4,6},{6,4},{5,7},{7,5},{8,10},{10,8},{9,1... | collective-permute-start | bytes 1179656 | tf_op jit(solution)/shard_map/ppermute | solution.py:227
  27.8 10.0 %collective-permute-start.4 = (bf16[1,2,64,768]{3,2,1,0:T(8,128)(2,1)S(1)}, bf16[1,2,64,768]{3,2,1,0:T(8,128)(2,1)S(1)}, u32[]{:S(2)}, u32[]{:S(2)}) collective-permute-start(bf16[1,2,64,768]{3,2,1,0:T(8,128)(2,1)S(1)} %slice.4), channel_id=1, source_target_pairs={{0,64},{2,194},{32,96},{34,226},{64,128},{66,2},{96,160},{98,34},{... | collective-permute-start | bytes 589832 | tf_op jit(solution)/shard_map/ppermute | solution.py:226
  32.5 12.5 %collective-permute-start.3 = (bf16[2,2,64,768]{3,2,1,0:T(8,128)(2,1)S(1)}, bf16[2,2,64,768]{3,2,1,0:T(8,128)(2,1)S(1)}, u32[]{:S(2)}, u32[]{:S(2)}) collective-permute-start(bf16[2,2,64,768]{3,2,1,0:T(8,128)(2,1)S(1)} %collective-permute-done.2.refs_3_), channel_id=1, source_target_pairs={{0,2},{2,0},{1,3},{3,1},{4,6},{6,4},{5,7},{7,5},{8,10},{10,8},{9,1... | collective-permute-start | bytes 1179656 | tf_op jit(solution)/shard_map/ppermute | solution.py:229
  37.7 7.2 %collective-permute-start.5 = (bf16[1,2,64,768]{3,2,1,0:T(8,128)(2,1)S(1)}, bf16[1,2,64,768]{3,2,1,0:T(8,128)(2,1)S(1)}, u32[]{:S(2)}, u32[]{:S(2)}) collective-permute-start(bf16[1,2,64,768]{3,2,1,0:T(8,128)(2,1)S(1)} %collective-permute-done.4.refs_5_), channel_id=1, source_target_pairs={{0,2},{2,0},{1,3},{3,1},{4,6},{6,4},{5,7},{7,5},{8,10},{10,8},{9,1... | collective-permute-start | bytes 589832 | tf_op jit(solution)/shard_map/ppermute | solution.py:230
  37.8 36.3 %copy-start.2 = (s32[128]{0:T(128)S(1)}, s32[128]{0:T(128)}, u32[]{:S(2)}) copy-start(s32[128]{0:T(128)} %counts_ref.1) | copy-start | bytes 1540
  40.0 0.7 copy-start.1
  74.1 2.3 %copy-start = (bf16[768,3072]{1,0:T(8,128)(2,1)S(1)}, bf16[768,3072]{1,0:T(8,128)(2,1)}, u32[]{:S(2)}) copy-start(bf16[768,3072]{1,0:T(8,128)(2,1)} %wo_ref.1) | copy-start | bytes 14155780
  79.7 5.8 %collective-permute-start.9 = (bf16[32,3072]{1,0:T(8,128)(2,1)S(1)}, bf16[32,3072]{1,0:T(8,128)(2,1)S(1)}, u32[]{:S(2)}, u32[]{:S(2)}) collective-permute-start(bf16[32,3072]{1,0:T(8,128)(2,1)S(1)} %get-tuple-element.14), channel_id=1, source_target_pairs={{0,1},{1,0},{2,3},{3,2},{4,5},{5,4},{6,7},{7,6},{8,9},{9,8},{10,11... | collective-permute-start | bytes 589832 | tf_op jit(solution)/shard_map/ppermute | solution.py:245

commit v2 on v1

--- a/solution.py
+++ b/solution.py
@@ -15,6 +15,8 @@
 HEADS = 6
 WIDE = HEADS * HEAD_DIM
 STATS = 128
+TOP_PARTS, TOTAL_PARTS = 3, 2
+Q_TILE = 256
 CTX = ("z", "xh", "y", "core")
 MASKED = -(2.0**24)
 FLOOR = -(2.0**22)
@@ -63,50 +65,58 @@
         hot_ref[j * FRAME : (j + 1) * FRAME, :] = jnp.where(rows == j, 1.0, 0.0).astype(jnp.bfloat16)
     keys_n = len(blocks) * FRAME
     ones = jnp.ones((keys_n, 128), jnp.bfloat16)
-    q_tile = 256
-    for h in range(HEADS):
-        cols = slice(h * HEAD_DIM, (h + 1) * HEAD_DIM)
-        k_head = jnp.concatenate([ref[slot, 0, :, cols] for ref, slot in blocks], axis=0)
-        v_head = jnp.concatenate([ref[slot, 1, :, cols] for ref, slot in blocks], axis=0)
-        k_wide = jnp.concatenate([k_head, bias_ref[...]], axis=1)
-        v_wide = jnp.concatenate([v_head, ones], axis=1)
-        for t in range(COLUMNS * FRAME // q_tile):
-            at = slice(t * q_tile, (t + 1) * q_tile)
-            frames_at = slice(t * q_tile // FRAME, (t + 1) * q_tile // FRAME)
-            q_head = q_ref[frames_at, :, cols].reshape(q_tile, HEAD_DIM)
+    lanes = lax.broadcasted_iota(jnp.int32, (Q_TILE, 128), 1)
+    for t in range(COLUMNS * FRAME // Q_TILE):
+        at = slice(t * Q_TILE, (t + 1) * Q_TILE)
+        frames_at = slice(t * Q_TILE // FRAME, (t + 1) * Q_TILE // FRAME)
+        tops = jnp.zeros((Q_TILE, 128), jnp.float32)
+        totals = jnp.zeros((Q_TILE, 128), jnp.float32)
+        for h in range(HEADS):
+            cols = slice(h * HEAD_DIM, (h + 1) * HEAD_DIM)
+            k_head = jnp.concatenate([ref[slot, 0, :, cols] for ref, slot in blocks], axis=0)
+            v_head = jnp.concatenate([ref[slot, 1, :, cols] for ref, slot in blocks], axis=0)
+            k_wide = jnp.concatenate([k_head, bias_ref[...]], axis=1)
+            v_wide = jnp.concatenate([v_head, ones], axis=1)
+            q_head = q_ref[frames_at, :, cols].reshape(Q_TILE, HEAD_DIM)
             q_wide = jnp.concatenate([q_head, hot_ref[at, :]], axis=1)
             scores = lax.dot_general(
                 q_wide, k_wide, (((1,), (1,)), ((), ())), preferred_element_type=jnp.float32
             )
-            top = jnp.maximum(jnp.max(scores, axis=1, keepdims=True), FLOOR)
+            top = jnp.broadcast_to(jnp.max(scores, axis=1, keepdims=True), (Q_TILE, 128))
             if has_state:
-                before = max_in[at, h : h + 1]
+                before = max_in[h, at, :]
                 top = jnp.maximum(top, before)
-            weights = jnp.exp2((scores - top) * EXP2_SCALE).astype(jnp.bfloat16)
+            else:
+                top = jnp.maximum(top, FLOOR)
+            weights = jnp.exp2((scores - jnp.tile(top, (1, keys_n // 128))) * EXP2_SCALE).astype(
+                jnp.bfloat16
+            )
             both = jnp.dot(weights, v_wide, preferred_element_type=jnp.float32)
-            acc, total = both[:, :HEAD_DIM], both[:, HEAD_DIM : HEAD_DIM + 1]
+            acc, total = both[:, :HEAD_DIM], both[:, HEAD_DIM:]
             if has_state:
                 fade = jnp.exp2((before - top) * EXP2_SCALE)
                 acc = acc + acc_in[at, cols] * fade
-                total = total + sum_in[at, h : h + 1] * fade
+                total = total + sum_in[h, at, :] * fade
             if not last:
-                acc_out, max_out, sum_out = outs
-                acc_out[at, cols] = acc
-                max_out[at, h : h + 1] = top
-                sum_out[at, h : h + 1] = total
+                outs[0][at, cols] = acc
+                outs[1][h, at, :] = top
+                outs[2][h, at, :] = total
             else:
-                (out,) = outs
+                tops = jnp.where(lanes == h, top, tops)
+                totals = jnp.where(lanes == h, total, totals)
                 mean = (acc * (1.0 / jnp.maximum(total, 1e-30))).astype(jnp.bfloat16)
-                out[frames_at, :, cols] = mean.reshape(q_tile // FRAME, FRAME, HEAD_DIM)
-                parts = []
-                for value, count in ((top, 3), (total, 2)):
-                    for _ in range(count):
-                        part = value.astype(jnp.bfloat16)
-                        parts.append(part)
-                        value = value - part.astype(jnp.float32)
-                for i, part in enumerate(parts):
-                    lane = WIDE + h * 8 + i
-                    out[frames_at, :, lane : lane + 1] = part.reshape(q_tile // FRAME, FRAME, 1)
+                outs[0][frames_at, :, cols] = mean.reshape(Q_TILE // FRAME, FRAME, HEAD_DIM)
+        if last:
+            packed, slot = jnp.zeros((Q_TILE, 128), jnp.float32), 0
+            for value, count in ((tops, TOP_PARTS), (totals, TOTAL_PARTS)):
+                for _ in range(count):
+                    part = value.astype(jnp.bfloat16).astype(jnp.float32)
+                    value = value - part
+                    packed = packed + (pltpu.roll(part, slot * 8, 1) if slot else part)
+                    slot += 1
+            outs[0][frames_at, :, WIDE:] = packed.astype(jnp.bfloat16).reshape(
+                Q_TILE // FRAME, FRAME, STATS
+            )
 
 
 def attend_call(place, counts, q_all, kv, offsets, state, last):
@@ -118,8 +128,8 @@
     else:
         out_shape = [
             jax.ShapeDtypeStruct((rows, WIDE), jnp.float32),
-            jax.ShapeDtypeStruct((rows, 128), jnp.float32),
-            jax.ShapeDtypeStruct((rows, 128), jnp.float32),
+            jax.ShapeDtypeStruct((HEADS, rows, 128), jnp.float32),
+            jax.ShapeDtypeStruct((HEADS, rows, 128), jnp.float32),
         ]
         out_specs = [pl.BlockSpec(memory_space=pltpu.VMEM)] * 3
     vmem = pl.BlockSpec(memory_space=pltpu.VMEM)
@@ -134,7 +144,7 @@
             pltpu.VMEM((keys_n, 128), jnp.bfloat16),
             pltpu.VMEM((rows, 128), jnp.bfloat16),
         ],
-        compiler_params=pltpu.CompilerParams(vmem_limit_bytes=40 * 2**20),
+        compiler_params=pltpu.CompilerParams(vmem_limit_bytes=24 * 2**20),
         cost_estimate=pl.CostEstimate(
             flops=flops, bytes_accessed=4 * 2**20, transcendentals=rows * keys_n * HEADS
         ),
@@ -147,23 +157,28 @@
     frame = (plane * COLUMNS + column) * 2 + core
     rows = lax.broadcasted_iota(jnp.int32, (FRAME, 1), 0)
     live = rows < counts_ref[frame]
+
+    def part(stats, i):
+        return pltpu.roll(stats, 128 - 8 * i, 1) if i else stats
+
+    tops, totals = [], []
+    for j in range(COLUMNS):
+        stats = parts_ref[j, :, WIDE:].astype(jnp.float32)
+        tops.append(sum(part(stats, i) for i in range(1, TOP_PARTS)) + stats)
+        totals.append(sum(part(stats, TOP_PARTS + i) for i in range(TOTAL_PARTS)))
+    top = functools.reduce(jnp.maximum, tops)
+    shares = [n * jnp.exp2((m - top) * EXP2_SCALE) for m, n in zip(tops, totals)]
+    total = functools.reduce(jnp.add, shares)
+    shares = [jnp.where(live, share / total, 0.0) for share in shares]
     for h in range(HEADS):
         cols = slice(h * HEAD_DIM, (h + 1) * HEAD_DIM)
-        tops, totals = [], []
-        for j in range(COLUMNS):
-            lane = WIDE + h * 8
-            st = parts_ref[j, :, WIDE : WIDE + STATS].astype(jnp.float32)
-            st = st[:, h * 8 : h * 8 + 5]
-            tops.append(st[:, 0:1] + st[:, 1:2] + st[:, 2:3])
-            totals.append(st[:, 3:4] + st[:, 4:5])
-        top = functools.reduce(jnp.maximum, tops)
-        shares = [n * jnp.exp2((m - top) * EXP2_SCALE) for m, n in zip(tops, totals)]
-        total = functools.reduce(jnp.add, shares)
-        acc = functools.reduce(
+        out = functools.reduce(
             jnp.add,
-            [parts_ref[j, :, cols].astype(jnp.float32) * shares[j] for j in range(COLUMNS)],
+            [
+                parts_ref[j, :, cols].astype(jnp.float32) * shares[j][:, h : h + 1]
+                for j in range(COLUMNS)
+            ],
         )
-        out = jnp.where(live, acc / total, 0.0)
         att_ref[:, cols] = out.astype(jnp.bfloat16)
     half = FRAME // tp_count
     mine = pl.ds(pl.multiple_of(tp * half, half), half)
@@ -189,7 +204,7 @@
         in_specs=[smem, smem, vmem, vmem],
         out_specs=[vmem, vmem],
         scratch_shapes=[pltpu.VMEM((FRAME, WIDE), jnp.bfloat16)],
-        compiler_params=pltpu.CompilerParams(vmem_limit_bytes=40 * 2**20),
+        compiler_params=pltpu.CompilerParams(vmem_limit_bytes=24 * 2**20),
         name="project",
     )(place, counts, parts, wo)
 
@@ -222,6 +237,7 @@
     q_all = lax.all_to_all(
         jnp.broadcast_to(queries[None], (COLUMNS, FRAME, WIDE)), ("xh", "y"), 0, 0, tiled=True
     )
+    second, q_all = lax.optimization_barrier((second, q_all))
     third = lax.ppermute(second, zc, split_ring(1))
     fourth = lax.ppermute(second[:1], zc, split_ring(2))
     near_o = lax.ppermute(near, "core", SWAP)

time: 86.5 us -> 78.7 us (0.910); the launches traced: 86.2 us -> 77.5 us
  Pallas kernels: 15.4 us -> 9.7 us
  local copies, waits for them, and re-layouts: 4.85 us -> 1.87 us
    pallas_call x2, Pallas kernels: 12.1 us -> 7.42 us  [attend_call(): pl.pallas_call(functools.partial(attend, offsets, state is not None, last...]
    unnamed x6, local copies, waits for them, and re-layouts: 3 us -> 0.02 us
    all_to_all x1, waiting for transfers between devices: 2.21 us -> 0.01 us  [on_device(): lax.all_to_all(jnp.broadcast_to(queries[None], (COLUMNS, FRAME, WIDE)), (...]
    ppermute x1, waiting for transfers between devices: 0.01 us -> 1.75 us  [on_device(): near = lax.ppermute(own2, zc, split_ring(1))]
    ppermute x1, waiting for transfers between devices: 1.43 us -> 0.01 us  [on_device(): own2 = jnp.stack([own, lax.ppermute(own, 'core', SWAP)])]
    pallas_call x1, Pallas kernels: 3.29 us -> 2.28 us  [project_call(): pl.pallas_call(functools.partial(project, 2), out_shape=[jax.ShapeDtypeSt...]
  transfers between devices with their start and end apart: 11 -> 11, of which waited for: 5 -> 5; matrix products, arithmetic and copies ran while one was open for 2% -> 3% of each run, Pallas kernels for 5% -> 6%
where the time goes in v2:
time: 78.7 us; the launch traced here: 77.5 us
  waiting for transfers between devices  22.3 us (28%)
  blocking collectives  22.1 us (28%)
  starting transfers between devices  19.7 us (25%)
  Pallas kernels  9.7 us (12%)
  local copies, waits for them, and re-layouts  1.87 us (2%)
  other arithmetic  1.81 us (2%)
    all_to_all x1, blocking collectives, on_device(): parts = lax.all_to_all(partial, ('xh', 'y'), 0, 0, tiled=True)  22.1 us
    ppermute x1, waiting for transfers between devices, on_device(): second = lax.ppermute(own2, zc, split_ring(2))  9.08 us
    pallas_call x2, Pallas kernels, attend_call(): pl.pallas_call(functools.partial(attend, offsets, state is not None, last...  7.42 us
    all_to_all x1, starting transfers between devices, on_device(): lax.all_to_all(jnp.broadcast_to(queries[None], (COLUMNS, FRAME, WIDE)), (...  7.06 us
    ppermute x1, waiting for transfers between devices, on_device(): fourth = lax.ppermute(second[:1], zc, split_ring(2))  5.68 us
    ppermute x1, waiting for transfers between devices, on_device(): got = lax.ppermute(send, 'tp', SWAP)  5.08 us
    ppermute x1, starting transfers between devices, on_device(): fourth = lax.ppermute(second[:1], zc, split_ring(2))  4.45 us
    ppermute x1, starting transfers between devices, on_device(): second = lax.ppermute(own2, zc, split_ring(2))  3.35 us
  transfers between devices with their start and end apart: 11, of which 5 were waited for; matrix products, arithmetic and copies ran while one was open for 3% of the time, Pallas kernels for 6%

profile of v2, /device:TPU:32, one launch (start us, length us, event | category | flops | bytes accessed | tf_op | source)
XLA Modules:
  0.0 77.5 jit_solution(14209366013668900951)
XLA Ops:
  0.0 1.0 %fusion = (bf16[1,2,64,768]{3,2,1,0:T(8,128)(2,1)S(1)}, bf16[2,64,768]{2,1,0:T(8,128)(2,1)S(1)}) fusion(bf16[1,64,768]{2,1,0:T(8,128)(2,1)} %bitcast.12, bf16[1,64,768]{2,1,0:T(8,128)(2,1)} %bitcast.13), kind=kLoop, calls=%fused_computation.4 | loop fusion | flops 98304 | bytes 589824 | tf_op jit(solution)/shard_map/stack | solution.py:233
  1.0 0.1 collective-permute-start
  1.1 1.8 %broadcast_in_dim.2 = bf16[8,64,768]{2,1,0:T(8,128)(2,1)} broadcast(bf16[64,768]{1,0:T(8,128)(2,1)} %param.5), dimensions={1,2} | broadcast | bytes 884736 | tf_op jit(solution)/shard_map/broadcast_in_dim | solution.py:238
  2.9 0.0 copy-start
  2.9 7.1 %all-to-all-start = ((bf16[8,64,768]{2,1,0:T(8,128)(2,1)}), bf16[8,64,768]{2,1,0:T(8,128)(2,1)S(1)}, u32[]{:S(2)}, u32[]{:S(2)}) async-start(bf16[8,64,768]{2,1,0:T(8,128)(2,1)} %broadcast_in_dim.2), calls=%async_computation | async-start | bytes 1572864 | tf_op jit(solution)/shard_map/all_to_all | solution.py:237
  10.0 0.0 collective-permute-done
  10.0 3.3 %collective-permute-start.1 = (bf16[2,2,64,768]{3,2,1,0:T(8,128)(2,1)S(1)}, bf16[2,2,64,768]{3,2,1,0:T(8,128)(2,1)S(1)}, u32[]{:S(2)}, u32[]{:S(2)}) collective-permute-start(bf16[2,2,64,768]{3,2,1,0:T(8,128)(2,1)S(1)} %pad_maximum_fusion.refs_3_), channel_id=1, source_target_pairs={{0,64},{2,194},{32,96},{34,226},{64,128},{66,2},{96,160},{98,34},{... | collective-permute-start | bytes 1179656 | tf_op jit(solution)/shard_map/ppermute | solution.py:236
  13.4 3.1 %collective-permute-start.6 = (bf16[2,2,64,768]{3,2,1,0:T(8,128)(2,1)S(1)}, bf16[2,2,64,768]{3,2,1,0:T(8,128)(2,1)S(1)}, u32[]{:S(2)}, u32[]{:S(2)}) collective-permute-start(bf16[2,2,64,768]{3,2,1,0:T(8,128)(2,1)S(1)} %pad_maximum_fusion.refs_3_), channel_id=1, source_target_pairs={{0,32},{2,226},{32,64},{34,2},{64,96},{66,34},{96,128},{98,66},{12... | collective-permute-start | bytes 1179656 | tf_op jit(solution)/shard_map/ppermute | solution.py:235
  16.5 9.1 %collective-permute-done.1.refs_6_ = bf16[2,2,64,768]{3,2,1,0:T(8,128)(2,1)S(1)} collective-permute-done((bf16[2,2,64,768]{3,2,1,0:T(8,128)(2,1)S(1)}, bf16[2,2,64,768]{3,2,1,0:T(8,128)(2,1)S(1)}, u32[]{:S(2)}, u32[]{:S(2)}) %collective-permute-start.1) | collective-permute-done | bytes 393248 | tf_op jit(solution)/shard_map/ppermute | solution.py:236
  25.6 0.0 all-to-all-done.refs_2_
  25.6 0.4 collective-permute-start.2
  26.0 1.7 %collective-permute-done.6.refs_4_ = bf16[2,2,64,768]{3,2,1,0:T(8,128)(2,1)S(1)} collective-permute-done((bf16[2,2,64,768]{3,2,1,0:T(8,128)(2,1)S(1)}, bf16[2,2,64,768]{3,2,1,0:T(8,128)(2,1)S(1)}, u32[]{:S(2)}, u32[]{:S(2)}) %collective-permute-start.6) | collective-permute-done | bytes 393248 | tf_op jit(solution)/shard_map/ppermute | solution.py:235
  27.7 0.0 collective-permute-start.7
  27.7 0.5 collective-permute-start.8
  28.2 4.5 %collective-permute-start.4 = (bf16[1,2,64,768]{3,2,1,0:T(8,128)(2,1)S(1)}, bf16[1,2,64,768]{3,2,1,0:T(8,128)(2,1)S(1)}, u32[]{:S(2)}, u32[]{:S(2)}) collective-permute-start(bf16[1,2,64,768]{3,2,1,0:T(8,128)(2,1)S(1)} %slice.3), channel_id=1, source_target_pairs={{0,64},{2,194},{32,96},{34,226},{64,128},{66,2},{96,160},{98,34},{... | collective-permute-start | bytes 589832 | tf_op jit(solution)/shard_map/ppermute | solution.py:242
  32.7 0.7 collective-permute-done.2.refs_3_
  33.4 0.0 collective-permute-start.3
  33.4 5.7 %collective-permute-done.4.refs_5_ = bf16[1,2,64,768]{3,2,1,0:T(8,128)(2,1)S(1)} collective-permute-done((bf16[1,2,64,768]{3,2,1,0:T(8,128)(2,1)S(1)}, bf16[1,2,64,768]{3,2,1,0:T(8,128)(2,1)S(1)}, u32[]{:S(2)}, u32[]{:S(2)}) %collective-permute-start.4) | collective-permute-done | bytes 196640 | tf_op jit(solution)/shard_map/ppermute | solution.py:242
  39.0 0.0 collective-permute-start.5
  39.0 0.1 pad_add_fusion.refs_0_.place_ref
  39.1 0.0 collective-permute-done.7.refs_5_
  39.1 0.0 collective-permute-done.8.refs_7_
  39.1 0.0 copy-done
  39.1 0.0 slice-start
  39.2 4.3 %attend_first.1 = (f32[512,768]{1,0:T(8,128)S(1)}, f32[6,512,128]{2,1,0:T(8,128)S(1)}, f32[6,512,128]{2,1,0:T(8,128)S(1)}) custom-call(s32[4]{0:T(128)S(1)} %pad_add_fusion.refs_0_.place_ref, s32[128]{0:T(128)S(1)} %copy-done, bf16[8,64,768]{2,1,0:T(8,128)(2,1)S(1)} %all-to-all-done.refs_2_, bf16[2,2,64,768]{3,2,1,0:T(8,128)(2,1)S(1)} %pad_maximum_fusion.refs_3_, ...), custom_call_target="tpu_custom_call" | custom-call | flops 1006632960 | bytes 4194304 | tf_op jit(solution)/shard_map/attend_first/pallas_call | solution.py:138
  43.4 0.0 collective-permute-done.5.refs_6_
  43.4 0.0 collective-permute-done.3.refs_4_
  43.5 0.0 slice-start.1
  43.5 3.1 %attend_last.1 = bf16[8,64,896]{2,1,0:T(8,128)(2,1)S(1)} custom-call(s32[4]{0:T(128)S(1)} %pad_add_fusion.refs_0_.place_ref, s32[128]{0:T(128)S(1)} %copy-done, bf16[8,64,768]{2,1,0:T(8,128)(2,1)S(1)} %all-to-all-done.refs_2_, bf16[2,2,64,768]{3,2,1,0:T(8,128)(2,1)S(1)} %collective-permute-done.2.refs_3_, ...), custom_call_target="tpu_custom_call" | custom-call | flops 603979776 | bytes 4194304 | tf_op jit(solution)/shard_map/attend_last/pallas_call | solution.py:138
  46.6 22.1 %all_to_all.10.parts_ref = bf16[8,64,896]{2,1,0:T(8,128)(2,1)S(1)} all-to-all(bf16[8,64,896]{2,1,0:T(8,128)(2,1)S(1)} %attend_last.1), channel_id=1, replica_groups=mesh['z'=8,'xh'=2,'y'=4,'core'=2,'tp'=2] {'xh','y'}, dimensions={0} | all-to-all | bytes 1835008 | tf_op jit(solution)/shard_map/all_to_all | solution.py:259
  68.8 0.0 slice-done
  68.8 0.0 slice-done.1
  68.8 2.3 %project.1 = (bf16[32,3072]{1,0:T(8,128)(2,1)S(1)}, f32[32,3072]{1,0:T(8,128)S(1)}) custom-call(s32[4]{0:T(128)S(1)} %pad_add_fusion.refs_0_.place_ref, s32[128]{0:T(128)S(1)} %copy-done, bf16[8,64,896]{2,1,0:T(8,128)(2,1)S(1)} %all_to_all.10.parts_ref, bf16[768,3072]{1,0:T(8,128)(2,1)S(1)} %bitcast.10), custom_call_target="tpu_custom_call" | custom-call | tf_op jit(solution)/shard_map/project/pallas_call | solution.py:198
  71.1 0.7 collective-permute-start.9
  71.7 5.1 %collective-permute-done.9 = bf16[32,3072]{1,0:T(8,128)(2,1)S(1)} collective-permute-done((bf16[32,3072]{1,0:T(8,128)(2,1)S(1)}, bf16[32,3072]{1,0:T(8,128)(2,1)S(1)}, u32[]{:S(2)}, u32[]{:S(2)}) %collective-permute-start.9) | collective-permute-done | bytes 196640 | tf_op jit(solution)/shard_map/ppermute | solution.py:261
  76.8 0.7 add_convert_fusion
  (3 shorter events, 0.1 us)
Async XLA Ops:
  1.0 9.0 %collective-permute-start = (bf16[2,64,768]{2,1,0:T(8,128)(2,1)S(1)}, bf16[2,64,768]{2,1,0:T(8,128)(2,1)S(1)}, u32[]{:S(2)}, u32[]{:S(2)}) collective-permute-start(bf16[2,64,768]{2,1,0:T(8,128)(2,1)S(1)} %get-tuple-element.20), channel_id=1, source_target_pairs={{0,2},{2,0},{1,3},{3,1},{4,6},{6,4},{5,7},{7,5},{8,10},{10,8},{9,1... | collective-permute-start | bytes 589832 | tf_op jit(solution)/shard_map/ppermute | solution.py:233
  2.9 36.2 %copy-start = (s32[128]{0:T(128)S(1)}, s32[128]{0:T(128)}, u32[]{:S(2)}) copy-start(s32[128]{0:T(128)} %counts_ref.1) | copy-start | bytes 1540
  2.9 22.7 %all-to-all-start = ((bf16[8,64,768]{2,1,0:T(8,128)(2,1)}), bf16[8,64,768]{2,1,0:T(8,128)(2,1)S(1)}, u32[]{:S(2)}, u32[]{:S(2)}) async-start(bf16[8,64,768]{2,1,0:T(8,128)(2,1)} %broadcast_in_dim.2), calls=%async_computation | async-start | bytes 1572864 | tf_op jit(solution)/shard_map/all_to_all | solution.py:237
  10.0 15.6 %collective-permute-start.1 = (bf16[2,2,64,768]{3,2,1,0:T(8,128)(2,1)S(1)}, bf16[2,2,64,768]{3,2,1,0:T(8,128)(2,1)S(1)}, u32[]{:S(2)}, u32[]{:S(2)}) collective-permute-start(bf16[2,2,64,768]{3,2,1,0:T(8,128)(2,1)S(1)} %pad_maximum_fusion.refs_3_), channel_id=1, source_target_pairs={{0,64},{2,194},{32,96},{34,226},{64,128},{66,2},{96,160},{98,34},{... | collective-permute-start | bytes 1179656 | tf_op jit(solution)/shard_map/ppermute | solution.py:236
  13.4 14.3 %collective-permute-start.6 = (bf16[2,2,64,768]{3,2,1,0:T(8,128)(2,1)S(1)}, bf16[2,2,64,768]{3,2,1,0:T(8,128)(2,1)S(1)}, u32[]{:S(2)}, u32[]{:S(2)}) collective-permute-start(bf16[2,2,64,768]{3,2,1,0:T(8,128)(2,1)S(1)} %pad_maximum_fusion.refs_3_), channel_id=1, source_target_pairs={{0,32},{2,226},{32,64},{34,2},{64,96},{66,34},{96,128},{98,66},{12... | collective-permute-start | bytes 1179656 | tf_op jit(solution)/shard_map/ppermute | solution.py:235
  25.6 7.8 %collective-permute-start.2 = (bf16[2,2,64,768]{3,2,1,0:T(8,128)(2,1)S(1)}, bf16[2,2,64,768]{3,2,1,0:T(8,128)(2,1)S(1)}, u32[]{:S(2)}, u32[]{:S(2)}) collective-permute-start(bf16[2,2,64,768]{3,2,1,0:T(8,128)(2,1)S(1)} %collective-permute-done.1.refs_6_), channel_id=1, source_target_pairs={{0,32},{2,226},{32,64},{34,2},{64,96},{66,34},{96,128},{98,66},{12... | collective-permute-start | bytes 1179656 | tf_op jit(solution)/shard_map/ppermute | solution.py:241
  27.7 11.4 %collective-permute-start.7 = (bf16[2,2,64,768]{3,2,1,0:T(8,128)(2,1)S(1)}, bf16[2,2,64,768]{3,2,1,0:T(8,128)(2,1)S(1)}, u32[]{:S(2)}, u32[]{:S(2)}) collective-permute-start(bf16[2,2,64,768]{3,2,1,0:T(8,128)(2,1)S(1)} %collective-permute-done.6.refs_4_), channel_id=1, source_target_pairs={{0,2},{2,0},{1,3},{3,1},{4,6},{6,4},{5,7},{7,5},{8,10},{10,8},{9,1... | collective-permute-start | bytes 1179656 | tf_op jit(solution)/shard_map/ppermute | solution.py:243
  27.7 11.4 %collective-permute-start.8 = (bf16[2,2,64,768]{3,2,1,0:T(8,128)(2,1)S(1)}, bf16[2,2,64,768]{3,2,1,0:T(8,128)(2,1)}, u32[]{:S(2)}, u32[]{:S(2)}) collective-permute-start(bf16[2,2,64,768]{3,2,1,0:T(8,128)(2,1)S(1)} %collective-permute-done.1.refs_6_), channel_id=1, source_target_pairs={{0,2},{2,0},{1,3},{3,1},{4,6},{6,4},{5,7},{7,5},{8,10},{10,8},{9,1... | collective-permute-start | bytes 1179656 | tf_op jit(solution)/shard_map/ppermute | solution.py:244
  28.2 10.8 %collective-permute-start.4 = (bf16[1,2,64,768]{3,2,1,0:T(8,128)(2,1)S(1)}, bf16[1,2,64,768]{3,2,1,0:T(8,128)(2,1)S(1)}, u32[]{:S(2)}, u32[]{:S(2)}) collective-permute-start(bf16[1,2,64,768]{3,2,1,0:T(8,128)(2,1)S(1)} %slice.3), channel_id=1, source_target_pairs={{0,64},{2,194},{32,96},{34,226},{64,128},{66,2},{96,160},{98,34},{... | collective-permute-start | bytes 589832 | tf_op jit(solution)/shard_map/ppermute | solution.py:242
  33.4 10.1 %collective-permute-start.3 = (bf16[2,2,64,768]{3,2,1,0:T(8,128)(2,1)S(1)}, bf16[2,2,64,768]{3,2,1,0:T(8,128)(2,1)S(1)}, u32[]{:S(2)}, u32[]{:S(2)}) collective-permute-start(bf16[2,2,64,768]{3,2,1,0:T(8,128)(2,1)S(1)} %collective-permute-done.2.refs_3_), channel_id=1, source_target_pairs={{0,2},{2,0},{1,3},{3,1},{4,6},{6,4},{5,7},{7,5},{8,10},{10,8},{9,1... | collective-permute-start | bytes 1179656 | tf_op jit(solution)/shard_map/ppermute | solution.py:245
  39.0 4.4 %collective-permute-start.5 = (bf16[1,2,64,768]{3,2,1,0:T(8,128)(2,1)S(1)}, bf16[1,2,64,768]{3,2,1,0:T(8,128)(2,1)S(1)}, u32[]{:S(2)}, u32[]{:S(2)}) collective-permute-start(bf16[1,2,64,768]{3,2,1,0:T(8,128)(2,1)S(1)} %collective-permute-done.4.refs_5_), channel_id=1, source_target_pairs={{0,2},{2,0},{1,3},{3,1},{4,6},{6,4},{5,7},{7,5},{8,10},{10,8},{9,1... | collective-permute-start | bytes 589832 | tf_op jit(solution)/shard_map/ppermute | solution.py:246
  39.1 29.6 %slice-start = ((s8[4718592]{0:T(1024)(128)(4,1)}), s8[4194304]{0:T(1024)(128)(4,1)S(1)}, s32[]{:S(2)}) async-start(s8[4718592]{0:T(1024)(128)(4,1)} %bitcast.9), calls=%async_computation.2 | async-start | bytes 8388608
  43.5 25.3 %slice-start.1 = ((s8[4718592]{0:T(1024)(128)(4,1)}), s8[524288]{0:T(1024)(128)(4,1)S(1)}, s32[]{:S(2)}) async-start(s8[4718592]{0:T(1024)(128)(4,1)} %bitcast.9), calls=%async_computation.3 | async-start | bytes 1048576
  71.1 5.8 %collective-permute-start.9 = (bf16[32,3072]{1,0:T(8,128)(2,1)S(1)}, bf16[32,3072]{1,0:T(8,128)(2,1)S(1)}, u32[]{:S(2)}, u32[]{:S(2)}) collective-permute-start(bf16[32,3072]{1,0:T(8,128)(2,1)S(1)} %get-tuple-element.18), channel_id=1, source_target_pairs={{0,1},{1,0},{2,3},{3,2},{4,5},{5,4},{6,7},{7,6},{8,9},{9,8},{10,11... | collective-permute-start | bytes 589832 | tf_op jit(solution)/shard_map/ppermute | solution.py:261

commit v3 on v2

--- a/solution.py
+++ b/solution.py
@@ -232,18 +232,17 @@
     own = jnp.stack([keys, values])
     own2 = jnp.stack([own, lax.ppermute(own, "core", SWAP)])
     zc = ("z", "core")
+    queries, own2 = lax.optimization_barrier((queries, own2))
+    second = lax.ppermute(own2, zc, split_ring(2))
     near = lax.ppermute(own2, zc, split_ring(1))
-    second = lax.ppermute(own2, zc, split_ring(2))
     q_all = lax.all_to_all(
         jnp.broadcast_to(queries[None], (COLUMNS, FRAME, WIDE)), ("xh", "y"), 0, 0, tiled=True
     )
-    second, q_all = lax.optimization_barrier((second, q_all))
+    fourth = lax.ppermute(second[:1], zc, split_ring(2))
     third = lax.ppermute(second, zc, split_ring(1))
-    fourth = lax.ppermute(second[:1], zc, split_ring(2))
+    near, second = lax.optimization_barrier((near, second))
     near_o = lax.ppermute(near, "core", SWAP)
     second_o = lax.ppermute(second, "core", SWAP)
-    third_o = lax.ppermute(third, "core", SWAP)
-    fourth_o = lax.ppermute(fourth, "core", SWAP)
     first = [own2, near, near_o, second, second_o]
     first_off = [
         ("both", 0, False),
@@ -252,9 +251,12 @@
         ("both", 2, False),
         ("both", 2, True),
     ]
+    state = attend_call(place, frame_tokens, q_all, first, first_off, None, False)
+    third, fourth, state = lax.optimization_barrier((third, fourth, state))
+    third_o = lax.ppermute(third, "core", SWAP)
+    fourth_o = lax.ppermute(fourth, "core", SWAP)
     rest = [third, third_o, fourth, fourth_o]
     rest_off = [("both", 3, False), ("both", 3, True), ("half", 4, False), ("half", 4, True)]
-    state = attend_call(place, frame_tokens, q_all, first, first_off, None, False)
     partial = attend_call(place, frame_tokens, q_all, rest, rest_off, state, True)
     parts = lax.all_to_all(partial, ("xh", "y"), 0, 0, tiled=True)
     send, keep = project_call(place, frame_tokens, parts, wo)

time: 78.7 us -> 73 us (0.928); the launches traced: 77.5 us -> 72.8 us
  waiting for transfers between devices: 22.3 us -> 15.1 us
  starting transfers between devices: 19.7 us -> 21.9 us
    ppermute x1, waiting for transfers between devices: 9.08 us -> 0.31 us  [on_device(): second = lax.ppermute(own2, zc, split_ring(2))]
    ppermute x1, waiting for transfers between devices: 5.68 us -> 1.27 us  [on_device(): fourth = lax.ppermute(second[:1], zc, split_ring(2))]
    all_to_all x1, waiting for transfers between devices: 0.01 us -> 3.35 us  [on_device(): lax.all_to_all(jnp.broadcast_to(queries[None], (COLUMNS, FRAME, WIDE)), (...]
    ppermute x1, starting transfers between devices: 0.38 us -> 2.46 us  [on_device(): third = lax.ppermute(second, zc, split_ring(1))]
    ppermute x1, waiting for transfers between devices: 0.01 us -> 1.49 us  [on_device(): fourth_o = lax.ppermute(fourth, 'core', SWAP)]
    ppermute x1, waiting for transfers between devices: 0.01 us -> 1.43 us  [on_device(): own2 = jnp.stack([own, lax.ppermute(own, 'core', SWAP)])]
  transfers between devices with their start and end apart: 11 -> 11, of which waited for: 5 -> 7; matrix products, arithmetic and copies ran while one was open for 3% -> 3% of each run, Pallas kernels for 6% -> 5%
where the time goes in v3:
time: 73 us; the launch traced here: 72.8 us
  blocking collectives  22.8 us (31%)
  starting transfers between devices  21.9 us (30%)
  waiting for transfers between devices  15.1 us (21%)
  Pallas kernels  9.17 us (13%)
  local copies, waits for them, and re-layouts  1.86 us (3%)
  other arithmetic  1.81 us (2%)
    all_to_all x1, blocking collectives, on_device(): parts = lax.all_to_all(partial, ('xh', 'y'), 0, 0, tiled=True)  22.8 us
    all_to_all x1, starting transfers between devices, on_device(): lax.all_to_all(jnp.broadcast_to(queries[None], (COLUMNS, FRAME, WIDE)), (...  6.93 us
    pallas_call x2, Pallas kernels, attend_call(): pl.pallas_call(functools.partial(attend, offsets, state is not None, last...  6.89 us
    ppermute x1, waiting for transfers between devices, on_device(): got = lax.ppermute(send, 'tp', SWAP)  5.09 us
    ppermute x1, starting transfers between devices, on_device(): fourth = lax.ppermute(second[:1], zc, split_ring(2))  4.27 us
    all_to_all x1, waiting for transfers between devices, on_device(): lax.all_to_all(jnp.broadcast_to(queries[None], (COLUMNS, FRAME, WIDE)), (...  3.35 us
    ppermute x1, starting transfers between devices, on_device(): second = lax.ppermute(own2, zc, split_ring(2))  3.35 us
    ppermute x1, starting transfers between devices, on_device(): near = lax.ppermute(own2, zc, split_ring(1))  3.13 us
  transfers between devices with their start and end apart: 11, of which 7 were waited for; matrix products, arithmetic and copies ran while one was open for 3% of the time, Pallas kernels for 5%

profile of v3, /device:TPU:32, one launch (start us, length us, event | category | flops | bytes accessed | tf_op | source)
XLA Modules:
  0.0 72.8 jit_solution(15505212103376529527)
XLA Ops:
  0.0 1.0 %fusion = (bf16[1,2,64,768]{3,2,1,0:T(8,128)(2,1)S(1)}, bf16[2,64,768]{2,1,0:T(8,128)(2,1)S(1)}) fusion(bf16[1,64,768]{2,1,0:T(8,128)(2,1)} %bitcast.12, bf16[1,64,768]{2,1,0:T(8,128)(2,1)} %bitcast.13), kind=kLoop, calls=%fused_computation.4 | loop fusion | flops 98304 | bytes 589824 | tf_op jit(solution)/shard_map/stack | solution.py:233
  1.0 0.1 collective-permute-start
  1.1 1.4 %collective-permute-done = bf16[2,64,768]{2,1,0:T(8,128)(2,1)S(1)} collective-permute-done((bf16[2,64,768]{2,1,0:T(8,128)(2,1)S(1)}, bf16[2,64,768]{2,1,0:T(8,128)(2,1)S(1)}, u32[]{:S(2)}, u32[]{:S(2)}) %collective-permute-start) | collective-permute-done | bytes 196640 | tf_op jit(solution)/shard_map/ppermute | solution.py:233
  2.5 0.0 copy-start
  2.6 3.3 %collective-permute-start.1 = (bf16[2,2,64,768]{3,2,1,0:T(8,128)(2,1)S(1)}, bf16[2,2,64,768]{3,2,1,0:T(8,128)(2,1)S(1)}, u32[]{:S(2)}, u32[]{:S(2)}) collective-permute-start(bf16[2,2,64,768]{3,2,1,0:T(8,128)(2,1)S(1)} %pad_maximum_fusion.refs_3_), channel_id=1, source_target_pairs={{0,64},{2,194},{32,96},{34,226},{64,128},{66,2},{96,160},{98,34},{... | collective-permute-start | bytes 1179656 | tf_op jit(solution)/shard_map/ppermute | solution.py:236
  5.9 3.1 %collective-permute-start.4 = (bf16[2,2,64,768]{3,2,1,0:T(8,128)(2,1)S(1)}, bf16[2,2,64,768]{3,2,1,0:T(8,128)(2,1)S(1)}, u32[]{:S(2)}, u32[]{:S(2)}) collective-permute-start(bf16[2,2,64,768]{3,2,1,0:T(8,128)(2,1)S(1)} %pad_maximum_fusion.refs_3_), channel_id=1, source_target_pairs={{0,32},{2,226},{32,64},{34,2},{64,96},{66,34},{96,128},{98,66},{12... | collective-permute-start | bytes 1179656 | tf_op jit(solution)/shard_map/ppermute | solution.py:237
  9.0 1.8 %broadcast_in_dim.2 = bf16[8,64,768]{2,1,0:T(8,128)(2,1)} broadcast(bf16[64,768]{1,0:T(8,128)(2,1)} %param.5), dimensions={1,2} | broadcast | bytes 884736 | tf_op jit(solution)/shard_map/broadcast_in_dim | solution.py:239
  10.9 6.9 %all-to-all-start = ((bf16[8,64,768]{2,1,0:T(8,128)(2,1)}), bf16[8,64,768]{2,1,0:T(8,128)(2,1)S(1)}, u32[]{:S(2)}, u32[]{:S(2)}) async-start(bf16[8,64,768]{2,1,0:T(8,128)(2,1)} %broadcast_in_dim.2), calls=%async_computation | async-start | bytes 1572864 | tf_op jit(solution)/shard_map/all_to_all | solution.py:238
  17.8 0.3 collective-permute-done.1.refs_6_
  18.1 2.1 %collective-permute-done.4.refs_4_ = bf16[2,2,64,768]{3,2,1,0:T(8,128)(2,1)S(1)} collective-permute-done((bf16[2,2,64,768]{3,2,1,0:T(8,128)(2,1)S(1)}, bf16[2,2,64,768]{3,2,1,0:T(8,128)(2,1)S(1)}, u32[]{:S(2)}, u32[]{:S(2)}) %collective-permute-start.4) | collective-permute-done | bytes 393248 | tf_op jit(solution)/shard_map/ppermute | solution.py:237
  20.2 0.5 collective-permute-start.5
  20.7 0.0 collective-permute-start.6
  20.8 2.5 %collective-permute-start.2 = (bf16[2,2,64,768]{3,2,1,0:T(8,128)(2,1)S(1)}, bf16[2,2,64,768]{3,2,1,0:T(8,128)(2,1)S(1)}, u32[]{:S(2)}, u32[]{:S(2)}) collective-permute-start(bf16[2,2,64,768]{3,2,1,0:T(8,128)(2,1)S(1)} %collective-permute-done.1.refs_6_), channel_id=1, source_target_pairs={{0,32},{2,226},{32,64},{34,2},{64,96},{66,34},{96,128},{98,66},{12... | collective-permute-start | bytes 1179656 | tf_op jit(solution)/shard_map/ppermute | solution.py:242
  23.2 4.3 %collective-permute-start.3 = (bf16[1,2,64,768]{3,2,1,0:T(8,128)(2,1)S(1)}, bf16[1,2,64,768]{3,2,1,0:T(8,128)(2,1)S(1)}, u32[]{:S(2)}, u32[]{:S(2)}) collective-permute-start(bf16[1,2,64,768]{3,2,1,0:T(8,128)(2,1)S(1)} %slice.4), channel_id=1, source_target_pairs={{0,64},{2,194},{32,96},{34,226},{64,128},{66,2},{96,160},{98,34},{... | collective-permute-start | bytes 589832 | tf_op jit(solution)/shard_map/ppermute | solution.py:241
  27.5 0.1 pad_add_fusion.refs_0_.place_ref
  27.6 3.4 %all-to-all-done.refs_2_ = bf16[8,64,768]{2,1,0:T(8,128)(2,1)S(1)} async-done(((bf16[8,64,768]{2,1,0:T(8,128)(2,1)}), bf16[8,64,768]{2,1,0:T(8,128)(2,1)S(1)}, u32[]{:S(2)}, u32[]{:S(2)}) %all-to-all-start) | async-done | bytes 786464 | tf_op jit(solution)/shard_map/all_to_all | solution.py:238
  30.9 0.0 collective-permute-done.5.refs_5_
  30.9 0.0 collective-permute-done.6.refs_7_
  30.9 0.0 copy-done
  30.9 0.0 slice-start
  31.0 3.7 %attend_first.1 = (f32[512,768]{1,0:T(8,128)S(1)}, f32[6,512,128]{2,1,0:T(8,128)S(1)}, f32[6,512,128]{2,1,0:T(8,128)S(1)}) custom-call(s32[4]{0:T(128)S(1)} %pad_add_fusion.refs_0_.place_ref, s32[128]{0:T(128)S(1)} %copy-done, bf16[8,64,768]{2,1,0:T(8,128)(2,1)S(1)} %all-to-all-done.refs_2_, bf16[2,2,64,768]{3,2,1,0:T(8,128)(2,1)S(1)} %pad_maximum_fusion.refs_3_, ...), custom_call_target="tpu_custom_call" | custom-call | flops 1006632960 | bytes 4194304 | tf_op jit(solution)/shard_map/attend_first/pallas_call | solution.py:138
  34.7 1.3 %collective-permute-done.3.refs_5_ = bf16[1,2,64,768]{3,2,1,0:T(8,128)(2,1)S(1)} collective-permute-done((bf16[1,2,64,768]{3,2,1,0:T(8,128)(2,1)S(1)}, bf16[1,2,64,768]{3,2,1,0:T(8,128)(2,1)S(1)}, u32[]{:S(2)}, u32[]{:S(2)}) %collective-permute-start.3) | collective-permute-done | bytes 196640 | tf_op jit(solution)/shard_map/ppermute | solution.py:241
  36.0 0.0 collective-permute-done.2.refs_3_
  36.0 0.0 slice-start.1
  36.0 0.0 collective-permute-start.7
  36.0 0.5 collective-permute-start.8
  36.5 1.5 %collective-permute-done.8.refs_6_ = bf16[1,2,64,768]{3,2,1,0:T(8,128)(2,1)S(1)} collective-permute-done((bf16[1,2,64,768]{3,2,1,0:T(8,128)(2,1)S(1)}, bf16[1,2,64,768]{3,2,1,0:T(8,128)(2,1)S(1)}, u32[]{:S(2)}, u32[]{:S(2)}) %collective-permute-start.8) | collective-permute-done | bytes 196640 | tf_op jit(solution)/shard_map/ppermute | solution.py:257
  38.0 0.0 collective-permute-done.7.refs_4_
  38.0 3.2 %attend_last.1 = bf16[8,64,896]{2,1,0:T(8,128)(2,1)S(1)} custom-call(s32[4]{0:T(128)S(1)} %pad_add_fusion.refs_0_.place_ref, s32[128]{0:T(128)S(1)} %copy-done, bf16[8,64,768]{2,1,0:T(8,128)(2,1)S(1)} %all-to-all-done.refs_2_, bf16[2,2,64,768]{3,2,1,0:T(8,128)(2,1)S(1)} %collective-permute-done.2.refs_3_, ...), custom_call_target="tpu_custom_call" | custom-call | flops 603979776 | bytes 4194304 | tf_op jit(solution)/shard_map/attend_last/pallas_call | solution.py:138
  41.1 22.8 %all_to_all.10.parts_ref = bf16[8,64,896]{2,1,0:T(8,128)(2,1)S(1)} all-to-all(bf16[8,64,896]{2,1,0:T(8,128)(2,1)S(1)} %attend_last.1), channel_id=1, replica_groups=mesh['z'=8,'xh'=2,'y'=4,'core'=2,'tp'=2] {'xh','y'}, dimensions={0} | all-to-all | bytes 1835008 | tf_op jit(solution)/shard_map/all_to_all | solution.py:261
  64.0 0.0 slice-done
  64.0 0.0 slice-done.1
  64.0 2.3 %project.1 = (bf16[32,3072]{1,0:T(8,128)(2,1)S(1)}, f32[32,3072]{1,0:T(8,128)S(1)}) custom-call(s32[4]{0:T(128)S(1)} %pad_add_fusion.refs_0_.place_ref, s32[128]{0:T(128)S(1)} %copy-done, bf16[8,64,896]{2,1,0:T(8,128)(2,1)S(1)} %all_to_all.10.parts_ref, bf16[768,3072]{1,0:T(8,128)(2,1)S(1)} %bitcast.10), custom_call_target="tpu_custom_call" | custom-call | tf_op jit(solution)/shard_map/project/pallas_call | solution.py:198
  66.3 0.7 collective-permute-start.9
  66.9 5.1 %collective-permute-done.9 = bf16[32,3072]{1,0:T(8,128)(2,1)S(1)} collective-permute-done((bf16[32,3072]{1,0:T(8,128)(2,1)S(1)}, bf16[32,3072]{1,0:T(8,128)(2,1)S(1)}, u32[]{:S(2)}, u32[]{:S(2)}) %collective-permute-start.9) | collective-permute-done | bytes 196640 | tf_op jit(solution)/shard_map/ppermute | solution.py:263
  72.0 0.7 add_convert_fusion
  (3 shorter events, 0.1 us)
Async XLA Ops:
  1.0 1.5 %collective-permute-start = (bf16[2,64,768]{2,1,0:T(8,128)(2,1)S(1)}, bf16[2,64,768]{2,1,0:T(8,128)(2,1)S(1)}, u32[]{:S(2)}, u32[]{:S(2)}) collective-permute-start(bf16[2,64,768]{2,1,0:T(8,128)(2,1)S(1)} %get-tuple-element.34), channel_id=1, source_target_pairs={{0,2},{2,0},{1,3},{3,1},{4,6},{6,4},{5,7},{7,5},{8,10},{10,8},{9,1... | collective-permute-start | bytes 589832 | tf_op jit(solution)/shard_map/ppermute | solution.py:233
  2.5 28.4 %copy-start = (s32[128]{0:T(128)S(1)}, s32[128]{0:T(128)}, u32[]{:S(2)}) copy-start(s32[128]{0:T(128)} %counts_ref.1) | copy-start | bytes 1540
  2.6 15.6 %collective-permute-start.1 = (bf16[2,2,64,768]{3,2,1,0:T(8,128)(2,1)S(1)}, bf16[2,2,64,768]{3,2,1,0:T(8,128)(2,1)S(1)}, u32[]{:S(2)}, u32[]{:S(2)}) collective-permute-start(bf16[2,2,64,768]{3,2,1,0:T(8,128)(2,1)S(1)} %pad_maximum_fusion.refs_3_), channel_id=1, source_target_pairs={{0,64},{2,194},{32,96},{34,226},{64,128},{66,2},{96,160},{98,34},{... | collective-permute-start | bytes 1179656 | tf_op jit(solution)/shard_map/ppermute | solution.py:236
  5.9 14.3 %collective-permute-start.4 = (bf16[2,2,64,768]{3,2,1,0:T(8,128)(2,1)S(1)}, bf16[2,2,64,768]{3,2,1,0:T(8,128)(2,1)S(1)}, u32[]{:S(2)}, u32[]{:S(2)}) collective-permute-start(bf16[2,2,64,768]{3,2,1,0:T(8,128)(2,1)S(1)} %pad_maximum_fusion.refs_3_), channel_id=1, source_target_pairs={{0,32},{2,226},{32,64},{34,2},{64,96},{66,34},{96,128},{98,66},{12... | collective-permute-start | bytes 1179656 | tf_op jit(solution)/shard_map/ppermute | solution.py:237
  10.9 20.1 %all-to-all-start = ((bf16[8,64,768]{2,1,0:T(8,128)(2,1)}), bf16[8,64,768]{2,1,0:T(8,128)(2,1)S(1)}, u32[]{:S(2)}, u32[]{:S(2)}) async-start(bf16[8,64,768]{2,1,0:T(8,128)(2,1)} %broadcast_in_dim.2), calls=%async_computation | async-start | bytes 1572864 | tf_op jit(solution)/shard_map/all_to_all | solution.py:238
  20.2 10.7 %collective-permute-start.5 = (bf16[2,2,64,768]{3,2,1,0:T(8,128)(2,1)S(1)}, bf16[2,2,64,768]{3,2,1,0:T(8,128)(2,1)S(1)}, u32[]{:S(2)}, u32[]{:S(2)}) collective-permute-start(bf16[2,2,64,768]{3,2,1,0:T(8,128)(2,1)S(1)} %collective-permute-done.4.refs_4_), channel_id=1, source_target_pairs={{0,2},{2,0},{1,3},{3,1},{4,6},{6,4},{5,7},{7,5},{8,10},{10,8},{9,1... | collective-permute-start | bytes 1179656 | tf_op jit(solution)/shard_map/ppermute | solution.py:244
  20.7 10.2 %collective-permute-start.6 = (bf16[2,2,64,768]{3,2,1,0:T(8,128)(2,1)S(1)}, bf16[2,2,64,768]{3,2,1,0:T(8,128)(2,1)S(1)}, u32[]{:S(2)}, u32[]{:S(2)}) collective-permute-start(bf16[2,2,64,768]{3,2,1,0:T(8,128)(2,1)S(1)} %collective-permute-done.1.refs_6_), channel_id=1, source_target_pairs={{0,2},{2,0},{1,3},{3,1},{4,6},{6,4},{5,7},{7,5},{8,10},{10,8},{9,1... | collective-permute-start | bytes 1179656 | tf_op jit(solution)/shard_map/ppermute | solution.py:245
  20.8 15.2 %collective-permute-start.2 = (bf16[2,2,64,768]{3,2,1,0:T(8,128)(2,1)S(1)}, bf16[2,2,64,768]{3,2,1,0:T(8,128)(2,1)S(1)}, u32[]{:S(2)}, u32[]{:S(2)}) collective-permute-start(bf16[2,2,64,768]{3,2,1,0:T(8,128)(2,1)S(1)} %collective-permute-done.1.refs_6_), channel_id=1, source_target_pairs={{0,32},{2,226},{32,64},{34,2},{64,96},{66,34},{96,128},{98,66},{12... | collective-permute-start | bytes 1179656 | tf_op jit(solution)/shard_map/ppermute | solution.py:242
  23.2 12.7 %collective-permute-start.3 = (bf16[1,2,64,768]{3,2,1,0:T(8,128)(2,1)S(1)}, bf16[1,2,64,768]{3,2,1,0:T(8,128)(2,1)S(1)}, u32[]{:S(2)}, u32[]{:S(2)}) collective-permute-start(bf16[1,2,64,768]{3,2,1,0:T(8,128)(2,1)S(1)} %slice.4), channel_id=1, source_target_pairs={{0,64},{2,194},{32,96},{34,226},{64,128},{66,2},{96,160},{98,34},{... | collective-permute-start | bytes 589832 | tf_op jit(solution)/shard_map/ppermute | solution.py:241
  30.9 33.0 %slice-start = ((s8[4718592]{0:T(1024)(128)(4,1)}), s8[4194304]{0:T(1024)(128)(4,1)S(1)}, s32[]{:S(2)}) async-start(s8[4718592]{0:T(1024)(128)(4,1)} %bitcast.9), calls=%async_computation.2 | async-start | bytes 8388608
  36.0 28.0 %slice-start.1 = ((s8[4718592]{0:T(1024)(128)(4,1)}), s8[524288]{0:T(1024)(128)(4,1)S(1)}, s32[]{:S(2)}) async-start(s8[4718592]{0:T(1024)(128)(4,1)} %bitcast.9), calls=%async_computation.3 | async-start | bytes 1048576
  36.0 2.0 %collective-permute-start.7 = (bf16[2,2,64,768]{3,2,1,0:T(8,128)(2,1)S(1)}, bf16[2,2,64,768]{3,2,1,0:T(8,128)(2,1)S(1)}, u32[]{:S(2)}, u32[]{:S(2)}) collective-permute-start(bf16[2,2,64,768]{3,2,1,0:T(8,128)(2,1)S(1)} %collective-permute-done.2.refs_3_), channel_id=1, source_target_pairs={{0,2},{2,0},{1,3},{3,1},{4,6},{6,4},{5,7},{7,5},{8,10},{10,8},{9,1... | collective-permute-start | bytes 1179656 | tf_op jit(solution)/shard_map/ppermute | solution.py:256
  36.0 2.0 %collective-permute-start.8 = (bf16[1,2,64,768]{3,2,1,0:T(8,128)(2,1)S(1)}, bf16[1,2,64,768]{3,2,1,0:T(8,128)(2,1)S(1)}, u32[]{:S(2)}, u32[]{:S(2)}) collective-permute-start(bf16[1,2,64,768]{3,2,1,0:T(8,128)(2,1)S(1)} %collective-permute-done.3.refs_5_), channel_id=1, source_target_pairs={{0,2},{2,0},{1,3},{3,1},{4,6},{6,4},{5,7},{7,5},{8,10},{10,8},{9,1... | collective-permute-start | bytes 589832 | tf_op jit(solution)/shard_map/ppermute | solution.py:257
  66.3 5.8 %collective-permute-start.9 = (bf16[32,3072]{1,0:T(8,128)(2,1)S(1)}, bf16[32,3072]{1,0:T(8,128)(2,1)S(1)}, u32[]{:S(2)}, u32[]{:S(2)}) collective-permute-start(bf16[32,3072]{1,0:T(8,128)(2,1)S(1)} %get-tuple-element.32), channel_id=1, source_target_pairs={{0,1},{1,0},{2,3},{3,2},{4,5},{5,4},{6,7},{7,6},{8,9},{9,8},{10,11... | collective-permute-start | bytes 589832 | tf_op jit(solution)/shard_map/ppermute | solution.py:263

commit v4 on v3

--- a/solution.py
+++ b/solution.py
@@ -14,7 +14,8 @@
 COLUMNS = 8
 HEADS = 6
 WIDE = HEADS * HEAD_DIM
-STATS = 128
+STATS = 16
+SENT_ROWS = HEADS * FRAME + STATS
 TOP_PARTS, TOTAL_PARTS = 3, 2
 Q_TILE = 256
 CTX = ("z", "xh", "y", "core")
@@ -105,25 +106,29 @@
                 tops = jnp.where(lanes == h, top, tops)
                 totals = jnp.where(lanes == h, total, totals)
                 mean = (acc * (1.0 / jnp.maximum(total, 1e-30))).astype(jnp.bfloat16)
-                outs[0][frames_at, :, cols] = mean.reshape(Q_TILE // FRAME, FRAME, HEAD_DIM)
+                head_rows = slice(h * FRAME, (h + 1) * FRAME)
+                outs[0][frames_at, head_rows, :] = mean.reshape(Q_TILE // FRAME, FRAME, HEAD_DIM)
         if last:
             packed, slot = jnp.zeros((Q_TILE, 128), jnp.float32), 0
             for value, count in ((tops, TOP_PARTS), (totals, TOTAL_PARTS)):
                 for _ in range(count):
                     part = value.astype(jnp.bfloat16).astype(jnp.float32)
                     value = value - part
-                    packed = packed + (pltpu.roll(part, slot * 8, 1) if slot else part)
+                    packed = packed + (pltpu.roll(part, slot * HEADS, 1) if slot else part)
                     slot += 1
-            outs[0][frames_at, :, WIDE:] = packed.astype(jnp.bfloat16).reshape(
-                Q_TILE // FRAME, FRAME, STATS
-            )
+            packed = packed.reshape(Q_TILE // FRAME, FRAME, 128)
+            for i in range(Q_TILE // FRAME):
+                folded = packed[i, :STATS]
+                for k in range(1, FRAME // STATS):
+                    folded = folded + pltpu.roll(packed[i, k * STATS : (k + 1) * STATS], 32 * k, 1)
+                outs[0][t * (Q_TILE // FRAME) + i, HEADS * FRAME :, :] = folded.astype(jnp.bfloat16)
 
 
 def attend_call(place, counts, q_all, kv, offsets, state, last):
     rows = COLUMNS * FRAME
     keys_n = sum(1 if kind == "half" else 2 for kind, _, _ in offsets) * FRAME
     if last:
-        out_shape = jax.ShapeDtypeStruct((COLUMNS, FRAME, WIDE + STATS), jnp.bfloat16)
+        out_shape = jax.ShapeDtypeStruct((COLUMNS, SENT_ROWS, HEAD_DIM), jnp.bfloat16)
         out_specs = pl.BlockSpec(memory_space=pltpu.VMEM)
     else:
         out_shape = [
@@ -152,60 +157,64 @@
     )(place, counts, q_all, *kv, *(state if state is not None else ()))
 
 
-def project(tp_count, place_ref, counts_ref, parts_ref, wo_ref, send_ref, keep_ref, att_ref):
+def project(own, place_ref, counts_ref, parts_ref, wo_ref, out_ref, share_ref):
     plane, column, core, tp = place_ref[0], place_ref[1], place_ref[2], place_ref[3]
     frame = (plane * COLUMNS + column) * 2 + core
     rows = lax.broadcasted_iota(jnp.int32, (FRAME, 1), 0)
     live = rows < counts_ref[frame]
 
     def part(stats, i):
-        return pltpu.roll(stats, 128 - 8 * i, 1) if i else stats
+        return pltpu.roll(stats, 128 - HEADS * i, 1) if i else stats
 
     tops, totals = [], []
     for j in range(COLUMNS):
-        stats = parts_ref[j, :, WIDE:].astype(jnp.float32)
+        folded = parts_ref[j, HEADS * FRAME :, :].astype(jnp.float32)
+        stats = jnp.concatenate(
+            [folded] + [pltpu.roll(folded, 128 - 32 * k, 1) for k in range(1, FRAME // STATS)], axis=0
+        )
         tops.append(sum(part(stats, i) for i in range(1, TOP_PARTS)) + stats)
         totals.append(sum(part(stats, TOP_PARTS + i) for i in range(TOTAL_PARTS)))
     top = functools.reduce(jnp.maximum, tops)
     shares = [n * jnp.exp2((m - top) * EXP2_SCALE) for m, n in zip(tops, totals)]
     total = functools.reduce(jnp.add, shares)
-    shares = [jnp.where(live, share / total, 0.0) for share in shares]
+    for j, share in enumerate(shares):
+        share_ref[j] = jnp.where(live, share / total, 0.0)
+    half = FRAME // 2
+    first = (tp if own else 1 - tp) * half
+    heads = []
     for h in range(HEADS):
-        cols = slice(h * HEAD_DIM, (h + 1) * HEAD_DIM)
-        out = functools.reduce(
-            jnp.add,
-            [
-                parts_ref[j, :, cols].astype(jnp.float32) * shares[j][:, h : h + 1]
-                for j in range(COLUMNS)
-            ],
+        at = pl.ds(pl.multiple_of(h * FRAME + first, half), half)
+        share_at = pl.ds(pl.multiple_of(first, half), half)
+        heads.append(
+            functools.reduce(
+                jnp.add,
+                [
+                    parts_ref[j, at, :].astype(jnp.float32) * share_ref[j, share_at, h : h + 1]
+                    for j in range(COLUMNS)
+                ],
+            ).astype(jnp.bfloat16)
         )
-        att_ref[:, cols] = out.astype(jnp.bfloat16)
-    half = FRAME // tp_count
-    mine = pl.ds(pl.multiple_of(tp * half, half), half)
-    theirs = pl.ds(pl.multiple_of((1 - tp) * half, half), half)
-    att = jnp.concatenate([att_ref[theirs, :], att_ref[mine, :]], axis=0)
+    att = jnp.concatenate(heads, axis=1)
     step = 512
     for n in range(0, wo_ref.shape[1], step):
-        out = jnp.dot(att, wo_ref[:, n : n + step], preferred_element_type=jnp.float32)
-        send_ref[:, n : n + step] = out[:half].astype(jnp.bfloat16)
-        keep_ref[:, n : n + step] = out[half:]
-
-
-def project_call(place, counts, parts, wo):
+        out_ref[:, n : n + step] = jnp.dot(
+            att, wo_ref[:, n : n + step], preferred_element_type=jnp.float32
+        ).astype(out_ref.dtype)
+
+
+def project_call(place, counts, parts, wo, own):
     vmem = pl.BlockSpec(memory_space=pltpu.VMEM)
     smem = pl.BlockSpec(memory_space=pltpu.SMEM)
-    width = wo.shape[1]
     return pl.pallas_call(
-        functools.partial(project, 2),
-        out_shape=[
-            jax.ShapeDtypeStruct((FRAME // 2, width), jnp.bfloat16),
-            jax.ShapeDtypeStruct((FRAME // 2, width), jnp.float32),
-        ],
+        functools.partial(project, own),
+        out_shape=jax.ShapeDtypeStruct(
+            (FRAME // 2, wo.shape[1]), jnp.float32 if own else jnp.bfloat16
+        ),
         in_specs=[smem, smem, vmem, vmem],
-        out_specs=[vmem, vmem],
-        scratch_shapes=[pltpu.VMEM((FRAME, WIDE), jnp.bfloat16)],
+        out_specs=vmem,
+        scratch_shapes=[pltpu.VMEM((COLUMNS, FRAME, 128), jnp.float32)],
         compiler_params=pltpu.CompilerParams(vmem_limit_bytes=24 * 2**20),
-        name="project",
+        name="project_own" if own else "project_partner",
     )(place, counts, parts, wo)
 
 
@@ -259,8 +268,8 @@
     rest_off = [("both", 3, False), ("both", 3, True), ("half", 4, False), ("half", 4, True)]
     partial = attend_call(place, frame_tokens, q_all, rest, rest_off, state, True)
     parts = lax.all_to_all(partial, ("xh", "y"), 0, 0, tiled=True)
-    send, keep = project_call(place, frame_tokens, parts, wo)
-    got = lax.ppermute(send, "tp", SWAP)
+    got = lax.ppermute(project_call(place, frame_tokens, parts, wo, False), "tp", SWAP)
+    keep = project_call(place, frame_tokens, parts, wo, True)
     return (keep + got.astype(jnp.float32)).astype(jnp.bfloat16)
 
 

time: 73 us -> 72 us (0.986)
  waiting for transfers between devices: 15.1 us -> 13.1 us
  Pallas kernels: 9.17 us -> 10.9 us
  blocking collectives: 22.8 us -> 22 us
    ppermute x1, waiting for transfers between devices: 5.09 us -> 3.13 us  [on_device(): lax.ppermute(project_call(place, frame_tokens, parts, wo, False), 'tp', S...]
    pallas_call x1 -> x2, Pallas kernels: 2.28 us -> 3.92 us  [project_call(): pl.pallas_call(functools.partial(project, own), out_shape=jax.ShapeDtypeS...]
    all_to_all x1, blocking collectives: 22.8 us -> 22 us  [on_device(): parts = lax.all_to_all(partial, ('xh', 'y'), 0, 0, tiled=True)]
  transfers between devices with their start and end apart: 11 -> 11, of which waited for: 7 -> 7; matrix products, arithmetic and copies ran while one was open for 3% -> 3% of each run, Pallas kernels for 5% -> 8%
where the time goes in v4:
time: 72 us; the launch traced here: 71.7 us
  blocking collectives  22 us (31%)
  starting transfers between devices  21.9 us (30%)
  waiting for transfers between devices  13.1 us (18%)
  Pallas kernels  10.9 us (15%)
  local copies, waits for them, and re-layouts  1.87 us (3%)
  other arithmetic  1.81 us (3%)
    all_to_all x1, blocking collectives, on_device(): parts = lax.all_to_all(partial, ('xh', 'y'), 0, 0, tiled=True)  22 us
    pallas_call x2, Pallas kernels, attend_call(): pl.pallas_call(functools.partial(attend, offsets, state is not None, last...  6.98 us
    all_to_all x1, starting transfers between devices, on_device(): lax.all_to_all(jnp.broadcast_to(queries[None], (COLUMNS, FRAME, WIDE)), (...  6.93 us
    ppermute x1, starting transfers between devices, on_device(): fourth = lax.ppermute(second[:1], zc, split_ring(2))  4.27 us
    pallas_call x2, Pallas kernels, project_call(): pl.pallas_call(functools.partial(project, own), out_shape=jax.ShapeDtypeS...  3.92 us
    all_to_all x1, waiting for transfers between devices, on_device(): lax.all_to_all(jnp.broadcast_to(queries[None], (COLUMNS, FRAME, WIDE)), (...  3.36 us
    ppermute x1, starting transfers between devices, on_device(): second = lax.ppermute(own2, zc, split_ring(2))  3.35 us
    ppermute x1, waiting for transfers between devices, on_device(): lax.ppermute(project_call(place, frame_tokens, parts, wo, False), 'tp', S...  3.13 us
  transfers between devices with their start and end apart: 11, of which 7 were waited for; matrix products, arithmetic and copies ran while one was open for 3% of the time, Pallas kernels for 8%

profile of v4, /device:TPU:32, one launch (start us, length us, event | category | flops | bytes accessed | tf_op | source)
XLA Modules:
  0.0 71.7 jit_solution(11843277492605772615)
XLA Ops:
  0.0 1.0 %fusion = (bf16[1,2,64,768]{3,2,1,0:T(8,128)(2,1)S(1)}, bf16[2,64,768]{2,1,0:T(8,128)(2,1)S(1)}) fusion(bf16[1,64,768]{2,1,0:T(8,128)(2,1)} %bitcast.12, bf16[1,64,768]{2,1,0:T(8,128)(2,1)} %bitcast.13), kind=kLoop, calls=%fused_computation.4 | loop fusion | flops 98304 | bytes 589824 | tf_op jit(solution)/shard_map/stack | solution.py:242
  1.0 0.1 collective-permute-start
  1.1 1.4 %collective-permute-done = bf16[2,64,768]{2,1,0:T(8,128)(2,1)S(1)} collective-permute-done((bf16[2,64,768]{2,1,0:T(8,128)(2,1)S(1)}, bf16[2,64,768]{2,1,0:T(8,128)(2,1)S(1)}, u32[]{:S(2)}, u32[]{:S(2)}) %collective-permute-start) | collective-permute-done | bytes 196640 | tf_op jit(solution)/shard_map/ppermute | solution.py:242
  2.5 0.0 copy-start
  2.6 3.3 %collective-permute-start.1 = (bf16[2,2,64,768]{3,2,1,0:T(8,128)(2,1)S(1)}, bf16[2,2,64,768]{3,2,1,0:T(8,128)(2,1)S(1)}, u32[]{:S(2)}, u32[]{:S(2)}) collective-permute-start(bf16[2,2,64,768]{3,2,1,0:T(8,128)(2,1)S(1)} %pad_maximum_fusion.refs_3_), channel_id=1, source_target_pairs={{0,64},{2,194},{32,96},{34,226},{64,128},{66,2},{96,160},{98,34},{... | collective-permute-start | bytes 1179656 | tf_op jit(solution)/shard_map/ppermute | solution.py:245
  5.9 3.1 %collective-permute-start.4 = (bf16[2,2,64,768]{3,2,1,0:T(8,128)(2,1)S(1)}, bf16[2,2,64,768]{3,2,1,0:T(8,128)(2,1)S(1)}, u32[]{:S(2)}, u32[]{:S(2)}) collective-permute-start(bf16[2,2,64,768]{3,2,1,0:T(8,128)(2,1)S(1)} %pad_maximum_fusion.refs_3_), channel_id=1, source_target_pairs={{0,32},{2,226},{32,64},{34,2},{64,96},{66,34},{96,128},{98,66},{12... | collective-permute-start | bytes 1179656 | tf_op jit(solution)/shard_map/ppermute | solution.py:246
  9.0 1.8 %broadcast_in_dim.2 = bf16[8,64,768]{2,1,0:T(8,128)(2,1)} broadcast(bf16[64,768]{1,0:T(8,128)(2,1)} %param.5), dimensions={1,2} | broadcast | bytes 884736 | tf_op jit(solution)/shard_map/broadcast_in_dim | solution.py:248
  10.9 6.9 %all-to-all-start = ((bf16[8,64,768]{2,1,0:T(8,128)(2,1)}), bf16[8,64,768]{2,1,0:T(8,128)(2,1)S(1)}, u32[]{:S(2)}, u32[]{:S(2)}) async-start(bf16[8,64,768]{2,1,0:T(8,128)(2,1)} %broadcast_in_dim.2), calls=%async_computation | async-start | bytes 1572864 | tf_op jit(solution)/shard_map/all_to_all | solution.py:247
  17.8 0.3 collective-permute-done.1.refs_6_
  18.1 2.1 %collective-permute-done.4.refs_4_ = bf16[2,2,64,768]{3,2,1,0:T(8,128)(2,1)S(1)} collective-permute-done((bf16[2,2,64,768]{3,2,1,0:T(8,128)(2,1)S(1)}, bf16[2,2,64,768]{3,2,1,0:T(8,128)(2,1)S(1)}, u32[]{:S(2)}, u32[]{:S(2)}) %collective-permute-start.4) | collective-permute-done | bytes 393248 | tf_op jit(solution)/shard_map/ppermute | solution.py:246
  20.2 0.5 collective-permute-start.5
  20.7 0.0 collective-permute-start.6
  20.8 2.5 %collective-permute-start.2 = (bf16[2,2,64,768]{3,2,1,0:T(8,128)(2,1)S(1)}, bf16[2,2,64,768]{3,2,1,0:T(8,128)(2,1)S(1)}, u32[]{:S(2)}, u32[]{:S(2)}) collective-permute-start(bf16[2,2,64,768]{3,2,1,0:T(8,128)(2,1)S(1)} %collective-permute-done.1.refs_6_), channel_id=1, source_target_pairs={{0,32},{2,226},{32,64},{34,2},{64,96},{66,34},{96,128},{98,66},{12... | collective-permute-start | bytes 1179656 | tf_op jit(solution)/shard_map/ppermute | solution.py:251
  23.2 4.3 %collective-permute-start.3 = (bf16[1,2,64,768]{3,2,1,0:T(8,128)(2,1)S(1)}, bf16[1,2,64,768]{3,2,1,0:T(8,128)(2,1)S(1)}, u32[]{:S(2)}, u32[]{:S(2)}) collective-permute-start(bf16[1,2,64,768]{3,2,1,0:T(8,128)(2,1)S(1)} %slice.4), channel_id=1, source_target_pairs={{0,64},{2,194},{32,96},{34,226},{64,128},{66,2},{96,160},{98,34},{... | collective-permute-start | bytes 589832 | tf_op jit(solution)/shard_map/ppermute | solution.py:250
  27.5 0.1 pad_add_fusion.refs_0_.place_ref
  27.6 3.4 %all-to-all-done.refs_2_ = bf16[8,64,768]{2,1,0:T(8,128)(2,1)S(1)} async-done(((bf16[8,64,768]{2,1,0:T(8,128)(2,1)}), bf16[8,64,768]{2,1,0:T(8,128)(2,1)S(1)}, u32[]{:S(2)}, u32[]{:S(2)}) %all-to-all-start) | async-done | bytes 786464 | tf_op jit(solution)/shard_map/all_to_all | solution.py:247
  30.9 0.0 collective-permute-done.5.refs_5_
  30.9 0.0 collective-permute-done.6.refs_7_
  30.9 0.0 copy-done
  31.0 0.0 slice-start
  31.0 3.7 %attend_first.1 = (f32[512,768]{1,0:T(8,128)S(1)}, f32[6,512,128]{2,1,0:T(8,128)S(1)}, f32[6,512,128]{2,1,0:T(8,128)S(1)}) custom-call(s32[4]{0:T(128)S(1)} %pad_add_fusion.refs_0_.place_ref, s32[128]{0:T(128)S(1)} %copy-done, bf16[8,64,768]{2,1,0:T(8,128)(2,1)S(1)} %all-to-all-done.refs_2_, bf16[2,2,64,768]{3,2,1,0:T(8,128)(2,1)S(1)} %pad_maximum_fusion.refs_3_, ...), custom_call_target="tpu_custom_call" | custom-call | flops 1006632960 | bytes 4194304 | tf_op jit(solution)/shard_map/attend_first/pallas_call | solution.py:143
  34.7 1.3 %collective-permute-done.3.refs_5_ = bf16[1,2,64,768]{3,2,1,0:T(8,128)(2,1)S(1)} collective-permute-done((bf16[1,2,64,768]{3,2,1,0:T(8,128)(2,1)S(1)}, bf16[1,2,64,768]{3,2,1,0:T(8,128)(2,1)S(1)}, u32[]{:S(2)}, u32[]{:S(2)}) %collective-permute-start.3) | collective-permute-done | bytes 196640 | tf_op jit(solution)/shard_map/ppermute | solution.py:250
  36.0 0.0 collective-permute-done.2.refs_3_
  36.0 0.0 slice-start.1
  36.0 0.0 collective-permute-start.7
  36.0 0.5 collective-permute-start.8
  36.5 1.5 %collective-permute-done.8.refs_6_ = bf16[1,2,64,768]{3,2,1,0:T(8,128)(2,1)S(1)} collective-permute-done((bf16[1,2,64,768]{3,2,1,0:T(8,128)(2,1)S(1)}, bf16[1,2,64,768]{3,2,1,0:T(8,128)(2,1)S(1)}, u32[]{:S(2)}, u32[]{:S(2)}) %collective-permute-start.8) | collective-permute-done | bytes 196640 | tf_op jit(solution)/shard_map/ppermute | solution.py:266
  38.0 0.0 collective-permute-done.7.refs_4_
  38.0 3.2 %attend_last.1 = bf16[8,400,128]{2,1,0:T(8,128)(2,1)S(1)} custom-call(s32[4]{0:T(128)S(1)} %pad_add_fusion.refs_0_.place_ref, s32[128]{0:T(128)S(1)} %copy-done, bf16[8,64,768]{2,1,0:T(8,128)(2,1)S(1)} %all-to-all-done.refs_2_, bf16[2,2,64,768]{3,2,1,0:T(8,128)(2,1)S(1)} %collective-permute-done.2.refs_3_, ...), custom_call_target="tpu_custom_call" | custom-call | flops 603979776 | bytes 4194304 | tf_op jit(solution)/shard_map/attend_last/pallas_call | solution.py:143
  41.2 22.0 %all_to_all.10.parts_ref = bf16[8,400,128]{2,1,0:T(8,128)(2,1)S(1)} all-to-all(bf16[8,400,128]{2,1,0:T(8,128)(2,1)S(1)} %attend_last.1), channel_id=1, replica_groups=mesh['z'=8,'xh'=2,'y'=4,'core'=2,'tp'=2] {'xh','y'}, dimensions={0} | all-to-all | bytes 1638400 | tf_op jit(solution)/shard_map/all_to_all | solution.py:270
  63.2 0.0 slice-done
  63.2 0.0 slice-done.1
  63.2 2.0 %project_partner.1 = bf16[32,3072]{1,0:T(8,128)(2,1)S(1)} custom-call(s32[4]{0:T(128)S(1)} %pad_add_fusion.refs_0_.place_ref, s32[128]{0:T(128)S(1)} %copy-done, bf16[8,400,128]{2,1,0:T(8,128)(2,1)S(1)} %all_to_all.10.parts_ref, bf16[768,3072]{1,0:T(8,128)(2,1)S(1)} %bitcast.10), custom_call_target="tpu_custom_call" | custom-call | tf_op jit(solution)/shard_map/project_partner/pallas_call | solution.py:208
  65.2 0.7 collective-permute-start.9
  65.9 2.0 %project_own.1 = f32[32,3072]{1,0:T(8,128)S(1)} custom-call(s32[4]{0:T(128)S(1)} %pad_add_fusion.refs_0_.place_ref, s32[128]{0:T(128)S(1)} %copy-done, bf16[8,400,128]{2,1,0:T(8,128)(2,1)S(1)} %all_to_all.10.parts_ref, bf16[768,3072]{1,0:T(8,128)(2,1)S(1)} %bitcast.10), custom_call_target="tpu_custom_call" | custom-call | tf_op jit(solution)/shard_map/project_own/pallas_call | solution.py:208
  67.9 3.1 %collective-permute-done.9 = bf16[32,3072]{1,0:T(8,128)(2,1)S(1)} collective-permute-done((bf16[32,3072]{1,0:T(8,128)(2,1)S(1)}, bf16[32,3072]{1,0:T(8,128)(2,1)S(1)}, u32[]{:S(2)}, u32[]{:S(2)}) %collective-permute-start.9) | collective-permute-done | bytes 196640 | tf_op jit(solution)/shard_map/ppermute | solution.py:271
  71.0 0.7 %add_convert_fusion = bf16[32,3072]{1,0:T(8,128)(2,1)} fusion(f32[32,3072]{1,0:T(8,128)S(1)} %project_own.1, bf16[32,3072]{1,0:T(8,128)(2,1)S(1)} %collective-permute-done.9), kind=kLoop, calls=%fused_computation.1 | loop fusion | flops 294912 | bytes 786432 | tf_op jit(solution)/shard_map/convert_element_type | solution.py:273
  (3 shorter events, 0.1 us)
Async XLA Ops:
  1.0 1.5 %collective-permute-start = (bf16[2,64,768]{2,1,0:T(8,128)(2,1)S(1)}, bf16[2,64,768]{2,1,0:T(8,128)(2,1)S(1)}, u32[]{:S(2)}, u32[]{:S(2)}) collective-permute-start(bf16[2,64,768]{2,1,0:T(8,128)(2,1)S(1)} %get-tuple-element.30), channel_id=1, source_target_pairs={{0,2},{2,0},{1,3},{3,1},{4,6},{6,4},{5,7},{7,5},{8,10},{10,8},{9,1... | collective-permute-start | bytes 589832 | tf_op jit(solution)/shard_map/ppermute | solution.py:242
  2.5 28.4 %copy-start = (s32[128]{0:T(128)S(1)}, s32[128]{0:T(128)}, u32[]{:S(2)}) copy-start(s32[128]{0:T(128)} %counts_ref.3) | copy-start | bytes 1540
  2.6 15.6 %collective-permute-start.1 = (bf16[2,2,64,768]{3,2,1,0:T(8,128)(2,1)S(1)}, bf16[2,2,64,768]{3,2,1,0:T(8,128)(2,1)S(1)}, u32[]{:S(2)}, u32[]{:S(2)}) collective-permute-start(bf16[2,2,64,768]{3,2,1,0:T(8,128)(2,1)S(1)} %pad_maximum_fusion.refs_3_), channel_id=1, source_target_pairs={{0,64},{2,194},{32,96},{34,226},{64,128},{66,2},{96,160},{98,34},{... | collective-permute-start | bytes 1179656 | tf_op jit(solution)/shard_map/ppermute | solution.py:245
  5.9 14.3 %collective-permute-start.4 = (bf16[2,2,64,768]{3,2,1,0:T(8,128)(2,1)S(1)}, bf16[2,2,64,768]{3,2,1,0:T(8,128)(2,1)S(1)}, u32[]{:S(2)}, u32[]{:S(2)}) collective-permute-start(bf16[2,2,64,768]{3,2,1,0:T(8,128)(2,1)S(1)} %pad_maximum_fusion.refs_3_), channel_id=1, source_target_pairs={{0,32},{2,226},{32,64},{34,2},{64,96},{66,34},{96,128},{98,66},{12... | collective-permute-start | bytes 1179656 | tf_op jit(solution)/shard_map/ppermute | solution.py:246
  10.9 20.1 %all-to-all-start = ((bf16[8,64,768]{2,1,0:T(8,128)(2,1)}), bf16[8,64,768]{2,1,0:T(8,128)(2,1)S(1)}, u32[]{:S(2)}, u32[]{:S(2)}) async-start(bf16[8,64,768]{2,1,0:T(8,128)(2,1)} %broadcast_in_dim.2), calls=%async_computation | async-start | bytes 1572864 | tf_op jit(solution)/shard_map/all_to_all | solution.py:247
  20.2 10.7 %collective-permute-start.5 = (bf16[2,2,64,768]{3,2,1,0:T(8,128)(2,1)S(1)}, bf16[2,2,64,768]{3,2,1,0:T(8,128)(2,1)S(1)}, u32[]{:S(2)}, u32[]{:S(2)}) collective-permute-start(bf16[2,2,64,768]{3,2,1,0:T(8,128)(2,1)S(1)} %collective-permute-done.4.refs_4_), channel_id=1, source_target_pairs={{0,2},{2,0},{1,3},{3,1},{4,6},{6,4},{5,7},{7,5},{8,10},{10,8},{9,1... | collective-permute-start | bytes 1179656 | tf_op jit(solution)/shard_map/ppermute | solution.py:253
  20.7 10.2 %collective-permute-start.6 = (bf16[2,2,64,768]{3,2,1,0:T(8,128)(2,1)S(1)}, bf16[2,2,64,768]{3,2,1,0:T(8,128)(2,1)S(1)}, u32[]{:S(2)}, u32[]{:S(2)}) collective-permute-start(bf16[2,2,64,768]{3,2,1,0:T(8,128)(2,1)S(1)} %collective-permute-done.1.refs_6_), channel_id=1, source_target_pairs={{0,2},{2,0},{1,3},{3,1},{4,6},{6,4},{5,7},{7,5},{8,10},{10,8},{9,1... | collective-permute-start | bytes 1179656 | tf_op jit(solution)/shard_map/ppermute | solution.py:254
  20.8 15.2 %collective-permute-start.2 = (bf16[2,2,64,768]{3,2,1,0:T(8,128)(2,1)S(1)}, bf16[2,2,64,768]{3,2,1,0:T(8,128)(2,1)S(1)}, u32[]{:S(2)}, u32[]{:S(2)}) collective-permute-start(bf16[2,2,64,768]{3,2,1,0:T(8,128)(2,1)S(1)} %collective-permute-done.1.refs_6_), channel_id=1, source_target_pairs={{0,32},{2,226},{32,64},{34,2},{64,96},{66,34},{96,128},{98,66},{12... | collective-permute-start | bytes 1179656 | tf_op jit(solution)/shard_map/ppermute | solution.py:251
  23.2 12.7 %collective-permute-start.3 = (bf16[1,2,64,768]{3,2,1,0:T(8,128)(2,1)S(1)}, bf16[1,2,64,768]{3,2,1,0:T(8,128)(2,1)S(1)}, u32[]{:S(2)}, u32[]{:S(2)}) collective-permute-start(bf16[1,2,64,768]{3,2,1,0:T(8,128)(2,1)S(1)} %slice.4), channel_id=1, source_target_pairs={{0,64},{2,194},{32,96},{34,226},{64,128},{66,2},{96,160},{98,34},{... | collective-permute-start | bytes 589832 | tf_op jit(solution)/shard_map/ppermute | solution.py:250
  31.0 32.3 %slice-start = ((s8[4718592]{0:T(1024)(128)(4,1)}), s8[4194304]{0:T(1024)(128)(4,1)S(1)}, s32[]{:S(2)}) async-start(s8[4718592]{0:T(1024)(128)(4,1)} %bitcast.9), calls=%async_computation.2 | async-start | bytes 8388608
  36.0 27.3 %slice-start.1 = ((s8[4718592]{0:T(1024)(128)(4,1)}), s8[524288]{0:T(1024)(128)(4,1)S(1)}, s32[]{:S(2)}) async-start(s8[4718592]{0:T(1024)(128)(4,1)} %bitcast.9), calls=%async_computation.3 | async-start | bytes 1048576
  36.0 2.0 %collective-permute-start.7 = (bf16[2,2,64,768]{3,2,1,0:T(8,128)(2,1)S(1)}, bf16[2,2,64,768]{3,2,1,0:T(8,128)(2,1)S(1)}, u32[]{:S(2)}, u32[]{:S(2)}) collective-permute-start(bf16[2,2,64,768]{3,2,1,0:T(8,128)(2,1)S(1)} %collective-permute-done.2.refs_3_), channel_id=1, source_target_pairs={{0,2},{2,0},{1,3},{3,1},{4,6},{6,4},{5,7},{7,5},{8,10},{10,8},{9,1... | collective-permute-start | bytes 1179656 | tf_op jit(solution)/shard_map/ppermute | solution.py:265
  36.0 2.0 %collective-permute-start.8 = (bf16[1,2,64,768]{3,2,1,0:T(8,128)(2,1)S(1)}, bf16[1,2,64,768]{3,2,1,0:T(8,128)(2,1)S(1)}, u32[]{:S(2)}, u32[]{:S(2)}) collective-permute-start(bf16[1,2,64,768]{3,2,1,0:T(8,128)(2,1)S(1)} %collective-permute-done.3.refs_5_), channel_id=1, source_target_pairs={{0,2},{2,0},{1,3},{3,1},{4,6},{6,4},{5,7},{7,5},{8,10},{10,8},{9,1... | collective-permute-start | bytes 589832 | tf_op jit(solution)/shard_map/ppermute | solution.py:266
  65.2 5.8 %collective-permute-start.9 = (bf16[32,3072]{1,0:T(8,128)(2,1)S(1)}, bf16[32,3072]{1,0:T(8,128)(2,1)S(1)}, u32[]{:S(2)}, u32[]{:S(2)}) collective-permute-start(bf16[32,3072]{1,0:T(8,128)(2,1)S(1)} %project_partner.1), channel_id=1, source_target_pairs={{0,1},{1,0},{2,3},{3,2},{4,5},{5,4},{6,7},{7,6},{8,9},{9,8},{10,11... | collective-permute-start | bytes 589832 | tf_op jit(solution)/shard_map/ppermute | solution.py:271

commit v5 on v4

--- a/solution.py
+++ b/solution.py
@@ -249,23 +249,30 @@
     )
     fourth = lax.ppermute(second[:1], zc, split_ring(2))
     third = lax.ppermute(second, zc, split_ring(1))
-    near, second = lax.optimization_barrier((near, second))
+    near, q_all = lax.optimization_barrier((near, q_all))
+    second_o = lax.ppermute(second, "core", SWAP)
+    state = attend_call(
+        place,
+        frame_tokens,
+        q_all,
+        [own2, second, second_o],
+        [("both", 0, False), ("both", 2, False), ("both", 2, True)],
+        None,
+        False,
+    )
+    near, third, fourth, state = lax.optimization_barrier((near, third, fourth, state))
     near_o = lax.ppermute(near, "core", SWAP)
-    second_o = lax.ppermute(second, "core", SWAP)
-    first = [own2, near, near_o, second, second_o]
-    first_off = [
-        ("both", 0, False),
+    third_o = lax.ppermute(third, "core", SWAP)
+    fourth_o = lax.ppermute(fourth, "core", SWAP)
+    rest = [near, near_o, third, third_o, fourth, fourth_o]
+    rest_off = [
         ("both", 1, False),
         ("both", 1, True),
-        ("both", 2, False),
-        ("both", 2, True),
+        ("both", 3, False),
+        ("both", 3, True),
+        ("half", 4, False),
+        ("half", 4, True),
     ]
-    state = attend_call(place, frame_tokens, q_all, first, first_off, None, False)
-    third, fourth, state = lax.optimization_barrier((third, fourth, state))
-    third_o = lax.ppermute(third, "core", SWAP)
-    fourth_o = lax.ppermute(fourth, "core", SWAP)
-    rest = [third, third_o, fourth, fourth_o]
-    rest_off = [("both", 3, False), ("both", 3, True), ("half", 4, False), ("half", 4, True)]
     partial = attend_call(place, frame_tokens, q_all, rest, rest_off, state, True)
     parts = lax.all_to_all(partial, ("xh", "y"), 0, 0, tiled=True)
     got = lax.ppermute(project_call(place, frame_tokens, parts, wo, False), "tp", SWAP)

time: 72 us -> 69.5 us (0.965)
  starting transfers between devices: 21.9 us -> 20 us
  waiting for transfers between devices: 13.1 us -> 12.3 us
    ppermute x1, waiting for transfers between devices: 2.13 us -> 0.01 us  [on_device(): near = lax.ppermute(own2, zc, split_ring(1))]
    ppermute x1, starting transfers between devices: 2.46 us -> 0.82 us  [on_device(): third = lax.ppermute(second, zc, split_ring(1))]
    all_to_all x1, waiting for transfers between devices: 3.36 us -> 4.75 us  [on_device(): lax.all_to_all(jnp.broadcast_to(queries[None], (COLUMNS, FRAME, WIDE)), (...]
  transfers between devices with their start and end apart: 11 -> 11, of which waited for: 7 -> 6; matrix products, arithmetic and copies ran while one was open for 3% -> 3% of each run, Pallas kernels for 8% -> 7%
where the time goes in v5:
time: 69.5 us; the launch traced here: 69.2 us
  blocking collectives  22.3 us (32%)
  starting transfers between devices  20 us (29%)
  waiting for transfers between devices  12.3 us (18%)
  Pallas kernels  10.9 us (16%)
  local copies, waits for them, and re-layouts  1.87 us (3%)
  other arithmetic  1.79 us (3%)
    all_to_all x1, blocking collectives, on_device(): parts = lax.all_to_all(partial, ('xh', 'y'), 0, 0, tiled=True)  22.3 us
    pallas_call x2, Pallas kernels, attend_call(): pl.pallas_call(functools.partial(attend, offsets, state is not None, last...  6.97 us
    all_to_all x1, starting transfers between devices, on_device(): lax.all_to_all(jnp.broadcast_to(queries[None], (COLUMNS, FRAME, WIDE)), (...  6.93 us
    all_to_all x1, waiting for transfers between devices, on_device(): lax.all_to_all(jnp.broadcast_to(queries[None], (COLUMNS, FRAME, WIDE)), (...  4.75 us
    ppermute x1, starting transfers between devices, on_device(): fourth = lax.ppermute(second[:1], zc, split_ring(2))  4.29 us
    pallas_call x2, Pallas kernels, project_call(): pl.pallas_call(functools.partial(project, own), out_shape=jax.ShapeDtypeS...  3.92 us
    ppermute x1, starting transfers between devices, on_device(): second = lax.ppermute(own2, zc, split_ring(2))  3.35 us
    ppermute x1, waiting for transfers between devices, on_device(): lax.ppermute(project_call(place, frame_tokens, parts, wo, False), 'tp', S...  3.15 us
  transfers between devices with their start and end apart: 11, of which 6 were waited for; matrix products, arithmetic and copies ran while one was open for 3% of the time, Pallas kernels for 7%

profile of v5, /device:TPU:32, one launch (start us, length us, event | category | flops | bytes accessed | tf_op | source)
XLA Modules:
  0.0 69.2 jit_solution(908181478274801994)
XLA Ops:
  0.0 1.0 %fusion = (bf16[1,2,64,768]{3,2,1,0:T(8,128)(2,1)S(1)}, bf16[2,64,768]{2,1,0:T(8,128)(2,1)S(1)}) fusion(bf16[1,64,768]{2,1,0:T(8,128)(2,1)} %bitcast.12, bf16[1,64,768]{2,1,0:T(8,128)(2,1)} %bitcast.13), kind=kLoop, calls=%fused_computation.4 | loop fusion | flops 98304 | bytes 589824 | tf_op jit(solution)/shard_map/stack | solution.py:242
  1.0 0.1 collective-permute-start
  1.1 1.4 %collective-permute-done = bf16[2,64,768]{2,1,0:T(8,128)(2,1)S(1)} collective-permute-done((bf16[2,64,768]{2,1,0:T(8,128)(2,1)S(1)}, bf16[2,64,768]{2,1,0:T(8,128)(2,1)S(1)}, u32[]{:S(2)}, u32[]{:S(2)}) %collective-permute-start) | collective-permute-done | bytes 196640 | tf_op jit(solution)/shard_map/ppermute | solution.py:242
  2.5 0.0 copy-start
  2.6 3.3 %collective-permute-start.2 = (bf16[2,2,64,768]{3,2,1,0:T(8,128)(2,1)S(1)}, bf16[2,2,64,768]{3,2,1,0:T(8,128)(2,1)S(1)}, u32[]{:S(2)}, u32[]{:S(2)}) collective-permute-start(bf16[2,2,64,768]{3,2,1,0:T(8,128)(2,1)S(1)} %pad_maximum_fusion.refs_3_), channel_id=1, source_target_pairs={{0,64},{2,194},{32,96},{34,226},{64,128},{66,2},{96,160},{98,34},{... | collective-permute-start | bytes 1179656 | tf_op jit(solution)/shard_map/ppermute | solution.py:245
  5.9 1.8 %broadcast_in_dim.2 = bf16[8,64,768]{2,1,0:T(8,128)(2,1)} broadcast(bf16[64,768]{1,0:T(8,128)(2,1)} %param.5), dimensions={1,2} | broadcast | bytes 884736 | tf_op jit(solution)/shard_map/broadcast_in_dim | solution.py:248
  7.7 6.9 %all-to-all-start = ((bf16[8,64,768]{2,1,0:T(8,128)(2,1)}), bf16[8,64,768]{2,1,0:T(8,128)(2,1)S(1)}, u32[]{:S(2)}, u32[]{:S(2)}) async-start(bf16[8,64,768]{2,1,0:T(8,128)(2,1)} %broadcast_in_dim.2), calls=%async_computation | async-start | bytes 1572864 | tf_op jit(solution)/shard_map/all_to_all | solution.py:247
  14.7 3.1 %collective-permute-start.1 = (bf16[2,2,64,768]{3,2,1,0:T(8,128)(2,1)S(1)}, bf16[2,2,64,768]{3,2,1,0:T(8,128)(2,1)S(1)}, u32[]{:S(2)}, u32[]{:S(2)}) collective-permute-start(bf16[2,2,64,768]{3,2,1,0:T(8,128)(2,1)S(1)} %pad_maximum_fusion.refs_3_), channel_id=1, source_target_pairs={{0,32},{2,226},{32,64},{34,2},{64,96},{66,34},{96,128},{98,66},{12... | collective-permute-start | bytes 1179656 | tf_op jit(solution)/shard_map/ppermute | solution.py:246
  17.8 0.2 collective-permute-done.2.refs_4_
  18.0 0.0 collective-permute-start.5
  18.0 0.8 %collective-permute-start.3 = (bf16[2,2,64,768]{3,2,1,0:T(8,128)(2,1)S(1)}, bf16[2,2,64,768]{3,2,1,0:T(8,128)(2,1)S(1)}, u32[]{:S(2)}, u32[]{:S(2)}) collective-permute-start(bf16[2,2,64,768]{3,2,1,0:T(8,128)(2,1)S(1)} %collective-permute-done.2.refs_4_), channel_id=1, source_target_pairs={{0,32},{2,226},{32,64},{34,2},{64,96},{66,34},{96,128},{98,66},{12... | collective-permute-start | bytes 1179656 | tf_op jit(solution)/shard_map/ppermute | solution.py:251
  18.8 4.3 %collective-permute-start.4 = (bf16[1,2,64,768]{3,2,1,0:T(8,128)(2,1)S(1)}, bf16[1,2,64,768]{3,2,1,0:T(8,128)(2,1)S(1)}, u32[]{:S(2)}, u32[]{:S(2)}) collective-permute-start(bf16[1,2,64,768]{3,2,1,0:T(8,128)(2,1)S(1)} %slice.4), channel_id=1, source_target_pairs={{0,64},{2,194},{32,96},{34,226},{64,128},{66,2},{96,160},{98,34},{... | collective-permute-start | bytes 589832 | tf_op jit(solution)/shard_map/ppermute | solution.py:250
  23.1 0.1 pad_add_fusion.refs_0_.place_ref
  23.2 0.0 collective-permute-done.1.refs_3_
  23.2 4.8 %all-to-all-done.refs_2_ = bf16[8,64,768]{2,1,0:T(8,128)(2,1)S(1)} async-done(((bf16[8,64,768]{2,1,0:T(8,128)(2,1)}), bf16[8,64,768]{2,1,0:T(8,128)(2,1)S(1)}, u32[]{:S(2)}, u32[]{:S(2)}) %all-to-all-start) | async-done | bytes 786464 | tf_op jit(solution)/shard_map/all_to_all | solution.py:247
  28.0 0.0 collective-permute-done.5.refs_5_
  28.0 0.0 copy-done
  28.0 0.0 slice-start
  28.0 2.6 %attend_first.1 = (f32[512,768]{1,0:T(8,128)S(1)}, f32[6,512,128]{2,1,0:T(8,128)S(1)}, f32[6,512,128]{2,1,0:T(8,128)S(1)}) custom-call(s32[4]{0:T(128)S(1)} %pad_add_fusion.refs_0_.place_ref, s32[128]{0:T(128)S(1)} %copy-done, bf16[8,64,768]{2,1,0:T(8,128)(2,1)S(1)} %all-to-all-done.refs_2_, bf16[2,2,64,768]{3,2,1,0:T(8,128)(2,1)S(1)} %pad_maximum_fusion.refs_3_, ...), custom_call_target="tpu_custom_call" | custom-call | flops 603979776 | bytes 4194304 | tf_op jit(solution)/shard_map/attend_first/pallas_call | solution.py:143
  30.6 0.9 %collective-permute-done.4.refs_7_ = bf16[1,2,64,768]{3,2,1,0:T(8,128)(2,1)S(1)} collective-permute-done((bf16[1,2,64,768]{3,2,1,0:T(8,128)(2,1)S(1)}, bf16[1,2,64,768]{3,2,1,0:T(8,128)(2,1)S(1)}, u32[]{:S(2)}, u32[]{:S(2)}) %collective-permute-start.4) | collective-permute-done | bytes 196640 | tf_op jit(solution)/shard_map/ppermute | solution.py:250
  31.5 0.0 collective-permute-done.3.refs_5_
  31.5 0.0 slice-start.1
  31.5 0.2 collective-permute-start.6
  31.7 0.3 collective-permute-start.7
  32.0 0.2 collective-permute-start.8
  32.2 1.9 %collective-permute-done.8.refs_8_ = bf16[1,2,64,768]{3,2,1,0:T(8,128)(2,1)S(1)} collective-permute-done((bf16[1,2,64,768]{3,2,1,0:T(8,128)(2,1)S(1)}, bf16[1,2,64,768]{3,2,1,0:T(8,128)(2,1)S(1)}, u32[]{:S(2)}, u32[]{:S(2)}) %collective-permute-start.8) | collective-permute-done | bytes 196640 | tf_op jit(solution)/shard_map/ppermute | solution.py:266
  34.1 0.0 collective-permute-done.6.refs_4_
  34.1 0.0 collective-permute-done.7.refs_6_
  34.1 4.3 %attend_last.1 = bf16[8,400,128]{2,1,0:T(8,128)(2,1)S(1)} custom-call(s32[4]{0:T(128)S(1)} %pad_add_fusion.refs_0_.place_ref, s32[128]{0:T(128)S(1)} %copy-done, bf16[8,64,768]{2,1,0:T(8,128)(2,1)S(1)} %all-to-all-done.refs_2_, bf16[2,2,64,768]{3,2,1,0:T(8,128)(2,1)S(1)} %collective-permute-done.1.refs_3_, ...), custom_call_target="tpu_custom_call" | custom-call | flops 1006632960 | bytes 4194304 | tf_op jit(solution)/shard_map/attend_last/pallas_call | solution.py:143
  38.4 22.3 %all_to_all.10.parts_ref = bf16[8,400,128]{2,1,0:T(8,128)(2,1)S(1)} all-to-all(bf16[8,400,128]{2,1,0:T(8,128)(2,1)S(1)} %attend_last.1), channel_id=1, replica_groups=mesh['z'=8,'xh'=2,'y'=4,'core'=2,'tp'=2] {'xh','y'}, dimensions={0} | all-to-all | bytes 1638400 | tf_op jit(solution)/shard_map/all_to_all | solution.py:277
  60.7 0.0 slice-done
  60.7 0.0 slice-done.1
  60.7 2.0 %project_partner.1 = bf16[32,3072]{1,0:T(8,128)(2,1)S(1)} custom-call(s32[4]{0:T(128)S(1)} %pad_add_fusion.refs_0_.place_ref, s32[128]{0:T(128)S(1)} %copy-done, bf16[8,400,128]{2,1,0:T(8,128)(2,1)S(1)} %all_to_all.10.parts_ref, bf16[768,3072]{1,0:T(8,128)(2,1)S(1)} %bitcast.10), custom_call_target="tpu_custom_call" | custom-call | tf_op jit(solution)/shard_map/project_partner/pallas_call | solution.py:208
  62.7 0.7 collective-permute-start.9
  63.3 2.0 %project_own.1 = f32[32,3072]{1,0:T(8,128)S(1)} custom-call(s32[4]{0:T(128)S(1)} %pad_add_fusion.refs_0_.place_ref, s32[128]{0:T(128)S(1)} %copy-done, bf16[8,400,128]{2,1,0:T(8,128)(2,1)S(1)} %all_to_all.10.parts_ref, bf16[768,3072]{1,0:T(8,128)(2,1)S(1)} %bitcast.10), custom_call_target="tpu_custom_call" | custom-call | tf_op jit(solution)/shard_map/project_own/pallas_call | solution.py:208
  65.3 3.2 %collective-permute-done.9 = bf16[32,3072]{1,0:T(8,128)(2,1)S(1)} collective-permute-done((bf16[32,3072]{1,0:T(8,128)(2,1)S(1)}, bf16[32,3072]{1,0:T(8,128)(2,1)S(1)}, u32[]{:S(2)}, u32[]{:S(2)}) %collective-permute-start.9) | collective-permute-done | bytes 196640 | tf_op jit(solution)/shard_map/ppermute | solution.py:278
  68.5 0.7 %add_convert_fusion = bf16[32,3072]{1,0:T(8,128)(2,1)} fusion(f32[32,3072]{1,0:T(8,128)S(1)} %project_own.1, bf16[32,3072]{1,0:T(8,128)(2,1)S(1)} %collective-permute-done.9), kind=kLoop, calls=%fused_computation.1 | loop fusion | flops 294912 | bytes 786432 | tf_op jit(solution)/shard_map/convert_element_type | solution.py:280
  (3 shorter events, 0.1 us)
Async XLA Ops:
  1.0 1.5 %collective-permute-start = (bf16[2,64,768]{2,1,0:T(8,128)(2,1)S(1)}, bf16[2,64,768]{2,1,0:T(8,128)(2,1)S(1)}, u32[]{:S(2)}, u32[]{:S(2)}) collective-permute-start(bf16[2,64,768]{2,1,0:T(8,128)(2,1)S(1)} %get-tuple-element.32), channel_id=1, source_target_pairs={{0,2},{2,0},{1,3},{3,1},{4,6},{6,4},{5,7},{7,5},{8,10},{10,8},{9,1... | collective-permute-start | bytes 589832 | tf_op jit(solution)/shard_map/ppermute | solution.py:242
  2.5 25.4 %copy-start = (s32[128]{0:T(128)S(1)}, s32[128]{0:T(128)}, u32[]{:S(2)}) copy-start(s32[128]{0:T(128)} %counts_ref.3) | copy-start | bytes 1540
  2.6 15.4 %collective-permute-start.2 = (bf16[2,2,64,768]{3,2,1,0:T(8,128)(2,1)S(1)}, bf16[2,2,64,768]{3,2,1,0:T(8,128)(2,1)S(1)}, u32[]{:S(2)}, u32[]{:S(2)}) collective-permute-start(bf16[2,2,64,768]{3,2,1,0:T(8,128)(2,1)S(1)} %pad_maximum_fusion.refs_3_), channel_id=1, source_target_pairs={{0,64},{2,194},{32,96},{34,226},{64,128},{66,2},{96,160},{98,34},{... | collective-permute-start | bytes 1179656 | tf_op jit(solution)/shard_map/ppermute | solution.py:245
  7.7 20.2 %all-to-all-start = ((bf16[8,64,768]{2,1,0:T(8,128)(2,1)}), bf16[8,64,768]{2,1,0:T(8,128)(2,1)S(1)}, u32[]{:S(2)}, u32[]{:S(2)}) async-start(bf16[8,64,768]{2,1,0:T(8,128)(2,1)} %broadcast_in_dim.2), calls=%async_computation | async-start | bytes 1572864 | tf_op jit(solution)/shard_map/all_to_all | solution.py:247
  14.7 8.5 %collective-permute-start.1 = (bf16[2,2,64,768]{3,2,1,0:T(8,128)(2,1)S(1)}, bf16[2,2,64,768]{3,2,1,0:T(8,128)(2,1)S(1)}, u32[]{:S(2)}, u32[]{:S(2)}) collective-permute-start(bf16[2,2,64,768]{3,2,1,0:T(8,128)(2,1)S(1)} %pad_maximum_fusion.refs_3_), channel_id=1, source_target_pairs={{0,32},{2,226},{32,64},{34,2},{64,96},{66,34},{96,128},{98,66},{12... | collective-permute-start | bytes 1179656 | tf_op jit(solution)/shard_map/ppermute | solution.py:246
  18.0 10.0 %collective-permute-start.5 = (bf16[2,2,64,768]{3,2,1,0:T(8,128)(2,1)S(1)}, bf16[2,2,64,768]{3,2,1,0:T(8,128)(2,1)S(1)}, u32[]{:S(2)}, u32[]{:S(2)}) collective-permute-start(bf16[2,2,64,768]{3,2,1,0:T(8,128)(2,1)S(1)} %collective-permute-done.2.refs_4_), channel_id=1, source_target_pairs={{0,2},{2,0},{1,3},{3,1},{4,6},{6,4},{5,7},{7,5},{8,10},{10,8},{9,1... | collective-permute-start | bytes 1179656 | tf_op jit(solution)/shard_map/ppermute | solution.py:253
  18.0 13.5 %collective-permute-start.3 = (bf16[2,2,64,768]{3,2,1,0:T(8,128)(2,1)S(1)}, bf16[2,2,64,768]{3,2,1,0:T(8,128)(2,1)S(1)}, u32[]{:S(2)}, u32[]{:S(2)}) collective-permute-start(bf16[2,2,64,768]{3,2,1,0:T(8,128)(2,1)S(1)} %collective-permute-done.2.refs_4_), channel_id=1, source_target_pairs={{0,32},{2,226},{32,64},{34,2},{64,96},{66,34},{96,128},{98,66},{12... | collective-permute-start | bytes 1179656 | tf_op jit(solution)/shard_map/ppermute | solution.py:251
  18.8 12.7 %collective-permute-start.4 = (bf16[1,2,64,768]{3,2,1,0:T(8,128)(2,1)S(1)}, bf16[1,2,64,768]{3,2,1,0:T(8,128)(2,1)S(1)}, u32[]{:S(2)}, u32[]{:S(2)}) collective-permute-start(bf16[1,2,64,768]{3,2,1,0:T(8,128)(2,1)S(1)} %slice.4), channel_id=1, source_target_pairs={{0,64},{2,194},{32,96},{34,226},{64,128},{66,2},{96,160},{98,34},{... | collective-permute-start | bytes 589832 | tf_op jit(solution)/shard_map/ppermute | solution.py:250
  28.0 32.7 %slice-start = ((s8[4718592]{0:T(1024)(128)(4,1)}), s8[4194304]{0:T(1024)(128)(4,1)S(1)}, s32[]{:S(2)}) async-start(s8[4718592]{0:T(1024)(128)(4,1)} %bitcast.9), calls=%async_computation.2 | async-start | bytes 8388608
  31.5 29.2 %slice-start.1 = ((s8[4718592]{0:T(1024)(128)(4,1)}), s8[524288]{0:T(1024)(128)(4,1)S(1)}, s32[]{:S(2)}) async-start(s8[4718592]{0:T(1024)(128)(4,1)} %bitcast.9), calls=%async_computation.3 | async-start | bytes 1048576
  31.5 2.6 %collective-permute-start.6 = (bf16[2,2,64,768]{3,2,1,0:T(8,128)(2,1)S(1)}, bf16[2,2,64,768]{3,2,1,0:T(8,128)(2,1)S(1)}, u32[]{:S(2)}, u32[]{:S(2)}) collective-permute-start(bf16[2,2,64,768]{3,2,1,0:T(8,128)(2,1)S(1)} %collective-permute-done.1.refs_3_), channel_id=1, source_target_pairs={{0,2},{2,0},{1,3},{3,1},{4,6},{6,4},{5,7},{7,5},{8,10},{10,8},{9,1... | collective-permute-start | bytes 1179656 | tf_op jit(solution)/shard_map/ppermute | solution.py:264
  31.7 2.4 %collective-permute-start.7 = (bf16[2,2,64,768]{3,2,1,0:T(8,128)(2,1)S(1)}, bf16[2,2,64,768]{3,2,1,0:T(8,128)(2,1)S(1)}, u32[]{:S(2)}, u32[]{:S(2)}) collective-permute-start(bf16[2,2,64,768]{3,2,1,0:T(8,128)(2,1)S(1)} %collective-permute-done.3.refs_5_), channel_id=1, source_target_pairs={{0,2},{2,0},{1,3},{3,1},{4,6},{6,4},{5,7},{7,5},{8,10},{10,8},{9,1... | collective-permute-start | bytes 1179656 | tf_op jit(solution)/shard_map/ppermute | solution.py:265
  32.0 2.1 %collective-permute-start.8 = (bf16[1,2,64,768]{3,2,1,0:T(8,128)(2,1)S(1)}, bf16[1,2,64,768]{3,2,1,0:T(8,128)(2,1)S(1)}, u32[]{:S(2)}, u32[]{:S(2)}) collective-permute-start(bf16[1,2,64,768]{3,2,1,0:T(8,128)(2,1)S(1)} %collective-permute-done.4.refs_7_), channel_id=1, source_target_pairs={{0,2},{2,0},{1,3},{3,1},{4,6},{6,4},{5,7},{7,5},{8,10},{10,8},{9,1... | collective-permute-start | bytes 589832 | tf_op jit(solution)/shard_map/ppermute | solution.py:266
  62.7 5.8 %collective-permute-start.9 = (bf16[32,3072]{1,0:T(8,128)(2,1)S(1)}, bf16[32,3072]{1,0:T(8,128)(2,1)S(1)}, u32[]{:S(2)}, u32[]{:S(2)}) collective-permute-start(bf16[32,3072]{1,0:T(8,128)(2,1)S(1)} %project_partner.1), channel_id=1, source_target_pairs={{0,1},{1,0},{2,3},{3,2},{4,5},{5,4},{6,7},{7,6},{8,9},{9,8},{10,11... | collective-permute-start | bytes 589832 | tf_op jit(solution)/shard_map/ppermute | solution.py:278

commit v6 on v5

--- a/solution.py
+++ b/solution.py
@@ -255,8 +255,8 @@
         place,
         frame_tokens,
         q_all,
-        [own2, second, second_o],
-        [("both", 0, False), ("both", 2, False), ("both", 2, True)],
+        [own2, near, second, second_o],
+        [("both", 0, False), ("both", 1, False), ("both", 2, False), ("both", 2, True)],
         None,
         False,
     )
@@ -264,9 +264,8 @@
     near_o = lax.ppermute(near, "core", SWAP)
     third_o = lax.ppermute(third, "core", SWAP)
     fourth_o = lax.ppermute(fourth, "core", SWAP)
-    rest = [near, near_o, third, third_o, fourth, fourth_o]
+    rest = [near_o, third, third_o, fourth, fourth_o]
     rest_off = [
-        ("both", 1, False),
         ("both", 1, True),
         ("both", 3, False),
         ("both", 3, True),

time: 69.5 us -> 68.7 us (0.988)
  Pallas kernels: 10.9 us -> 10.2 us
where the time goes in v6:
time: 68.7 us; the launch traced here: 68.4 us
  blocking collectives  22.3 us (32%)
  starting transfers between devices  20.1 us (29%)
  waiting for transfers between devices  12 us (17%)
  Pallas kernels  10.2 us (15%)
  local copies, waits for them, and re-layouts  1.87 us (3%)
  other arithmetic  1.79 us (3%)
    all_to_all x1, blocking collectives, on_device(): parts = lax.all_to_all(partial, ('xh', 'y'), 0, 0, tiled=True)  22.3 us
    all_to_all x1, starting transfers between devices, on_device(): lax.all_to_all(jnp.broadcast_to(queries[None], (COLUMNS, FRAME, WIDE)), (...  6.93 us
    pallas_call x2, Pallas kernels, attend_call(): pl.pallas_call(functools.partial(attend, offsets, state is not None, last...  6.32 us
    all_to_all x1, waiting for transfers between devices, on_device(): lax.all_to_all(jnp.broadcast_to(queries[None], (COLUMNS, FRAME, WIDE)), (...  4.75 us
    ppermute x1, starting transfers between devices, on_device(): fourth = lax.ppermute(second[:1], zc, split_ring(2))  4.29 us
    pallas_call x2, Pallas kernels, project_call(): pl.pallas_call(functools.partial(project, own), out_shape=jax.ShapeDtypeS...  3.92 us
    ppermute x1, starting transfers between devices, on_device(): second = lax.ppermute(own2, zc, split_ring(2))  3.35 us
    ppermute x1, waiting for transfers between devices, on_device(): lax.ppermute(project_call(place, frame_tokens, parts, wo, False), 'tp', S...  3.14 us
  transfers between devices with their start and end apart: 11, of which 6 were waited for; matrix products, arithmetic and copies ran while one was open for 3% of the time, Pallas kernels for 7%

profile of v6, /device:TPU:32, one launch (start us, length us, event | category | flops | bytes accessed | tf_op | source)
XLA Modules:
  0.0 68.4 jit_solution(15012485737760119853)
XLA Ops:
  0.0 1.0 %fusion = (bf16[1,2,64,768]{3,2,1,0:T(8,128)(2,1)S(1)}, bf16[2,64,768]{2,1,0:T(8,128)(2,1)S(1)}) fusion(bf16[1,64,768]{2,1,0:T(8,128)(2,1)} %bitcast.12, bf16[1,64,768]{2,1,0:T(8,128)(2,1)} %bitcast.13), kind=kLoop, calls=%fused_computation.4 | loop fusion | flops 98304 | bytes 589824 | tf_op jit(solution)/shard_map/stack | solution.py:242
  1.0 0.1 collective-permute-start
  1.1 1.4 %collective-permute-done = bf16[2,64,768]{2,1,0:T(8,128)(2,1)S(1)} collective-permute-done((bf16[2,64,768]{2,1,0:T(8,128)(2,1)S(1)}, bf16[2,64,768]{2,1,0:T(8,128)(2,1)S(1)}, u32[]{:S(2)}, u32[]{:S(2)}) %collective-permute-start) | collective-permute-done | bytes 196640 | tf_op jit(solution)/shard_map/ppermute | solution.py:242
  2.5 0.0 copy-start
  2.6 3.3 %collective-permute-start.2 = (bf16[2,2,64,768]{3,2,1,0:T(8,128)(2,1)S(1)}, bf16[2,2,64,768]{3,2,1,0:T(8,128)(2,1)S(1)}, u32[]{:S(2)}, u32[]{:S(2)}) collective-permute-start(bf16[2,2,64,768]{3,2,1,0:T(8,128)(2,1)S(1)} %pad_maximum_fusion.refs_3_), channel_id=1, source_target_pairs={{0,64},{2,194},{32,96},{34,226},{64,128},{66,2},{96,160},{98,34},{... | collective-permute-start | bytes 1179656 | tf_op jit(solution)/shard_map/ppermute | solution.py:245
  5.9 1.8 %broadcast_in_dim.2 = bf16[8,64,768]{2,1,0:T(8,128)(2,1)} broadcast(bf16[64,768]{1,0:T(8,128)(2,1)} %param.5), dimensions={1,2} | broadcast | bytes 884736 | tf_op jit(solution)/shard_map/broadcast_in_dim | solution.py:248
  7.7 6.9 %all-to-all-start = ((bf16[8,64,768]{2,1,0:T(8,128)(2,1)}), bf16[8,64,768]{2,1,0:T(8,128)(2,1)S(1)}, u32[]{:S(2)}, u32[]{:S(2)}) async-start(bf16[8,64,768]{2,1,0:T(8,128)(2,1)} %broadcast_in_dim.2), calls=%async_computation | async-start | bytes 1572864 | tf_op jit(solution)/shard_map/all_to_all | solution.py:247
  14.7 3.1 %collective-permute-start.1 = (bf16[2,2,64,768]{3,2,1,0:T(8,128)(2,1)S(1)}, bf16[2,2,64,768]{3,2,1,0:T(8,128)(2,1)S(1)}, u32[]{:S(2)}, u32[]{:S(2)}) collective-permute-start(bf16[2,2,64,768]{3,2,1,0:T(8,128)(2,1)S(1)} %pad_maximum_fusion.refs_3_), channel_id=1, source_target_pairs={{0,32},{2,226},{32,64},{34,2},{64,96},{66,34},{96,128},{98,66},{12... | collective-permute-start | bytes 1179656 | tf_op jit(solution)/shard_map/ppermute | solution.py:246
  17.8 0.2 collective-permute-done.2.refs_5_
  18.0 0.0 collective-permute-start.5
  18.0 0.8 %collective-permute-start.3 = (bf16[2,2,64,768]{3,2,1,0:T(8,128)(2,1)S(1)}, bf16[2,2,64,768]{3,2,1,0:T(8,128)(2,1)S(1)}, u32[]{:S(2)}, u32[]{:S(2)}) collective-permute-start(bf16[2,2,64,768]{3,2,1,0:T(8,128)(2,1)S(1)} %collective-permute-done.2.refs_5_), channel_id=1, source_target_pairs={{0,32},{2,226},{32,64},{34,2},{64,96},{66,34},{96,128},{98,66},{12... | collective-permute-start | bytes 1179656 | tf_op jit(solution)/shard_map/ppermute | solution.py:251
  18.8 4.3 %collective-permute-start.4 = (bf16[1,2,64,768]{3,2,1,0:T(8,128)(2,1)S(1)}, bf16[1,2,64,768]{3,2,1,0:T(8,128)(2,1)S(1)}, u32[]{:S(2)}, u32[]{:S(2)}) collective-permute-start(bf16[1,2,64,768]{3,2,1,0:T(8,128)(2,1)S(1)} %slice.4), channel_id=1, source_target_pairs={{0,64},{2,194},{32,96},{34,226},{64,128},{66,2},{96,160},{98,34},{... | collective-permute-start | bytes 589832 | tf_op jit(solution)/shard_map/ppermute | solution.py:250
  23.1 0.1 pad_add_fusion.refs_0_.place_ref
  23.2 0.0 collective-permute-done.1.refs_4_
  23.2 4.8 %all-to-all-done.refs_2_ = bf16[8,64,768]{2,1,0:T(8,128)(2,1)S(1)} async-done(((bf16[8,64,768]{2,1,0:T(8,128)(2,1)}), bf16[8,64,768]{2,1,0:T(8,128)(2,1)S(1)}, u32[]{:S(2)}, u32[]{:S(2)}) %all-to-all-start) | async-done | bytes 786464 | tf_op jit(solution)/shard_map/all_to_all | solution.py:247
  28.0 0.0 collective-permute-done.5.refs_6_
  28.0 0.0 copy-done
  28.0 0.0 slice-start
  28.0 2.8 %attend_first.1 = (f32[512,768]{1,0:T(8,128)S(1)}, f32[6,512,128]{2,1,0:T(8,128)S(1)}, f32[6,512,128]{2,1,0:T(8,128)S(1)}) custom-call(s32[4]{0:T(128)S(1)} %pad_add_fusion.refs_0_.place_ref, s32[128]{0:T(128)S(1)} %copy-done, bf16[8,64,768]{2,1,0:T(8,128)(2,1)S(1)} %all-to-all-done.refs_2_, bf16[2,2,64,768]{3,2,1,0:T(8,128)(2,1)S(1)} %pad_maximum_fusion.refs_3_, ...), custom_call_target="tpu_custom_call" | custom-call | flops 805306368 | bytes 4194304 | tf_op jit(solution)/shard_map/attend_first/pallas_call | solution.py:143
  30.8 0.7 %collective-permute-done.4.refs_6_ = bf16[1,2,64,768]{3,2,1,0:T(8,128)(2,1)S(1)} collective-permute-done((bf16[1,2,64,768]{3,2,1,0:T(8,128)(2,1)S(1)}, bf16[1,2,64,768]{3,2,1,0:T(8,128)(2,1)S(1)}, u32[]{:S(2)}, u32[]{:S(2)}) %collective-permute-start.4) | collective-permute-done | bytes 196640 | tf_op jit(solution)/shard_map/ppermute | solution.py:250
  31.5 0.0 collective-permute-done.3.refs_4_
  31.5 0.0 slice-start.1
  31.5 0.3 collective-permute-start.6
  31.9 0.2 collective-permute-start.7
  32.0 0.3 collective-permute-start.8
  32.4 1.7 %collective-permute-done.8.refs_7_ = bf16[1,2,64,768]{3,2,1,0:T(8,128)(2,1)S(1)} collective-permute-done((bf16[1,2,64,768]{3,2,1,0:T(8,128)(2,1)S(1)}, bf16[1,2,64,768]{3,2,1,0:T(8,128)(2,1)S(1)}, u32[]{:S(2)}, u32[]{:S(2)}) %collective-permute-start.8) | collective-permute-done | bytes 196640 | tf_op jit(solution)/shard_map/ppermute | solution.py:266
  34.1 0.0 collective-permute-done.6.refs_3_
  34.1 0.0 collective-permute-done.7.refs_5_
  34.1 3.5 %attend_last.1 = bf16[8,400,128]{2,1,0:T(8,128)(2,1)S(1)} custom-call(s32[4]{0:T(128)S(1)} %pad_add_fusion.refs_0_.place_ref, s32[128]{0:T(128)S(1)} %copy-done, bf16[8,64,768]{2,1,0:T(8,128)(2,1)S(1)} %all-to-all-done.refs_2_, bf16[2,2,64,768]{3,2,1,0:T(8,128)(2,1)S(1)} %collective-permute-done.6.refs_3_, ...), custom_call_target="tpu_custom_call" | custom-call | flops 805306368 | bytes 4194304 | tf_op jit(solution)/shard_map/attend_last/pallas_call | solution.py:143
  37.6 22.3 %all_to_all.10.parts_ref = bf16[8,400,128]{2,1,0:T(8,128)(2,1)S(1)} all-to-all(bf16[8,400,128]{2,1,0:T(8,128)(2,1)S(1)} %attend_last.1), channel_id=1, replica_groups=mesh['z'=8,'xh'=2,'y'=4,'core'=2,'tp'=2] {'xh','y'}, dimensions={0} | all-to-all | bytes 1638400 | tf_op jit(solution)/shard_map/all_to_all | solution.py:276
  59.9 0.0 slice-done
  59.9 0.0 slice-done.1
  59.9 2.0 %project_partner.1 = bf16[32,3072]{1,0:T(8,128)(2,1)S(1)} custom-call(s32[4]{0:T(128)S(1)} %pad_add_fusion.refs_0_.place_ref, s32[128]{0:T(128)S(1)} %copy-done, bf16[8,400,128]{2,1,0:T(8,128)(2,1)S(1)} %all_to_all.10.parts_ref, bf16[768,3072]{1,0:T(8,128)(2,1)S(1)} %bitcast.10), custom_call_target="tpu_custom_call" | custom-call | tf_op jit(solution)/shard_map/project_partner/pallas_call | solution.py:208
  61.9 0.7 collective-permute-start.9
  62.5 2.0 %project_own.1 = f32[32,3072]{1,0:T(8,128)S(1)} custom-call(s32[4]{0:T(128)S(1)} %pad_add_fusion.refs_0_.place_ref, s32[128]{0:T(128)S(1)} %copy-done, bf16[8,400,128]{2,1,0:T(8,128)(2,1)S(1)} %all_to_all.10.parts_ref, bf16[768,3072]{1,0:T(8,128)(2,1)S(1)} %bitcast.10), custom_call_target="tpu_custom_call" | custom-call | tf_op jit(solution)/shard_map/project_own/pallas_call | solution.py:208
  64.5 3.1 %collective-permute-done.9 = bf16[32,3072]{1,0:T(8,128)(2,1)S(1)} collective-permute-done((bf16[32,3072]{1,0:T(8,128)(2,1)S(1)}, bf16[32,3072]{1,0:T(8,128)(2,1)S(1)}, u32[]{:S(2)}, u32[]{:S(2)}) %collective-permute-start.9) | collective-permute-done | bytes 196640 | tf_op jit(solution)/shard_map/ppermute | solution.py:277
  67.7 0.7 %add_convert_fusion = bf16[32,3072]{1,0:T(8,128)(2,1)} fusion(f32[32,3072]{1,0:T(8,128)S(1)} %project_own.1, bf16[32,3072]{1,0:T(8,128)(2,1)S(1)} %collective-permute-done.9), kind=kLoop, calls=%fused_computation.1 | loop fusion | flops 294912 | bytes 786432 | tf_op jit(solution)/shard_map/convert_element_type | solution.py:279
  (3 shorter events, 0.1 us)
Async XLA Ops:
  1.0 1.5 %collective-permute-start = (bf16[2,64,768]{2,1,0:T(8,128)(2,1)S(1)}, bf16[2,64,768]{2,1,0:T(8,128)(2,1)S(1)}, u32[]{:S(2)}, u32[]{:S(2)}) collective-permute-start(bf16[2,64,768]{2,1,0:T(8,128)(2,1)S(1)} %get-tuple-element.32), channel_id=1, source_target_pairs={{0,2},{2,0},{1,3},{3,1},{4,6},{6,4},{5,7},{7,5},{8,10},{10,8},{9,1... | collective-permute-start | bytes 589832 | tf_op jit(solution)/shard_map/ppermute | solution.py:242
  2.5 25.4 %copy-start = (s32[128]{0:T(128)S(1)}, s32[128]{0:T(128)}, u32[]{:S(2)}) copy-start(s32[128]{0:T(128)} %counts_ref.3) | copy-start | bytes 1540
  2.6 15.4 %collective-permute-start.2 = (bf16[2,2,64,768]{3,2,1,0:T(8,128)(2,1)S(1)}, bf16[2,2,64,768]{3,2,1,0:T(8,128)(2,1)S(1)}, u32[]{:S(2)}, u32[]{:S(2)}) collective-permute-start(bf16[2,2,64,768]{3,2,1,0:T(8,128)(2,1)S(1)} %pad_maximum_fusion.refs_3_), channel_id=1, source_target_pairs={{0,64},{2,194},{32,96},{34,226},{64,128},{66,2},{96,160},{98,34},{... | collective-permute-start | bytes 1179656 | tf_op jit(solution)/shard_map/ppermute | solution.py:245
  7.7 20.2 %all-to-all-start = ((bf16[8,64,768]{2,1,0:T(8,128)(2,1)}), bf16[8,64,768]{2,1,0:T(8,128)(2,1)S(1)}, u32[]{:S(2)}, u32[]{:S(2)}) async-start(bf16[8,64,768]{2,1,0:T(8,128)(2,1)} %broadcast_in_dim.2), calls=%async_computation | async-start | bytes 1572864 | tf_op jit(solution)/shard_map/all_to_all | solution.py:247
  14.7 8.5 %collective-permute-start.1 = (bf16[2,2,64,768]{3,2,1,0:T(8,128)(2,1)S(1)}, bf16[2,2,64,768]{3,2,1,0:T(8,128)(2,1)S(1)}, u32[]{:S(2)}, u32[]{:S(2)}) collective-permute-start(bf16[2,2,64,768]{3,2,1,0:T(8,128)(2,1)S(1)} %pad_maximum_fusion.refs_3_), channel_id=1, source_target_pairs={{0,32},{2,226},{32,64},{34,2},{64,96},{66,34},{96,128},{98,66},{12... | collective-permute-start | bytes 1179656 | tf_op jit(solution)/shard_map/ppermute | solution.py:246
  18.0 10.0 %collective-permute-start.5 = (bf16[2,2,64,768]{3,2,1,0:T(8,128)(2,1)S(1)}, bf16[2,2,64,768]{3,2,1,0:T(8,128)(2,1)S(1)}, u32[]{:S(2)}, u32[]{:S(2)}) collective-permute-start(bf16[2,2,64,768]{3,2,1,0:T(8,128)(2,1)S(1)} %collective-permute-done.2.refs_5_), channel_id=1, source_target_pairs={{0,2},{2,0},{1,3},{3,1},{4,6},{6,4},{5,7},{7,5},{8,10},{10,8},{9,1... | collective-permute-start | bytes 1179656 | tf_op jit(solution)/shard_map/ppermute | solution.py:253
  18.0 13.5 %collective-permute-start.3 = (bf16[2,2,64,768]{3,2,1,0:T(8,128)(2,1)S(1)}, bf16[2,2,64,768]{3,2,1,0:T(8,128)(2,1)S(1)}, u32[]{:S(2)}, u32[]{:S(2)}) collective-permute-start(bf16[2,2,64,768]{3,2,1,0:T(8,128)(2,1)S(1)} %collective-permute-done.2.refs_5_), channel_id=1, source_target_pairs={{0,32},{2,226},{32,64},{34,2},{64,96},{66,34},{96,128},{98,66},{12... | collective-permute-start | bytes 1179656 | tf_op jit(solution)/shard_map/ppermute | solution.py:251
  18.8 12.7 %collective-permute-start.4 = (bf16[1,2,64,768]{3,2,1,0:T(8,128)(2,1)S(1)}, bf16[1,2,64,768]{3,2,1,0:T(8,128)(2,1)S(1)}, u32[]{:S(2)}, u32[]{:S(2)}) collective-permute-start(bf16[1,2,64,768]{3,2,1,0:T(8,128)(2,1)S(1)} %slice.4), channel_id=1, source_target_pairs={{0,64},{2,194},{32,96},{34,226},{64,128},{66,2},{96,160},{98,34},{... | collective-permute-start | bytes 589832 | tf_op jit(solution)/shard_map/ppermute | solution.py:250
  28.0 31.9 %slice-start = ((s8[4718592]{0:T(1024)(128)(4,1)}), s8[4194304]{0:T(1024)(128)(4,1)S(1)}, s32[]{:S(2)}) async-start(s8[4718592]{0:T(1024)(128)(4,1)} %bitcast.9), calls=%async_computation.2 | async-start | bytes 8388608
  31.5 28.4 %slice-start.1 = ((s8[4718592]{0:T(1024)(128)(4,1)}), s8[524288]{0:T(1024)(128)(4,1)S(1)}, s32[]{:S(2)}) async-start(s8[4718592]{0:T(1024)(128)(4,1)} %bitcast.9), calls=%async_computation.3 | async-start | bytes 1048576
  31.5 2.6 %collective-permute-start.6 = (bf16[2,2,64,768]{3,2,1,0:T(8,128)(2,1)S(1)}, bf16[2,2,64,768]{3,2,1,0:T(8,128)(2,1)S(1)}, u32[]{:S(2)}, u32[]{:S(2)}) collective-permute-start(bf16[2,2,64,768]{3,2,1,0:T(8,128)(2,1)S(1)} %collective-permute-done.1.refs_4_), channel_id=1, source_target_pairs={{0,2},{2,0},{1,3},{3,1},{4,6},{6,4},{5,7},{7,5},{8,10},{10,8},{9,1... | collective-permute-start | bytes 1179656 | tf_op jit(solution)/shard_map/ppermute | solution.py:264
  31.9 2.2 %collective-permute-start.7 = (bf16[2,2,64,768]{3,2,1,0:T(8,128)(2,1)S(1)}, bf16[2,2,64,768]{3,2,1,0:T(8,128)(2,1)S(1)}, u32[]{:S(2)}, u32[]{:S(2)}) collective-permute-start(bf16[2,2,64,768]{3,2,1,0:T(8,128)(2,1)S(1)} %collective-permute-done.3.refs_4_), channel_id=1, source_target_pairs={{0,2},{2,0},{1,3},{3,1},{4,6},{6,4},{5,7},{7,5},{8,10},{10,8},{9,1... | collective-permute-start | bytes 1179656 | tf_op jit(solution)/shard_map/ppermute | solution.py:265
  32.0 2.1 %collective-permute-start.8 = (bf16[1,2,64,768]{3,2,1,0:T(8,128)(2,1)S(1)}, bf16[1,2,64,768]{3,2,1,0:T(8,128)(2,1)S(1)}, u32[]{:S(2)}, u32[]{:S(2)}) collective-permute-start(bf16[1,2,64,768]{3,2,1,0:T(8,128)(2,1)S(1)} %collective-permute-done.4.refs_6_), channel_id=1, source_target_pairs={{0,2},{2,0},{1,3},{3,1},{4,6},{6,4},{5,7},{7,5},{8,10},{10,8},{9,1... | collective-permute-start | bytes 589832 | tf_op jit(solution)/shard_map/ppermute | solution.py:266
  61.9 5.8 %collective-permute-start.9 = (bf16[32,3072]{1,0:T(8,128)(2,1)S(1)}, bf16[32,3072]{1,0:T(8,128)(2,1)S(1)}, u32[]{:S(2)}, u32[]{:S(2)}) collective-permute-start(bf16[32,3072]{1,0:T(8,128)(2,1)S(1)} %project_partner.1), channel_id=1, source_target_pairs={{0,1},{1,0},{2,3},{3,2},{4,5},{5,4},{6,7},{7,6},{8,9},{9,8},{10,11... | collective-permute-start | bytes 589832 | tf_op jit(solution)/shard_map/ppermute | solution.py:277

commit v7 on v6

--- a/solution.py
+++ b/solution.py
@@ -260,8 +260,8 @@
         None,
         False,
     )
-    near, third, fourth, state = lax.optimization_barrier((near, third, fourth, state))
     near_o = lax.ppermute(near, "core", SWAP)
+    third, fourth, state = lax.optimization_barrier((third, fourth, state))
     third_o = lax.ppermute(third, "core", SWAP)
     fourth_o = lax.ppermute(fourth, "core", SWAP)
     rest = [near_o, third, third_o, fourth, fourth_o]

time: 68.7 us -> 68.2 us (level)
  waiting for transfers between devices: 12 us -> 11 us
  starting transfers between devices: 20.1 us -> 20.9 us
    ppermute x1, waiting for transfers between devices: 0.74 us -> 0.01 us  [on_device(): fourth = lax.ppermute(second[:1], zc, split_ring(2))]
  transfers between devices with their start and end apart: 11 -> 11, of which waited for: 6 -> 5; matrix products, arithmetic and copies ran while one was open for 3% -> 3% of each run, Pallas kernels for 7% -> 7%
where the time goes in v7:
time: 68.2 us; the launch traced here: 67.8 us
  blocking collectives  21.9 us (32%)
  starting transfers between devices  20.9 us (31%)
  waiting for transfers between devices  11 us (16%)
  Pallas kernels  10.2 us (15%)
  local copies, waits for them, and re-layouts  1.87 us (3%)
  other arithmetic  1.79 us (3%)
    all_to_all x1, blocking collectives, on_device(): parts = lax.all_to_all(partial, ('xh', 'y'), 0, 0, tiled=True)  21.9 us
    all_to_all x1, starting transfers between devices, on_device(): lax.all_to_all(jnp.broadcast_to(queries[None], (COLUMNS, FRAME, WIDE)), (...  6.93 us
    pallas_call x2, Pallas kernels, attend_call(): pl.pallas_call(functools.partial(attend, offsets, state is not None, last...  6.32 us
    all_to_all x1, waiting for transfers between devices, on_device(): lax.all_to_all(jnp.broadcast_to(queries[None], (COLUMNS, FRAME, WIDE)), (...  4.75 us
    ppermute x1, starting transfers between devices, on_device(): fourth = lax.ppermute(second[:1], zc, split_ring(2))  4.29 us
    pallas_call x2, Pallas kernels, project_call(): pl.pallas_call(functools.partial(project, own), out_shape=jax.ShapeDtypeS...  3.92 us
    ppermute x1, starting transfers between devices, on_device(): second = lax.ppermute(own2, zc, split_ring(2))  3.35 us
    ppermute x1, waiting for transfers between devices, on_device(): lax.ppermute(project_call(place, frame_tokens, parts, wo, False), 'tp', S...  3.13 us
  transfers between devices with their start and end apart: 11, of which 5 were waited for; matrix products, arithmetic and copies ran while one was open for 3% of the time, Pallas kernels for 7%

profile of v7, /device:TPU:32, one launch (start us, length us, event | category | flops | bytes accessed | tf_op | source)
XLA Modules:
  0.0 67.8 jit_solution(576434977068154038)
XLA Ops:
  0.0 1.0 %fusion = (bf16[1,2,64,768]{3,2,1,0:T(8,128)(2,1)S(1)}, bf16[2,64,768]{2,1,0:T(8,128)(2,1)S(1)}) fusion(bf16[1,64,768]{2,1,0:T(8,128)(2,1)} %bitcast.12, bf16[1,64,768]{2,1,0:T(8,128)(2,1)} %bitcast.13), kind=kLoop, calls=%fused_computation.4 | loop fusion | flops 98304 | bytes 589824 | tf_op jit(solution)/shard_map/stack | solution.py:242
  1.0 0.1 collective-permute-start
  1.1 1.4 %collective-permute-done = bf16[2,64,768]{2,1,0:T(8,128)(2,1)S(1)} collective-permute-done((bf16[2,64,768]{2,1,0:T(8,128)(2,1)S(1)}, bf16[2,64,768]{2,1,0:T(8,128)(2,1)S(1)}, u32[]{:S(2)}, u32[]{:S(2)}) %collective-permute-start) | collective-permute-done | bytes 196640 | tf_op jit(solution)/shard_map/ppermute | solution.py:242
  2.5 0.0 copy-start
  2.6 3.3 %collective-permute-start.3 = (bf16[2,2,64,768]{3,2,1,0:T(8,128)(2,1)S(1)}, bf16[2,2,64,768]{3,2,1,0:T(8,128)(2,1)S(1)}, u32[]{:S(2)}, u32[]{:S(2)}) collective-permute-start(bf16[2,2,64,768]{3,2,1,0:T(8,128)(2,1)S(1)} %pad_maximum_fusion.refs_3_), channel_id=1, source_target_pairs={{0,64},{2,194},{32,96},{34,226},{64,128},{66,2},{96,160},{98,34},{... | collective-permute-start | bytes 1179656 | tf_op jit(solution)/shard_map/ppermute | solution.py:245
  5.9 1.8 %broadcast_in_dim.2 = bf16[8,64,768]{2,1,0:T(8,128)(2,1)} broadcast(bf16[64,768]{1,0:T(8,128)(2,1)} %param.5), dimensions={1,2} | broadcast | bytes 884736 | tf_op jit(solution)/shard_map/broadcast_in_dim | solution.py:248
  7.7 6.9 %all-to-all-start = ((bf16[8,64,768]{2,1,0:T(8,128)(2,1)}), bf16[8,64,768]{2,1,0:T(8,128)(2,1)S(1)}, u32[]{:S(2)}, u32[]{:S(2)}) async-start(bf16[8,64,768]{2,1,0:T(8,128)(2,1)} %broadcast_in_dim.2), calls=%async_computation | async-start | bytes 1572864 | tf_op jit(solution)/shard_map/all_to_all | solution.py:247
  14.7 3.1 %collective-permute-start.1 = (bf16[2,2,64,768]{3,2,1,0:T(8,128)(2,1)S(1)}, bf16[2,2,64,768]{3,2,1,0:T(8,128)(2,1)S(1)}, u32[]{:S(2)}, u32[]{:S(2)}) collective-permute-start(bf16[2,2,64,768]{3,2,1,0:T(8,128)(2,1)S(1)} %pad_maximum_fusion.refs_3_), channel_id=1, source_target_pairs={{0,32},{2,226},{32,64},{34,2},{64,96},{66,34},{96,128},{98,66},{12... | collective-permute-start | bytes 1179656 | tf_op jit(solution)/shard_map/ppermute | solution.py:246
  17.8 0.2 collective-permute-done.3.refs_5_
  18.0 0.0 collective-permute-start.6
  18.0 0.8 %collective-permute-start.4 = (bf16[2,2,64,768]{3,2,1,0:T(8,128)(2,1)S(1)}, bf16[2,2,64,768]{3,2,1,0:T(8,128)(2,1)S(1)}, u32[]{:S(2)}, u32[]{:S(2)}) collective-permute-start(bf16[2,2,64,768]{3,2,1,0:T(8,128)(2,1)S(1)} %collective-permute-done.3.refs_5_), channel_id=1, source_target_pairs={{0,32},{2,226},{32,64},{34,2},{64,96},{66,34},{96,128},{98,66},{12... | collective-permute-start | bytes 1179656 | tf_op jit(solution)/shard_map/ppermute | solution.py:251
  18.8 4.3 %collective-permute-start.5 = (bf16[1,2,64,768]{3,2,1,0:T(8,128)(2,1)S(1)}, bf16[1,2,64,768]{3,2,1,0:T(8,128)(2,1)S(1)}, u32[]{:S(2)}, u32[]{:S(2)}) collective-permute-start(bf16[1,2,64,768]{3,2,1,0:T(8,128)(2,1)S(1)} %slice.4), channel_id=1, source_target_pairs={{0,64},{2,194},{32,96},{34,226},{64,128},{66,2},{96,160},{98,34},{... | collective-permute-start | bytes 589832 | tf_op jit(solution)/shard_map/ppermute | solution.py:250
  23.1 0.1 pad_add_fusion.refs_0_.place_ref
  23.2 0.0 collective-permute-done.1.refs_4_
  23.2 4.8 %all-to-all-done.refs_2_ = bf16[8,64,768]{2,1,0:T(8,128)(2,1)S(1)} async-done(((bf16[8,64,768]{2,1,0:T(8,128)(2,1)}), bf16[8,64,768]{2,1,0:T(8,128)(2,1)S(1)}, u32[]{:S(2)}, u32[]{:S(2)}) %all-to-all-start) | async-done | bytes 786464 | tf_op jit(solution)/shard_map/all_to_all | solution.py:247
  28.0 1.0 %collective-permute-start.2 = (bf16[2,2,64,768]{3,2,1,0:T(8,128)(2,1)S(1)}, bf16[2,2,64,768]{3,2,1,0:T(8,128)(2,1)S(1)}, u32[]{:S(2)}, u32[]{:S(2)}) collective-permute-start(bf16[2,2,64,768]{3,2,1,0:T(8,128)(2,1)S(1)} %collective-permute-done.1.refs_4_), channel_id=1, source_target_pairs={{0,2},{2,0},{1,3},{3,1},{4,6},{6,4},{5,7},{7,5},{8,10},{10,8},{9,1... | collective-permute-start | bytes 1179656 | tf_op jit(solution)/shard_map/ppermute | solution.py:263
  28.9 0.0 collective-permute-done.6.refs_6_
  28.9 0.0 copy-done
  28.9 0.0 slice-start
  28.9 2.8 %attend_first.1 = (f32[512,768]{1,0:T(8,128)S(1)}, f32[6,512,128]{2,1,0:T(8,128)S(1)}, f32[6,512,128]{2,1,0:T(8,128)S(1)}) custom-call(s32[4]{0:T(128)S(1)} %pad_add_fusion.refs_0_.place_ref, s32[128]{0:T(128)S(1)} %copy-done, bf16[8,64,768]{2,1,0:T(8,128)(2,1)S(1)} %all-to-all-done.refs_2_, bf16[2,2,64,768]{3,2,1,0:T(8,128)(2,1)S(1)} %pad_maximum_fusion.refs_3_, ...), custom_call_target="tpu_custom_call" | custom-call | flops 805306368 | bytes 4194304 | tf_op jit(solution)/shard_map/attend_first/pallas_call | solution.py:143
  31.7 0.0 collective-permute-done.5.refs_6_
  31.8 0.0 collective-permute-done.4.refs_4_
  31.8 0.0 slice-start.1
  31.8 0.1 collective-permute-start.7
  31.9 0.5 collective-permute-start.8
  32.4 1.5 %collective-permute-done.8.refs_7_ = bf16[1,2,64,768]{3,2,1,0:T(8,128)(2,1)S(1)} collective-permute-done((bf16[1,2,64,768]{3,2,1,0:T(8,128)(2,1)S(1)}, bf16[1,2,64,768]{3,2,1,0:T(8,128)(2,1)S(1)}, u32[]{:S(2)}, u32[]{:S(2)}) %collective-permute-start.8) | collective-permute-done | bytes 196640 | tf_op jit(solution)/shard_map/ppermute | solution.py:266
  33.9 0.0 collective-permute-done.2.refs_3_
  33.9 0.0 collective-permute-done.7.refs_5_
  33.9 3.5 %attend_last.1 = bf16[8,400,128]{2,1,0:T(8,128)(2,1)S(1)} custom-call(s32[4]{0:T(128)S(1)} %pad_add_fusion.refs_0_.place_ref, s32[128]{0:T(128)S(1)} %copy-done, bf16[8,64,768]{2,1,0:T(8,128)(2,1)S(1)} %all-to-all-done.refs_2_, bf16[2,2,64,768]{3,2,1,0:T(8,128)(2,1)S(1)} %collective-permute-done.2.refs_3_, ...), custom_call_target="tpu_custom_call" | custom-call | flops 805306368 | bytes 4194304 | tf_op jit(solution)/shard_map/attend_last/pallas_call | solution.py:143
  37.4 21.9 %all_to_all.10.parts_ref = bf16[8,400,128]{2,1,0:T(8,128)(2,1)S(1)} all-to-all(bf16[8,400,128]{2,1,0:T(8,128)(2,1)S(1)} %attend_last.1), channel_id=1, replica_groups=mesh['z'=8,'xh'=2,'y'=4,'core'=2,'tp'=2] {'xh','y'}, dimensions={0} | all-to-all | bytes 1638400 | tf_op jit(solution)/shard_map/all_to_all | solution.py:276
  59.3 0.0 slice-done
  59.3 0.0 slice-done.1
  59.3 2.0 %project_partner.1 = bf16[32,3072]{1,0:T(8,128)(2,1)S(1)} custom-call(s32[4]{0:T(128)S(1)} %pad_add_fusion.refs_0_.place_ref, s32[128]{0:T(128)S(1)} %copy-done, bf16[8,400,128]{2,1,0:T(8,128)(2,1)S(1)} %all_to_all.10.parts_ref, bf16[768,3072]{1,0:T(8,128)(2,1)S(1)} %bitcast.10), custom_call_target="tpu_custom_call" | custom-call | tf_op jit(solution)/shard_map/project_partner/pallas_call | solution.py:208
  61.3 0.7 %collective-permute-start.9 = (bf16[32,3072]{1,0:T(8,128)(2,1)S(1)}, bf16[32,3072]{1,0:T(8,128)(2,1)S(1)}, u32[]{:S(2)}, u32[]{:S(2)}) collective-permute-start(bf16[32,3072]{1,0:T(8,128)(2,1)S(1)} %project_partner.1), channel_id=1, source_target_pairs={{0,1},{1,0},{2,3},{3,2},{4,5},{5,4},{6,7},{7,6},{8,9},{9,8},{10,11... | collective-permute-start | bytes 589832 | tf_op jit(solution)/shard_map/ppermute | solution.py:277
  62.0 2.0 %project_own.1 = f32[32,3072]{1,0:T(8,128)S(1)} custom-call(s32[4]{0:T(128)S(1)} %pad_add_fusion.refs_0_.place_ref, s32[128]{0:T(128)S(1)} %copy-done, bf16[8,400,128]{2,1,0:T(8,128)(2,1)S(1)} %all_to_all.10.parts_ref, bf16[768,3072]{1,0:T(8,128)(2,1)S(1)} %bitcast.10), custom_call_target="tpu_custom_call" | custom-call | tf_op jit(solution)/shard_map/project_own/pallas_call | solution.py:208
  64.0 3.1 %collective-permute-done.9 = bf16[32,3072]{1,0:T(8,128)(2,1)S(1)} collective-permute-done((bf16[32,3072]{1,0:T(8,128)(2,1)S(1)}, bf16[32,3072]{1,0:T(8,128)(2,1)S(1)}, u32[]{:S(2)}, u32[]{:S(2)}) %collective-permute-start.9) | collective-permute-done | bytes 196640 | tf_op jit(solution)/shard_map/ppermute | solution.py:277
  67.1 0.7 %add_convert_fusion = bf16[32,3072]{1,0:T(8,128)(2,1)} fusion(f32[32,3072]{1,0:T(8,128)S(1)} %project_own.1, bf16[32,3072]{1,0:T(8,128)(2,1)S(1)} %collective-permute-done.9), kind=kLoop, calls=%fused_computation.1 | loop fusion | flops 294912 | bytes 786432 | tf_op jit(solution)/shard_map/convert_element_type | solution.py:279
  (3 shorter events, 0.1 us)
Async XLA Ops:
  1.0 1.5 %collective-permute-start = (bf16[2,64,768]{2,1,0:T(8,128)(2,1)S(1)}, bf16[2,64,768]{2,1,0:T(8,128)(2,1)S(1)}, u32[]{:S(2)}, u32[]{:S(2)}) collective-permute-start(bf16[2,64,768]{2,1,0:T(8,128)(2,1)S(1)} %get-tuple-element.30), channel_id=1, source_target_pairs={{0,2},{2,0},{1,3},{3,1},{4,6},{6,4},{5,7},{7,5},{8,10},{10,8},{9,1... | collective-permute-start | bytes 589832 | tf_op jit(solution)/shard_map/ppermute | solution.py:242
  2.5 26.4 %copy-start = (s32[128]{0:T(128)S(1)}, s32[128]{0:T(128)}, u32[]{:S(2)}) copy-start(s32[128]{0:T(128)} %counts_ref.3) | copy-start | bytes 1540
  2.6 15.4 %collective-permute-start.3 = (bf16[2,2,64,768]{3,2,1,0:T(8,128)(2,1)S(1)}, bf16[2,2,64,768]{3,2,1,0:T(8,128)(2,1)S(1)}, u32[]{:S(2)}, u32[]{:S(2)}) collective-permute-start(bf16[2,2,64,768]{3,2,1,0:T(8,128)(2,1)S(1)} %pad_maximum_fusion.refs_3_), channel_id=1, source_target_pairs={{0,64},{2,194},{32,96},{34,226},{64,128},{66,2},{96,160},{98,34},{... | collective-permute-start | bytes 1179656 | tf_op jit(solution)/shard_map/ppermute | solution.py:245
  7.7 20.2 %all-to-all-start = ((bf16[8,64,768]{2,1,0:T(8,128)(2,1)}), bf16[8,64,768]{2,1,0:T(8,128)(2,1)S(1)}, u32[]{:S(2)}, u32[]{:S(2)}) async-start(bf16[8,64,768]{2,1,0:T(8,128)(2,1)} %broadcast_in_dim.2), calls=%async_computation | async-start | bytes 1572864 | tf_op jit(solution)/shard_map/all_to_all | solution.py:247
  14.7 8.5 %collective-permute-start.1 = (bf16[2,2,64,768]{3,2,1,0:T(8,128)(2,1)S(1)}, bf16[2,2,64,768]{3,2,1,0:T(8,128)(2,1)S(1)}, u32[]{:S(2)}, u32[]{:S(2)}) collective-permute-start(bf16[2,2,64,768]{3,2,1,0:T(8,128)(2,1)S(1)} %pad_maximum_fusion.refs_3_), channel_id=1, source_target_pairs={{0,32},{2,226},{32,64},{34,2},{64,96},{66,34},{96,128},{98,66},{12... | collective-permute-start | bytes 1179656 | tf_op jit(solution)/shard_map/ppermute | solution.py:246
  18.0 10.9 %collective-permute-start.6 = (bf16[2,2,64,768]{3,2,1,0:T(8,128)(2,1)S(1)}, bf16[2,2,64,768]{3,2,1,0:T(8,128)(2,1)S(1)}, u32[]{:S(2)}, u32[]{:S(2)}) collective-permute-start(bf16[2,2,64,768]{3,2,1,0:T(8,128)(2,1)S(1)} %collective-permute-done.3.refs_5_), channel_id=1, source_target_pairs={{0,2},{2,0},{1,3},{3,1},{4,6},{6,4},{5,7},{7,5},{8,10},{10,8},{9,1... | collective-permute-start | bytes 1179656 | tf_op jit(solution)/shard_map/ppermute | solution.py:253
  18.0 13.8 %collective-permute-start.4 = (bf16[2,2,64,768]{3,2,1,0:T(8,128)(2,1)S(1)}, bf16[2,2,64,768]{3,2,1,0:T(8,128)(2,1)S(1)}, u32[]{:S(2)}, u32[]{:S(2)}) collective-permute-start(bf16[2,2,64,768]{3,2,1,0:T(8,128)(2,1)S(1)} %collective-permute-done.3.refs_5_), channel_id=1, source_target_pairs={{0,32},{2,226},{32,64},{34,2},{64,96},{66,34},{96,128},{98,66},{12... | collective-permute-start | bytes 1179656 | tf_op jit(solution)/shard_map/ppermute | solution.py:251
  18.8 12.9 %collective-permute-start.5 = (bf16[1,2,64,768]{3,2,1,0:T(8,128)(2,1)S(1)}, bf16[1,2,64,768]{3,2,1,0:T(8,128)(2,1)S(1)}, u32[]{:S(2)}, u32[]{:S(2)}) collective-permute-start(bf16[1,2,64,768]{3,2,1,0:T(8,128)(2,1)S(1)} %slice.4), channel_id=1, source_target_pairs={{0,64},{2,194},{32,96},{34,226},{64,128},{66,2},{96,160},{98,34},{... | collective-permute-start | bytes 589832 | tf_op jit(solution)/shard_map/ppermute | solution.py:250
  28.0 5.9 %collective-permute-start.2 = (bf16[2,2,64,768]{3,2,1,0:T(8,128)(2,1)S(1)}, bf16[2,2,64,768]{3,2,1,0:T(8,128)(2,1)S(1)}, u32[]{:S(2)}, u32[]{:S(2)}) collective-permute-start(bf16[2,2,64,768]{3,2,1,0:T(8,128)(2,1)S(1)} %collective-permute-done.1.refs_4_), channel_id=1, source_target_pairs={{0,2},{2,0},{1,3},{3,1},{4,6},{6,4},{5,7},{7,5},{8,10},{10,8},{9,1... | collective-permute-start | bytes 1179656 | tf_op jit(solution)/shard_map/ppermute | solution.py:263
  28.9 30.4 %slice-start = ((s8[4718592]{0:T(1024)(128)(4,1)}), s8[4194304]{0:T(1024)(128)(4,1)S(1)}, s32[]{:S(2)}) async-start(s8[4718592]{0:T(1024)(128)(4,1)} %bitcast.9), calls=%async_computation.2 | async-start | bytes 8388608
  31.8 27.6 %slice-start.1 = ((s8[4718592]{0:T(1024)(128)(4,1)}), s8[524288]{0:T(1024)(128)(4,1)S(1)}, s32[]{:S(2)}) async-start(s8[4718592]{0:T(1024)(128)(4,1)} %bitcast.9), calls=%async_computation.3 | async-start | bytes 1048576
  31.8 2.1 %collective-permute-start.7 = (bf16[2,2,64,768]{3,2,1,0:T(8,128)(2,1)S(1)}, bf16[2,2,64,768]{3,2,1,0:T(8,128)(2,1)S(1)}, u32[]{:S(2)}, u32[]{:S(2)}) collective-permute-start(bf16[2,2,64,768]{3,2,1,0:T(8,128)(2,1)S(1)} %collective-permute-done.4.refs_4_), channel_id=1, source_target_pairs={{0,2},{2,0},{1,3},{3,1},{4,6},{6,4},{5,7},{7,5},{8,10},{10,8},{9,1... | collective-permute-start | bytes 1179656 | tf_op jit(solution)/shard_map/ppermute | solution.py:265
  31.9 2.0 %collective-permute-start.8 = (bf16[1,2,64,768]{3,2,1,0:T(8,128)(2,1)S(1)}, bf16[1,2,64,768]{3,2,1,0:T(8,128)(2,1)S(1)}, u32[]{:S(2)}, u32[]{:S(2)}) collective-permute-start(bf16[1,2,64,768]{3,2,1,0:T(8,128)(2,1)S(1)} %collective-permute-done.5.refs_6_), channel_id=1, source_target_pairs={{0,2},{2,0},{1,3},{3,1},{4,6},{6,4},{5,7},{7,5},{8,10},{10,8},{9,1... | collective-permute-start | bytes 589832 | tf_op jit(solution)/shard_map/ppermute | solution.py:266
  61.3 5.8 %collective-permute-start.9 = (bf16[32,3072]{1,0:T(8,128)(2,1)S(1)}, bf16[32,3072]{1,0:T(8,128)(2,1)S(1)}, u32[]{:S(2)}, u32[]{:S(2)}) collective-permute-start(bf16[32,3072]{1,0:T(8,128)(2,1)S(1)} %project_partner.1), channel_id=1, source_target_pairs={{0,1},{1,0},{2,3},{3,2},{4,5},{5,4},{6,7},{7,6},{8,9},{9,8},{10,11... | collective-permute-start | bytes 589832 | tf_op jit(solution)/shard_map/ppermute | solution.py:277
